TPU v7x, 32 devices: a whole 2x2x4 slice. The times are simulated.
32 devices in a mesh: pipe: 2 (over x), expert: 16 (over z, y, core).
Axes of the slice: x: 2, y: 2, z: 4, core: 2. Of those that a mesh axis runs over, the one named last changes fastest.
Arguments:
- tokens: bfloat16 [2, 2048, 2560], P('pipe', 'expert'), may hold values from -48 to 48
- routes: int32 [2, 2048, 6], P('pipe', 'expert'), may hold values from 0 to 15, all different within a row; in each aligned block of 128 rows (0 to 127, 128 to 255, ..., all dimensions but the last counted through in order) at most 64 rows name the same one
- gates: float32 [2, 2048, 6], P('pipe', 'expert'), may hold values from 0.05 to 0.5
- capacity: int32 [2, 16], P('pipe'), may hold values from 32 to 64, as said below
- w_down_kv: bfloat16 [2, 2560, 256], P('pipe', 'expert'), may hold values from -1 to 1
- kv_gain: float32 [2, 256], P('pipe'), may hold values from 0.1 to 1.9
- w_query: bfloat16 [2, 256, 256], P('pipe'), may hold values from -1 to 12
- w_out: bfloat16 [2, 256, 2560], P('pipe', 'expert'), may hold values from -0.375 to 0.375
- w_gate_up: bfloat16 [2, 16, 2560, 1536], P('pipe', 'expert'), may hold values from -0.125 to 0.125
- w_expert_down: bfloat16 [2, 16, 768, 2560], P('pipe', 'expert'), may hold values from -0.21875 to 0.21875
Outputs:
- section_output: bfloat16 [2, 2048, 2560], P('pipe', 'expert')
Inputs may be any that keep to these rules, and one draw needn't show every extreme that they name: `routes`: in each aligned block of 128 rows (the rows of one device) no expert is named by more than 64 rows of a micro-batch. `capacity`: in every section some expert accepts 64 rows.
All inputs are finite; a program needn't handle non-finite values.
Results may differ from a plain program's by a relative error of at most 0.019.
Values may be sent and summed in bfloat16 or wider, within the bound.
No kernel may reach another device: no remote copies, remote signals or barrier semaphores. Data moves between devices by JAX's collectives and lax.ppermute only.
A program may use at most 128 MiB of HBM per device.

v0:
```python
import jax
import jax.numpy as jnp
from jax import lax
from jax.sharding import PartitionSpec as P


def shifted(x, axis, by):
    count = lax.axis_size(axis)
    return lax.ppermute(x, axis, [(i, (i + by) % count) for i in range(count)])


def on_device(
    tokens, routes, gates, capacity, w_down_kv, kv_gain, w_query, w_out, w_gate_up, w_expert_down
):
    owners = lax.axis_size("expert")
    position = lax.axis_index("expert")
    rows_here = tokens.shape[1]
    width = tokens.shape[2]
    top_count = routes.shape[2]
    latent_width = w_query.shape[1]
    hidden_width = w_expert_down.shape[2]
    most = max(2, 4 * rows_here * top_count // (3 * owners))
    down_kv, out_proj = (
        lax.all_gather(w_down_kv[0], "expert", axis=0, tiled=True),
        lax.all_gather(w_out[0], "expert", axis=0, tiled=True),
    )
    inputs = tokens[0]
    raw = jnp.dot(inputs, down_kv, preferred_element_type=jnp.float32)
    latent = (raw * lax.rsqrt(jnp.mean(raw * raw, -1, keepdims=True) + 1e-06) * kv_gain[0]).astype(
        jnp.bfloat16
    )
    query = jnp.dot(latent, w_query[0], preferred_element_type=jnp.float32).astype(jnp.bfloat16)
    factor = latent_width ** (-0.5)
    query_place = position * rows_here + jnp.arange(rows_here)
    piece = lax.all_gather(latent, "expert", axis=0, tiled=True)
    peak = jnp.full((rows_here, 1), -1e30, jnp.float32)
    scores = jnp.dot(query, piece.T, preferred_element_type=jnp.float32) * factor
    key_place = jnp.arange(piece.shape[0])
    allowed = key_place[None, :] <= query_place[:, None]
    scores = jnp.where(allowed, scores, -1e30)
    newest = jnp.maximum(peak, jnp.max(scores, -1, keepdims=True))
    weights = jnp.where(allowed, jnp.exp(scores - newest), 0.0)
    total = jnp.sum(weights, -1, keepdims=True)
    accum = jnp.dot(weights.astype(jnp.bfloat16), piece, preferred_element_type=jnp.float32)
    peak, total, accum = (newest, total, accum)
    attended = (accum / total).astype(jnp.bfloat16)
    hidden_state = (
        inputs.astype(jnp.float32) + jnp.dot(attended, out_proj, preferred_element_type=jnp.float32)
    ).astype(jnp.bfloat16)
    flat_routes = routes[0].reshape(-1)
    onehot = (flat_routes[:, None] == jnp.arange(owners)[None, :]).astype(jnp.int32)
    ranking = jnp.sum((jnp.cumsum(onehot, 0) - 1) * onehot, 1)
    limits = jnp.sum(onehot * capacity[0][None, :], 1)
    kept = ranking < limits
    target = jnp.where(kept, flat_routes * most + ranking, -1)
    slot_ids = jnp.arange(owners * most)
    dispatch = (target[None, :] == slot_ids[:, None]).reshape(owners * most, rows_here, top_count)
    dispatch = jnp.any(dispatch, 2).astype(jnp.bfloat16)
    outgoing = jnp.dot(dispatch, hidden_state, preferred_element_type=jnp.float32).astype(
        jnp.bfloat16
    )
    outgoing = outgoing.reshape(owners, most, width)
    gate_up = w_gate_up[0, 0]
    expert_down = w_expert_down[0, 0]
    received = lax.all_to_all(outgoing, "expert", split_axis=0, concat_axis=0, tiled=True)
    shaped = received.shape
    flat_rows = received.reshape(-1, width)
    both = jnp.dot(flat_rows, gate_up, preferred_element_type=jnp.float32)
    inner = (jax.nn.silu(both[:, :hidden_width]) * both[:, hidden_width:]).astype(jnp.bfloat16)
    result = (
        jnp.dot(inner, expert_down, preferred_element_type=jnp.float32)
        .astype(jnp.bfloat16)
        .reshape(shaped)
    )
    returned = lax.all_to_all(result, "expert", split_axis=0, concat_axis=0, tiled=True)
    returned = returned.reshape(owners * most, width)
    picked = returned[jnp.maximum(target, 0)]
    weight = jnp.where(kept, gates[0].reshape(-1), 0.0)
    expert_sum = jnp.sum((picked * weight[:, None]).reshape(rows_here, top_count, width), 1)
    combined = (hidden_state.astype(jnp.float32) + expert_sum).astype(jnp.bfloat16)
    output = shifted(combined, "pipe", 1)
    return output[None]


def solution(mesh):
    return jax.shard_map(
        on_device,
        mesh=mesh,
        in_specs=(
            P("pipe", "expert", None),
            P("pipe", "expert", None),
            P("pipe", "expert", None),
            P("pipe", None),
            P("pipe", "expert", None),
            P("pipe", None),
            P("pipe", None, None),
            P("pipe", "expert", None),
            P("pipe", "expert", None, None),
            P("pipe", "expert", None, None),
        ),
        out_specs=P("pipe", "expert", None),
        check_vma=False,
    )
```

profile of v0, /device:TPU:12, one launch (start us, length us, event | category | flops | bytes accessed | tf_op | source)
XLA Modules:
  0.0 438.9 jit_solution(16922249988305410858)
XLA Ops:
  6.5 0.7 all-gather.8.cloned.1.call-update
  7.3 40.6 %all-gather.8.cloned.1.call-done = bf16[1,2560,256]{2,1,0:T(8,128)(2,1)} async-done(((bf16[1,160,256]{2,1,0:T(8,128)(2,1)}), bf16[1,2560,256]{2,1,0:T(8,128)(2,1)}) %all-gather.8.cloned.1.call-update) | async-done | bytes 1310736 | tf_op jit(solution)/shard_map/all_gather | solution.py:24
  47.9 1.9 multiply_reduce_fusion.1
  49.9 1.4 multiply_convert_fusion
  52.0 0.8 copy.19
  53.1 1.7 reduce-window.6
  55.1 0.8 select_reduce_fusion
  56.1 0.8 copy.24
  57.6 31.1 %all-gather.6.cloned.1.call-done = bf16[2048,256]{1,0:T(8,128)(2,1)} async-done(((bf16[128,256]{1,0:T(8,128)(2,1)}), bf16[2048,256]{1,0:T(8,128)(2,1)}) %all-gather.6.cloned.1.call-update) | async-done | bytes 1048592 | tf_op jit(solution)/shard_map/all_gather | solution.py:35
  88.7 1.9 fusion.36
  90.9 37.3 %all-gather.10.cloned.1.call-done = bf16[1,256,2560]{2,1,0:T(8,128)(2,1)} async-done(((bf16[1,16,2560]{2,1,0:T(8,128)(2,1)}), bf16[1,256,2560]{2,1,0:T(8,128)(2,1)}) %all-gather.10.cloned.1.call-update) | async-done | bytes 1310736 | tf_op jit(solution)/shard_map/all_gather | solution.py:25
  128.3 2.5 fusion.3
  130.8 1.5 convolution_convert_fusion.1
  132.3 120.3 %all_to_all.10 = bf16[16,64,2560]{2,1,0:T(8,128)(2,1)S(1)} all-to-all(bf16[16,64,2560]{2,1,0:T(8,128)(2,1)S(1)} %bitcast.61), channel_id=1, replica_groups=mesh['pipe'=2,'expert'=16] {'expert'}, dimensions={0} | all-to-all | bytes 10485760 | tf_op jit(solution)/shard_map/all_to_all | solution.py:65
  252.6 8.3 %fusion = f32[1024,1536]{1,0:T(8,128)S(1)} fusion(bf16[1024,2560]{1,0:T(8,128)(2,1)S(1)} %bitcast.63, bf16[1,1,2560,1536]{3,2,1,0:T(8,128)(2,1)S(1)} %bitcast.69), kind=kOutput, calls=%fused_computation.2 | convolution fusion | flops 8053063680 | bytes 19398656 | tf_op jit(solution)/shard_map/dot_general | solution.py:68
  260.9 6.1 %convolution_convert_fusion = bf16[1024,2560]{1,0:T(8,128)(2,1)} fusion(bf16[1,1,768,2560]{3,2,1,0:T(8,128)(2,1)S(1)} %copy-done.2, f32[1024,1536]{1,0:T(8,128)S(1)} %fusion), kind=kOutput, calls=%fused_computation.4 | convolution fusion | flops 4033871872 | bytes 15466496 | tf_op jit(solution)/shard_map/dot_general | solution.py:71
  267.0 5.5 %all-to-all-start.1 = ((bf16[16,64,2560]{2,1,0:T(8,128)(2,1)}), bf16[16,64,2560]{2,1,0:T(8,128)(2,1)}, u32[]{:S(2)}, u32[]{:S(2)}) async-start(bf16[16,64,2560]{2,1,0:T(8,128)(2,1)} %bitcast.62), calls=%async_computation.1 | async-start | bytes 10485760 | tf_op jit(solution)/shard_map/all_to_all | solution.py:75
  272.7 114.6 %all-to-all-done.1 = bf16[16,64,2560]{2,1,0:T(8,128)(2,1)} async-done(((bf16[16,64,2560]{2,1,0:T(8,128)(2,1)}), bf16[16,64,2560]{2,1,0:T(8,128)(2,1)}, u32[]{:S(2)}, u32[]{:S(2)}) %all-to-all-start.1) | async-done | bytes 5242912 | tf_op jit(solution)/shard_map/all_to_all | solution.py:75
  387.3 11.5 %gather_fusion = bf16[768,2560]{1,0:T(8,128)(2,1)} fusion(bf16[1024,2560]{1,0:T(8,128)(2,1)} %bitcast.13, s32[1024]{0:T(1024)S(1)} %pad_clamp_fusion), kind=kCustom, calls=%fused_computation | custom fusion | bytes 7867392 | tf_op jit(solution)/shard_map/gather | solution.py:77
  398.8 7.7 %reshape.130 = f32[128,6,2560]{2,1,0:T(8,128)} reshape(bf16[768,2560]{1,0:T(8,128)(2,1)} %gather_fusion) | data formatting | bytes 11796480 | tf_op jit(solution)/shard_map/convert_element_type | solution.py:79
  406.5 7.9 %multiply_reduce_fusion = f32[128,2560]{1,0:T(8,128)S(1)} fusion(f32[128,6,2560]{2,1,0:T(8,128)} %reshape.130, f32[128,6]{1,0:T(8,128)S(1)} %get-tuple-element.7), kind=kLoop, calls=%fused_computation.1 | loop fusion | flops 3604480 | bytes 9178112 | tf_op jit(solution)/shard_map/reduce_sum | solution.py:79
  414.6 1.5 collective-permute-start
  416.1 15.5 %collective-permute-done = bf16[128,2560]{1,0:T(8,128)(2,1)S(1)} collective-permute-done((bf16[128,2560]{1,0:T(8,128)(2,1)S(1)}, bf16[128,2560]{1,0:T(8,128)(2,1)S(1)}, u32[]{:S(2)}, u32[]{:S(2)}) %collective-permute-start) | collective-permute-done | bytes 655392 | tf_op jit(solution)/shard_map/ppermute | solution.py:9
  431.6 0.8 copy.28
  (36 shorter events, 2.9 us)
Async XLA Ops:
  6.5 82.1 %copy-start = (bf16[1,256,256]{2,1,0:T(8,128)(2,1)S(1)}, bf16[1,256,256]{2,1,0:T(8,128)(2,1)}, u32[]{:S(2)}) copy-start(bf16[1,256,256]{2,1,0:T(8,128)(2,1)} %param.16) | copy-start | bytes 393220
  6.5 121.7 %copy-start.1 = (bf16[1,128,2560]{2,1,0:T(8,128)(2,1)S(1)}, bf16[1,128,2560]{2,1,0:T(8,128)(2,1)}, u32[]{:S(2)}) copy-start(bf16[1,128,2560]{2,1,0:T(8,128)(2,1)} %param.10) | copy-start | bytes 1966084
  6.5 41.4 %all-gather.8.cloned.1.call-start = ((), (), s32[]{:S(2)}) async-start(), calls=%async_computation.3 | async-start | bytes 1392640 | tf_op jit(solution)/shard_map/all_gather | solution.py:24
  7.3 81.4 %all-gather.6.cloned.1.call-start = ((), (), s32[]{:S(2)}) async-start(), calls=%async_computation.2 | async-start | bytes 1114112 | tf_op jit(solution)/shard_map/all_gather | solution.py:35
  51.3 77.0 %all-gather.10.cloned.1.call-start = ((), (), s32[]{:S(2)}) async-start(), calls=%async_computation.4 | async-start | bytes 1392640 | tf_op jit(solution)/shard_map/all_gather | solution.py:25
  130.8 121.8 %slice-start = ((s8[7864320]{0:T(1024)(128)(4,1)}), s8[4194304]{0:T(1024)(128)(4,1)S(1)}, s32[]{:S(2)}) async-start(s8[7864320]{0:T(1024)(128)(4,1)} %bitcast.68), calls=%async_computation.5 | async-start | bytes 8388608
  132.3 120.3 %slice-start.1 = ((s8[7864320]{0:T(1024)(128)(4,1)}), s8[3670016]{0:T(1024)(128)(4,1)S(1)}, s32[]{:S(2)}) async-start(s8[7864320]{0:T(1024)(128)(4,1)} %bitcast.68), calls=%async_computation.6 | async-start | bytes 7340032
  252.6 8.3 %copy-start.2 = (bf16[1,1,768,2560]{3,2,1,0:T(8,128)(2,1)S(1)}, bf16[1,1,768,2560]{3,2,1,0:T(8,128)(2,1)}, u32[]{:S(2)}) copy-start(bf16[1,1,768,2560]{3,2,1,0:T(8,128)(2,1)} %param.19) | copy-start | bytes 11796484
  267.0 120.3 %all-to-all-start.1 = ((bf16[16,64,2560]{2,1,0:T(8,128)(2,1)}), bf16[16,64,2560]{2,1,0:T(8,128)(2,1)}, u32[]{:S(2)}, u32[]{:S(2)}) async-start(bf16[16,64,2560]{2,1,0:T(8,128)(2,1)} %bitcast.62), calls=%async_computation.1 | async-start | bytes 10485760 | tf_op jit(solution)/shard_map/all_to_all | solution.py:75
  414.6 17.0 %collective-permute-start = (bf16[128,2560]{1,0:T(8,128)(2,1)S(1)}, bf16[128,2560]{1,0:T(8,128)(2,1)S(1)}, u32[]{:S(2)}, u32[]{:S(2)}) collective-permute-start(bf16[128,2560]{1,0:T(8,128)(2,1)S(1)} %add_convert_fusion), channel_id=1, source_target_pairs={{0,16},{16,0},{1,17},{17,1},{2,18},{18,2},{3,19},{19,3},{4,20},{20... | collective-permute-start | bytes 1966088 | tf_op jit(solution)/shard_map/ppermute | solution.py:9
Sparse Core Ops, SparseCore 0:
  9.6 38.2 all-gather.7
  51.4 37.1 all-gather.5
  90.9 37.2 all-gather.9
where the time goes:
time: 440 us; the launch traced here: 439 us
  waiting for transfers between devices  240 us (55%)
  blocking collectives  120 us (27%)
  local copies, waits for them, and re-layouts  22.7 us (5%)
  matrix products  22.2 us (5%)
  between operations  13.3 us (3%)
  other arithmetic  12.9 us (3%)
  starting transfers between devices  7.16 us (2%)
    all_to_all x1, blocking collectives, on_device(): lax.all_to_all(outgoing, 'expert', split_axis=0, concat_axis=0, tiled=True)  120 us
    all_to_all x1, waiting for transfers between devices, on_device(): lax.all_to_all(result, 'expert', split_axis=0, concat_axis=0, tiled=True)  115 us
    all_gather x1, waiting for transfers between devices, on_device(): lax.all_gather(w_down_kv[0], 'expert', axis=0, tiled=True)  40.6 us
    all_gather x1, waiting for transfers between devices, on_device(): lax.all_gather(w_out[0], 'expert', axis=0, tiled=True)  37.3 us
    all_gather x1, waiting for transfers between devices, on_device(): piece = lax.all_gather(latent, 'expert', axis=0, tiled=True)  31.1 us
    ppermute x1, waiting for transfers between devices, shifted(): return lax.ppermute(x, axis, [(i, (i + by) % count) for i in range(count)])  15.5 us
    gather x1, local copies, waits for them, and re-layouts, on_device(): picked = returned[jnp.maximum(target, 0)]  11.5 us
  transfers between devices with their start and end apart: 5, of which 5 were waited for; matrix products, arithmetic and copies ran while one was open for 2% of the time, Pallas kernels for 0%

commit v1 on v0

v1 whole, which is shorter than its diff:
```python
import functools

import jax
import jax.numpy as jnp
import numpy as np
from jax import lax
from jax.experimental import pallas as pl
from jax.experimental.pallas import tpu as pltpu
from jax.sharding import PartitionSpec as P

BF = jnp.bfloat16
F32 = jnp.float32
VMEM = pl.BlockSpec(memory_space=pltpu.VMEM)
SMEM = pl.BlockSpec(memory_space=pltpu.SMEM)
LIMIT = 48 * 1024 * 1024


def chip_at(place, chips):
    place %= chips
    half = chips // 2
    return 2 * place if place < half else 2 * (chips - 1 - place) + 1


def call(body, outs, ins, limit=LIMIT, flops=0, moved=0):
    return pl.pallas_call(
        body,
        out_shape=outs,
        in_specs=ins,
        out_specs=jax.tree.map(lambda _: VMEM, outs),
        compiler_params=pltpu.CompilerParams(vmem_limit_bytes=limit),
        cost_estimate=pl.CostEstimate(flops=flops, transcendentals=0, bytes_accessed=moved),
    )


def dot(a, b):
    return jnp.dot(a, b, preferred_element_type=F32)


def dot_first(a, b):
    return lax.dot_general(a, b, (((0,), (0,)), ((), ())), preferred_element_type=F32)


def dot_last(a, b):
    return lax.dot_general(a, b, (((1,), (1,)), ((), ())), preferred_element_type=F32)


def slots_of(row, most):
    ids = lax.broadcasted_iota(jnp.int32, (most, row.shape[1]), 0).astype(F32)
    return jnp.where(ids == row, 1.0, 0.0)


def pack_body(routes, gates, capacity, down, out, aux):
    rows, top = routes.shape
    experts = capacity.shape[1]
    width = out.shape[1]
    latent = down.shape[1]
    expert = lax.broadcasted_iota(jnp.int32, (rows, experts), 1)
    named = jnp.zeros((rows, experts), F32)
    gate = jnp.zeros((rows, experts), F32)
    for k in range(top):
        hit = routes[:, k : k + 1] == expert
        named = named + jnp.where(hit, 1.0, 0.0)
        gate = gate + jnp.where(hit, gates[:, k : k + 1], 0.0)
    row = lax.broadcasted_iota(jnp.int32, (rows, rows), 0)
    col = lax.broadcasted_iota(jnp.int32, (rows, rows), 1)
    rank = dot(jnp.where(row > col, 1.0, 0.0).astype(BF), named.astype(BF))
    kept = (named > 0.5) & (rank < capacity[...].astype(F32))
    same = jnp.where(row == col, 1.0, 0.0).astype(BF)
    slot = dot_first(jnp.where(kept, rank, -1.0).astype(BF), same)
    gate = dot_first(jnp.where(kept, gate, 0.0).astype(BF), same)
    aux[...] = jnp.zeros_like(aux)
    for q in range(down.shape[0] // 16):
        aux[0:16, q * latent : (q + 1) * latent] = down[16 * q : 16 * q + 16, :]
    aux[16:32, 0:width] = out[...]
    aux[0:experts, width : width + rows] = slot.astype(BF)
    aux[0:experts, width + rows : width + 2 * rows] = gate.astype(BF)


def unpack_body(groups, ids, aux, down, meta):
    owners, _, wide = aux.shape
    latent = down.shape[1]
    rows = meta.shape[1] // 2
    chips = owners // 2
    for e in range(owners):
        for q in range(groups):
            at = (e * groups + q) * 16
            down[at : at + 16, :] = aux[e, 0:16, q * latent : (q + 1) * latent]
    row = lax.broadcasted_iota(jnp.int32, (32, 2 * rows), 0)
    for part, (blocks, expert) in enumerate(((0, 0), (0, 1), (1, 0))):
        mine = row == ids[2, expert]
        for k in range(chips):
            block = aux[ids[blocks, k], :, wide - 2 * rows : wide].astype(F32)
            meta[part * chips + k : part * chips + k + 1, :] = jnp.sum(
                jnp.where(mine, block, 0.0), 0, keepdims=True
            )


def arrive_body(ks, most, chips, meta, down, gain, *refs):
    count = len(ks)
    pieces, (own, other, latents) = refs[: 2 * count], refs[2 * count :]
    for i, k in enumerate(ks):
        x = jnp.concatenate([pieces[2 * i][...], pieces[2 * i + 1][...]], 0)
        rows = x.shape[0]
        pick = jnp.concatenate(
            [slots_of(meta[j * chips + k : j * chips + k + 1, 0:rows], most) for j in (0, 1)], 0
        ).astype(BF)
        chosen = dot(pick, x).astype(BF)
        own[i] = chosen[:most]
        other[i] = chosen[most:]
        raw = dot(x, down[...])
        scale = lax.rsqrt(jnp.mean(raw * raw, -1, keepdims=True) + 1e-06)
        latents[i] = (raw * scale * gain[...]).astype(BF)


def attend(rows, place, keys, key_place, w_query):
    query = (dot(rows, w_query) * (rows.shape[1] ** -0.5)).astype(BF)
    scores = [
        jnp.where(at <= place, dot_last(query, piece), -1e30)
        for piece, at in zip(keys, key_place, strict=True)
    ]
    peak = functools.reduce(jnp.maximum, [jnp.max(s, -1, keepdims=True) for s in scores])
    weights = [jnp.exp(s - peak) for s in scores]
    total = sum(jnp.sum(w, -1, keepdims=True) for w in weights)
    accum = sum(dot(w.astype(BF), piece) for w, piece in zip(weights, keys, strict=True))
    return (accum / total).astype(BF)


def load_keys(latents, places):
    keys = [ref[...].reshape(-1, ref.shape[-1]) for ref in latents]
    spots, start = [], 0
    for key in keys:
        spots.append(places[:, start : start + key.shape[0]])
        start += key.shape[0]
    return keys, spots


def expert_body(ks, groups, most, chips, ids, meta, places, w_query, w_out, gate_up, expert_down, *refs):
    n = len(groups)
    own, other, lat_a, lat_b = (refs[i * n : (i + 1) * n] for i in range(4))
    out_a, out_b = refs[4 * n :]
    rows = lat_a[0].shape[1]
    hidden_width = expert_down.shape[0]
    keys, spots = load_keys(list(lat_a) + list(lat_b), places)
    where = {k: (g, i) for g, group in enumerate(groups) for i, k in enumerate(group)}
    chosen, latent, place, gate = [], [], [], []
    for side, (xs, lats) in enumerate(((own, lat_a), (other, lat_b))):
        for k in ks:
            g, i = where[k]
            at = (0 if side == 0 else 2 * chips) + k
            pick = slots_of(meta[at : at + 1, 0:rows], most)
            token = lax.broadcasted_iota(jnp.int32, (most, rows), 1).astype(F32)
            spot = jnp.sum(pick * token, -1, keepdims=True).astype(jnp.int32)
            place.append(spot + ids[side, k] * rows)
            gate.append(jnp.sum(pick * meta[at : at + 1, rows : 2 * rows], -1, keepdims=True))
            latent.append(dot(pick.astype(BF), lats[g][i]).astype(BF))
            chosen.append(xs[g][i])
    attended = attend(
        jnp.concatenate(latent, 0), jnp.concatenate(place, 0), keys, spots, w_query[...]
    )
    hidden = (jnp.concatenate(chosen, 0).astype(F32) + dot(attended, w_out[...])).astype(BF)
    both = dot(hidden, gate_up[...])
    inner = (jax.nn.silu(both[:, :hidden_width]) * both[:, hidden_width:]).astype(BF)
    result = (dot(inner, expert_down[...]) * jnp.concatenate(gate, 0)).astype(BF)
    half = len(ks) * most
    out_a[...] = result[:half]
    out_b[...] = result[half:]


def spread(k, most, chips, rows, meta, mine, theirs, cols):
    one = slots_of(meta[k : k + 1, 0:rows], most).astype(BF)
    two = slots_of(meta[chips + k : chips + k + 1, 0:rows], most).astype(BF)
    return dot_first(one, mine[:, cols]) + dot_first(two, theirs[:, cols])


def combine_body(k, at, most, chips, first, size, meta, mine, theirs, *refs):
    rows = meta.shape[1] // 2
    cols = slice(first, first + size)
    spot = slice(at * most, (at + 1) * most)
    total = spread(k, most, chips, rows, meta, mine.at[spot], theirs.at[spot], cols)
    if len(refs) > 1:
        total = total + refs[0][...].astype(F32)
    refs[-1][...] = total.astype(BF)


def own_body(at, most, chips, n, ids, meta, places, w_query, w_out, tokens, mine, theirs, *refs):
    latents, outs = refs[: 2 * n], refs[2 * n :]
    rows = tokens.shape[0]
    keys, spots = load_keys(latents, places)
    place = ids[0, 0] * rows + lax.broadcasted_iota(jnp.int32, (rows, 1), 0)
    attended = attend(latents[0][0], place, keys, spots, w_query[...])
    hidden = (tokens[...].astype(F32) + dot(attended, w_out[...])).astype(BF).astype(F32)
    spot = slice(at * most, (at + 1) * most)
    first = 0
    for out in outs:
        cols = slice(first, first + out.shape[1])
        total = spread(0, most, chips, rows, meta, mine.at[spot], theirs.at[spot], cols)
        out[...] = (hidden[:, cols] + total).astype(BF)
        first += out.shape[1]


def final_body(*refs):
    ins, out = refs[:-1], refs[-1]
    first = 0
    for one, two in zip(ins[0::2], ins[1::2], strict=True):
        size = one.shape[1]
        out[:, first : first + size] = (one[...].astype(F32) + two[...].astype(F32)).astype(BF)
        first += size


def on_device(
    tokens, routes, gates, capacity, w_down_kv, kv_gain, w_query, w_out, w_gate_up, w_expert_down
):
    pipes = lax.axis_size("pipe")
    owners = lax.axis_size("expert")
    chips = owners // 2
    me = lax.axis_index("expert")
    rows, width = tokens.shape[1:]
    top = routes.shape[2]
    latent = w_query.shape[1]
    most = max(2, 4 * rows * top // (3 * owners))
    shape = jax.ShapeDtypeStruct

    ring, blocks = [], np.zeros((owners, chips), np.int32)
    for r in range(chips):
        even, odd = 2 * chip_at(r, chips), 2 * chip_at(r, chips) + 1
        ring.append((even, 2 * chip_at(r + 1, chips)))
        ring.append((odd, 2 * chip_at(r - 1, chips) + 1))
        for k in range(chips):
            blocks[even, k] = 2 * chip_at(r - k, chips)
            blocks[odd, k] = 2 * chip_at(r + k, chips) + 1
    step = lambda x: lax.ppermute(x, "expert", ring)
    sibling = lambda x: lax.ppermute(x, "expert", [(i, i ^ 1) for i in range(owners)])
    last = [
        (p * owners + a, ((p + 1) % pipes) * owners + b) for p in range(pipes) for a, b in ring
    ]
    onward = lambda x: lax.ppermute(x, "pipe", [(p, (p + 1) % pipes) for p in range(pipes)])

    table = jnp.asarray(np.stack([blocks, blocks[np.arange(owners) ^ 1]], 1))
    order = lax.dynamic_index_in_dim(table, me, 0, keepdims=False)
    whose = jnp.zeros((chips,), jnp.int32).at[0].set(me).at[1].set(me ^ 1)
    ids = jnp.concatenate([order, whose[None]], 0)
    places = (order[:, :, None] * rows + jnp.arange(rows)[None, None, :]).reshape(1, -1)

    out_shard = w_out[0]
    if out_shard.shape[0] < 16:
        out_shard = jnp.pad(out_shard, ((0, 16 - out_shard.shape[0]), (0, 0)))
    aux = call(pack_body, shape((32, width + 2 * rows), BF), [VMEM] * 5)(
        routes[0], gates[0], capacity, w_down_kv[0], out_shard
    )
    aux = lax.all_gather(aux, "expert", axis=0)
    down, meta = call(
        functools.partial(unpack_body, w_down_kv.shape[1] // 16),
        (shape((owners * w_down_kv.shape[1], latent), BF), shape((3 * chips, 2 * rows), F32)),
        [SMEM, VMEM],
    )(ids, aux)
    out_proj = aux[:, 16 : 16 + w_out.shape[1], :width].reshape(-1, width)

    half = rows // 2
    held = [(tokens[0, :half], tokens[0, half:])]
    for k in range(1, chips):
        held.append(tuple(step(x) for x in held[-1]))

    cut = chips - 2
    groups = (tuple(range(cut)), tuple(range(cut, chips)))
    own, other, lat_a, lat_b = [], [], [], []
    for group in groups:
        n = len(group)
        picked, away, lat = call(
            functools.partial(arrive_body, group, most, chips),
            (
                shape((n, most, width), BF),
                shape((n, most, width), BF),
                shape((n, rows, latent), BF),
            ),
            [VMEM] * (3 + 2 * n),
            flops=2 * n * rows * width * (latent + 2 * most),
        )(meta, down, kv_gain, *[x for k in group for x in held[k]])
        own.append(picked)
        other.append(sibling(away))
        lat_a.append(lat)
        lat_b.append(sibling(lat))

    sequence = list(range(1, chips)) + [0]
    chunks = [sequence[i : i + 2] for i in range(0, chips, 2)]
    gate_up, expert_down = w_gate_up[0, 0], w_expert_down[0, 0]
    mine, theirs = {}, {}
    for ks in chunks:
        size = len(ks) * most
        out_a, out_b = call(
            functools.partial(expert_body, tuple(ks), groups, most, chips),
            (shape((size, width), BF), shape((size, width), BF)),
            [SMEM] + [VMEM] * (6 + 4 * len(groups)),
            flops=4 * size * (3 * width * expert_down.shape[0] + 2 * latent * owners * rows),
        )(
            ids,
            meta,
            places,
            w_query[0],
            out_proj,
            gate_up,
            expert_down,
            *own,
            *other,
            *lat_a,
            *lat_b,
        )
        back = sibling(out_b)
        for i, k in enumerate(ks):
            mine[k], theirs[k] = (out_a, i), (back, i)

    pieces = [(0, width // 2), (width // 2, width - width // 2)]
    passing = [None] * len(pieces)
    for k in range(1, chips):
        for i, (first, size) in enumerate(pieces):
            more = [] if passing[i] is None else [passing[i]]
            total = call(
                functools.partial(combine_body, k, mine[k][1], most, chips, first, size),
                shape((rows, size), BF),
                [VMEM] * (3 + len(more)),
                flops=4 * rows * most * size,
            )(meta, mine[k][0], theirs[k][0], *more)
            if k < chips - 1:
                passing[i] = step(total)
            else:
                passing[i] = lax.ppermute(total, ("pipe", "expert"), last)
    kept = call(
        functools.partial(own_body, mine[0][1], most, chips, len(groups)),
        tuple(shape((rows, size), BF) for _, size in pieces),
        [SMEM] + [VMEM] * (7 + 2 * len(groups)),
        flops=2 * rows * latent * (width + 2 * owners * rows),
    )(ids, meta, places, w_query[0], out_proj, tokens[0], mine[0][0], theirs[0][0], *lat_a, *lat_b)
    kept = [onward(x) for x in kept]
    output = call(final_body, shape((rows, width), BF), [VMEM] * (2 * len(pieces)))(
        *[x for pair in zip(kept, passing, strict=True) for x in pair]
    )
    return output[None]


def solution(mesh):
    return jax.shard_map(
        on_device,
        mesh=mesh,
        in_specs=(
            P("pipe", "expert", None),
            P("pipe", "expert", None),
            P("pipe", "expert", None),
            P("pipe", None),
            P("pipe", "expert", None),
            P("pipe", None),
            P("pipe", None, None),
            P("pipe", "expert", None),
            P("pipe", "expert", None, None),
            P("pipe", "expert", None, None),
        ),
        out_specs=P("pipe", "expert", None),
        check_vma=False,
    )
```

time: 440 us -> 221 us (0.50)
  the two profiles are of different devices: /device:TPU:12 before, /device:TPU:0 now
where the time goes in v1:
time: 221 us; the launch traced here: 220 us
  waiting for transfers between devices  78.6 us (36%)
  Pallas kernels  59.8 us (27%)
  starting transfers between devices  56.9 us (26%)
  between operations  13.7 us (6%)
  local copies, waits for them, and re-layouts  10.4 us (5%)
    ppermute x26, waiting for transfers between devices, on_device(): step = lambda x: lax.ppermute(x, 'expert', ring)  53.8 us
    ppermute x26, starting transfers between devices, on_device(): step = lambda x: lax.ppermute(x, 'expert', ring)  50.3 us
    pallas_call x4, Pallas kernels, on_device(): call(functools.partial(expert_body, tuple(ks), groups, most, chips), (sha...  43.3 us
    ppermute x2, waiting for transfers between devices, on_device(): lax.ppermute(x, 'pipe', [(p, (p + 1) % pipes) for p in range(pipes)])  18.6 us
    unnamed x18, local copies, waits for them, and re-layouts  7.11 us
    ppermute x2, waiting for transfers between devices, on_device(): passing[i] = lax.ppermute(total, ('pipe', 'expert'), last)  6.14 us
    pallas_call x2, Pallas kernels, on_device(): call(functools.partial(arrive_body, group, most, chips), (shape((n, most,...  6.11 us
    pallas_call x14, Pallas kernels, on_device(): call(functools.partial(combine_body, k, mine[k][1], most, chips, first, s...  5.03 us
  transfers between devices with their start and end apart: 39, of which 24 were waited for; matrix products, arithmetic and copies ran while one was open for 2% of the time, Pallas kernels for 19%

profile of v1, /device:TPU:0, one launch (start us, length us, event | category | flops | bytes accessed | tf_op | source)
XLA Modules:
  0.0 220.3 jit_solution(11493234572814146657)
XLA Ops:
  12.9 3.1 %collective-permute-start.1 = (bf16[64,2560]{1,0:T(8,128)(2,1)S(1)}, bf16[64,2560]{1,0:T(8,128)(2,1)S(1)}, u32[]{:S(2)}, u32[]{:S(2)}) collective-permute-start(bf16[64,2560]{1,0:T(8,128)(2,1)S(1)} %get-tuple-element.65.refs_1_), channel_id=1, source_target_pairs={{0,4},{1,3},{4,8},{5,1},{8,12},{9,5},{12,14},{13,9},{14,10},{15,13... | collective-permute-start | bytes 983048 | tf_op jit(solution)/shard_map/ppermute | solution.py:231
  17.6 3.4 %collective-permute-done.1.refs_3_ = bf16[64,2560]{1,0:T(8,128)(2,1)S(1)} collective-permute-done((bf16[64,2560]{1,0:T(8,128)(2,1)S(1)}, bf16[64,2560]{1,0:T(8,128)(2,1)S(1)}, u32[]{:S(2)}, u32[]{:S(2)}) %collective-permute-start.1) | collective-permute-done | bytes 327712 | tf_op jit(solution)/shard_map/ppermute | solution.py:231
  23.1 2.7 %collective-permute-done.refs_2_ = bf16[64,2560]{1,0:T(8,128)(2,1)S(1)} collective-permute-done((bf16[64,2560]{1,0:T(8,128)(2,1)S(1)}, bf16[64,2560]{1,0:T(8,128)(2,1)S(1)}, u32[]{:S(2)}, u32[]{:S(2)}) %collective-permute-start) | collective-permute-done | bytes 327712 | tf_op jit(solution)/shard_map/ppermute | solution.py:231
  28.3 3.4 %collective-permute-done.3.refs_5_ = bf16[64,2560]{1,0:T(8,128)(2,1)S(1)} collective-permute-done((bf16[64,2560]{1,0:T(8,128)(2,1)S(1)}, bf16[64,2560]{1,0:T(8,128)(2,1)S(1)}, u32[]{:S(2)}, u32[]{:S(2)}) %collective-permute-start.3) | collective-permute-done | bytes 327712 | tf_op jit(solution)/shard_map/ppermute | solution.py:231
  34.2 2.7 %collective-permute-done.2.refs_4_ = bf16[64,2560]{1,0:T(8,128)(2,1)S(1)} collective-permute-done((bf16[64,2560]{1,0:T(8,128)(2,1)S(1)}, bf16[64,2560]{1,0:T(8,128)(2,1)S(1)}, u32[]{:S(2)}, u32[]{:S(2)}) %collective-permute-start.2) | collective-permute-done | bytes 327712 | tf_op jit(solution)/shard_map/ppermute | solution.py:231
  42.9 6.5 %collective-permute-done.4.refs_6_ = bf16[64,2560]{1,0:T(8,128)(2,1)S(1)} collective-permute-done((bf16[64,2560]{1,0:T(8,128)(2,1)S(1)}, bf16[64,2560]{1,0:T(8,128)(2,1)S(1)}, u32[]{:S(2)}, u32[]{:S(2)}) %collective-permute-start.4) | collective-permute-done | bytes 327712 | tf_op jit(solution)/shard_map/ppermute | solution.py:231
  51.9 3.8 %collective-permute-done.7.refs_9_ = bf16[64,2560]{1,0:T(8,128)(2,1)S(1)} collective-permute-done((bf16[64,2560]{1,0:T(8,128)(2,1)S(1)}, bf16[64,2560]{1,0:T(8,128)(2,1)S(1)}, u32[]{:S(2)}, u32[]{:S(2)}) %collective-permute-start.7) | collective-permute-done | bytes 327712 | tf_op jit(solution)/shard_map/ppermute | solution.py:231
  55.7 3.1 %collective-permute-start.9 = (bf16[64,2560]{1,0:T(8,128)(2,1)S(1)}, bf16[64,2560]{1,0:T(8,128)(2,1)}, u32[]{:S(2)}, u32[]{:S(2)}) collective-permute-start(bf16[64,2560]{1,0:T(8,128)(2,1)S(1)} %collective-permute-done.7.refs_9_), channel_id=1, source_target_pairs={{0,4},{1,3},{4,8},{5,1},{8,12},{9,5},{12,14},{13,9},{14,10},{15,13... | collective-permute-start | bytes 983048 | tf_op jit(solution)/shard_map/ppermute | solution.py:231
  58.8 3.8 %collective-permute-done.6.refs_8_ = bf16[64,2560]{1,0:T(8,128)(2,1)S(1)} collective-permute-done((bf16[64,2560]{1,0:T(8,128)(2,1)S(1)}, bf16[64,2560]{1,0:T(8,128)(2,1)S(1)}, u32[]{:S(2)}, u32[]{:S(2)}) %collective-permute-start.6) | collective-permute-done | bytes 327712 | tf_op jit(solution)/shard_map/ppermute | solution.py:231
  70.2 5.2 %shard_map.111 = (bf16[6,64,2560]{2,1,0:T(8,128)(2,1)}, bf16[6,64,2560]{2,1,0:T(8,128)(2,1)}, bf16[6,128,256]{2,1,0:T(8,128)(2,1)S(1)}) custom-call(f32[24,256]{1,0:T(8,128)S(1)} %get-tuple-element.47.meta, bf16[2560,256]{1,0:T(8,128)(2,1)S(1)} %get-tuple-element.48.down, f32[1,256]{1,0:T(1,128)S(1)} %copy-done.5, ...), custom_call_target="tpu_custom_call" | custom-call | flops 1509949440 | tf_op jit(solution)/shard_map/pallas_call | solution.py:268
  79.0 3.7 %collective-permute-done.11.refs_1_ = bf16[64,2560]{1,0:T(8,128)(2,1)S(1)} collective-permute-done((bf16[64,2560]{1,0:T(8,128)(2,1)}, bf16[64,2560]{1,0:T(8,128)(2,1)S(1)}, u32[]{:S(2)}, u32[]{:S(2)}) %collective-permute-start.11) | collective-permute-done | bytes 327712 | tf_op jit(solution)/shard_map/ppermute | solution.py:231
  89.8 3.5 %collective-permute-done.12.refs_2_ = bf16[64,2560]{1,0:T(8,128)(2,1)S(1)} collective-permute-done((bf16[64,2560]{1,0:T(8,128)(2,1)S(1)}, bf16[64,2560]{1,0:T(8,128)(2,1)S(1)}, u32[]{:S(2)}, u32[]{:S(2)}) %collective-permute-start.12) | collective-permute-done | bytes 327712 | tf_op jit(solution)/shard_map/ppermute | solution.py:231
  98.4 10.8 %shard_map.117 = (bf16[128,2560]{1,0:T(8,128)(2,1)S(1)}, bf16[128,2560]{1,0:T(8,128)(2,1)S(1)}) custom-call(s32[3,8]{1,0:T(4,128)S(1)} %pad_add_fusion.ids, f32[24,256]{1,0:T(8,128)S(1)} %get-tuple-element.47.meta, s32[1,2048]{1,0:T(1,128)S(1)} %bitcast.37, bf16[256,256]{1,0:T(8,128)(2,1)S(1)} %bitcast.31, bf16[256,2560]{1,0:T(8,128)(2,1)S(1)} %bitcast.24, ...), custom_call_target="tpu_custom_call" | custom-call | flops 3556769792 | tf_op jit(solution)/shard_map/pallas_call | solution.py:289
  109.7 10.8 %shard_map.116 = (bf16[128,2560]{1,0:T(8,128)(2,1)S(1)}, bf16[128,2560]{1,0:T(8,128)(2,1)S(1)}) custom-call(s32[3,8]{1,0:T(4,128)S(1)} %pad_add_fusion.ids, f32[24,256]{1,0:T(8,128)S(1)} %get-tuple-element.47.meta, s32[1,2048]{1,0:T(1,128)S(1)} %bitcast.38, bf16[256,256]{1,0:T(8,128)(2,1)S(1)} %bitcast.32, bf16[256,2560]{1,0:T(8,128)(2,1)S(1)} %bitcast.25, ...), custom_call_target="tpu_custom_call" | custom-call | flops 3556769792 | tf_op jit(solution)/shard_map/pallas_call | solution.py:289
  125.0 3.1 %collective-permute-done.23.refs_0_ = bf16[128,1280]{1,0:T(8,128)(2,1)S(1)} collective-permute-done((bf16[128,1280]{1,0:T(8,128)(2,1)S(1)}, bf16[128,1280]{1,0:T(8,128)(2,1)S(1)}, u32[]{:S(2)}, u32[]{:S(2)}) %collective-permute-start.23) | collective-permute-done | bytes 327712 | tf_op jit(solution)/shard_map/ppermute | solution.py:231
  141.7 10.8 %shard_map.115 = (bf16[128,2560]{1,0:T(8,128)(2,1)S(1)}, bf16[128,2560]{1,0:T(8,128)(2,1)S(1)}) custom-call(s32[3,8]{1,0:T(4,128)S(1)} %pad_add_fusion.ids, f32[24,256]{1,0:T(8,128)S(1)} %get-tuple-element.47.meta, s32[1,2048]{1,0:T(1,128)S(1)} %bitcast.39, bf16[256,256]{1,0:T(8,128)(2,1)S(1)} %bitcast.33, bf16[256,2560]{1,0:T(8,128)(2,1)S(1)} %bitcast.26, ...), custom_call_target="tpu_custom_call" | custom-call | flops 3556769792 | tf_op jit(solution)/shard_map/pallas_call | solution.py:289
  156.7 10.8 %shard_map.113 = (bf16[128,2560]{1,0:T(8,128)(2,1)S(1)}, bf16[128,2560]{1,0:T(8,128)(2,1)S(1)}) custom-call(s32[3,8]{1,0:T(4,128)S(1)} %pad_add_fusion.ids, f32[24,256]{1,0:T(8,128)S(1)} %get-tuple-element.47.meta, s32[1,2048]{1,0:T(1,128)S(1)} %bitcast.40, bf16[256,256]{1,0:T(8,128)(2,1)S(1)} %bitcast.34, bf16[256,2560]{1,0:T(8,128)(2,1)S(1)} %bitcast.27, ...), custom_call_target="tpu_custom_call" | custom-call | flops 3556769792 | tf_op jit(solution)/shard_map/pallas_call | solution.py:289
  170.5 4.6 %collective-permute-done.27.refs_0_ = bf16[128,1280]{1,0:T(8,128)(2,1)S(1)} collective-permute-done((bf16[128,1280]{1,0:T(8,128)(2,1)S(1)}, bf16[128,1280]{1,0:T(8,128)(2,1)S(1)}, u32[]{:S(2)}, u32[]{:S(2)}) %collective-permute-start.27) | collective-permute-done | bytes 327712 | tf_op jit(solution)/shard_map/ppermute | solution.py:231
  175.6 3.0 %collective-permute-done.35.refs_0_ = bf16[128,1280]{1,0:T(8,128)(2,1)S(1)} collective-permute-done((bf16[128,1280]{1,0:T(8,128)(2,1)S(1)}, bf16[128,1280]{1,0:T(8,128)(2,1)S(1)}, u32[]{:S(2)}, u32[]{:S(2)}) %collective-permute-start.35) | collective-permute-done | bytes 327712 | tf_op jit(solution)/shard_map/ppermute | solution.py:231
  184.0 2.9 %collective-permute-start.29 = (bf16[128,1280]{1,0:T(8,128)(2,1)S(1)}, bf16[128,1280]{1,0:T(8,128)(2,1)S(1)}, u32[]{:S(2)}, u32[]{:S(2)}) collective-permute-start(bf16[128,1280]{1,0:T(8,128)(2,1)S(1)} %shard_map.124), channel_id=1, source_target_pairs={{0,20},{1,19},{4,24},{5,17},{8,28},{9,21},{12,30},{13,25},{14,26},... | collective-permute-start | bytes 983048 | tf_op jit(solution)/shard_map/ppermute | solution.py:325
  187.7 11.5 %collective-permute-done.19.refs_0_ = bf16[128,1280]{1,0:T(8,128)(2,1)S(1)} collective-permute-done((bf16[128,1280]{1,0:T(8,128)(2,1)S(1)}, bf16[128,1280]{1,0:T(8,128)(2,1)S(1)}, u32[]{:S(2)}, u32[]{:S(2)}) %collective-permute-start.19) | collective-permute-done | bytes 327712 | tf_op jit(solution)/shard_map/ppermute | solution.py:236
  199.3 7.0 %collective-permute-done.30.refs_2_ = bf16[128,1280]{1,0:T(8,128)(2,1)S(1)} collective-permute-done((bf16[128,1280]{1,0:T(8,128)(2,1)S(1)}, bf16[128,1280]{1,0:T(8,128)(2,1)S(1)}, u32[]{:S(2)}, u32[]{:S(2)}) %collective-permute-start.30) | collective-permute-done | bytes 327712 | tf_op jit(solution)/shard_map/ppermute | solution.py:236
  206.3 2.6 %collective-permute-done.29.refs_1_ = bf16[128,1280]{1,0:T(8,128)(2,1)S(1)} collective-permute-done((bf16[128,1280]{1,0:T(8,128)(2,1)S(1)}, bf16[128,1280]{1,0:T(8,128)(2,1)S(1)}, u32[]{:S(2)}, u32[]{:S(2)}) %collective-permute-start.29) | collective-permute-done | bytes 327712 | tf_op jit(solution)/shard_map/ppermute | solution.py:325
  208.9 3.5 %collective-permute-done.37.refs_3_ = bf16[128,1280]{1,0:T(8,128)(2,1)S(1)} collective-permute-done((bf16[128,1280]{1,0:T(8,128)(2,1)S(1)}, bf16[128,1280]{1,0:T(8,128)(2,1)S(1)}, u32[]{:S(2)}, u32[]{:S(2)}) %collective-permute-start.37) | collective-permute-done | bytes 327712 | tf_op jit(solution)/shard_map/ppermute | solution.py:325
  (105 shorter events, 80.0 us)
Async XLA Ops:
  6.5 59.3 %all-gather.3.cloned.1.call-start = ((), (), s32[]{:S(2)}) async-start(), calls=%async_computation | async-start | bytes 3063808 | tf_op jit(solution)/shard_map/all_gather | solution.py:250
  16.0 9.8 %collective-permute-start = (bf16[64,2560]{1,0:T(8,128)(2,1)S(1)}, bf16[64,2560]{1,0:T(8,128)(2,1)S(1)}, u32[]{:S(2)}, u32[]{:S(2)}) collective-permute-start(bf16[64,2560]{1,0:T(8,128)(2,1)S(1)} %get-tuple-element.66.refs_0_), channel_id=1, source_target_pairs={{0,4},{1,3},{4,8},{5,1},{8,12},{9,5},{12,14},{13,9},{14,10},{15,13... | collective-permute-start | bytes 983048 | tf_op jit(solution)/shard_map/ppermute | solution.py:231
  21.0 10.7 %collective-permute-start.3 = (bf16[64,2560]{1,0:T(8,128)(2,1)S(1)}, bf16[64,2560]{1,0:T(8,128)(2,1)S(1)}, u32[]{:S(2)}, u32[]{:S(2)}) collective-permute-start(bf16[64,2560]{1,0:T(8,128)(2,1)S(1)} %collective-permute-done.1.refs_3_), channel_id=1, source_target_pairs={{0,4},{1,3},{4,8},{5,1},{8,12},{9,5},{12,14},{13,9},{14,10},{15,13... | collective-permute-start | bytes 983048 | tf_op jit(solution)/shard_map/ppermute | solution.py:231
  25.8 11.1 %collective-permute-start.2 = (bf16[64,2560]{1,0:T(8,128)(2,1)S(1)}, bf16[64,2560]{1,0:T(8,128)(2,1)S(1)}, u32[]{:S(2)}, u32[]{:S(2)}) collective-permute-start(bf16[64,2560]{1,0:T(8,128)(2,1)S(1)} %collective-permute-done.refs_2_), channel_id=1, source_target_pairs={{0,4},{1,3},{4,8},{5,1},{8,12},{9,5},{12,14},{13,9},{14,10},{15,13... | collective-permute-start | bytes 983048 | tf_op jit(solution)/shard_map/ppermute | solution.py:231
  31.7 8.7 %collective-permute-start.5 = (bf16[64,2560]{1,0:T(8,128)(2,1)S(1)}, bf16[64,2560]{1,0:T(8,128)(2,1)S(1)}, u32[]{:S(2)}, u32[]{:S(2)}) collective-permute-start(bf16[64,2560]{1,0:T(8,128)(2,1)S(1)} %collective-permute-done.3.refs_5_), channel_id=1, source_target_pairs={{0,4},{1,3},{4,8},{5,1},{8,12},{9,5},{12,14},{13,9},{14,10},{15,13... | collective-permute-start | bytes 983048 | tf_op jit(solution)/shard_map/ppermute | solution.py:231
  36.9 12.5 %collective-permute-start.4 = (bf16[64,2560]{1,0:T(8,128)(2,1)S(1)}, bf16[64,2560]{1,0:T(8,128)(2,1)S(1)}, u32[]{:S(2)}, u32[]{:S(2)}) collective-permute-start(bf16[64,2560]{1,0:T(8,128)(2,1)S(1)} %collective-permute-done.2.refs_4_), channel_id=1, source_target_pairs={{0,4},{1,3},{4,8},{5,1},{8,12},{9,5},{12,14},{13,9},{14,10},{15,13... | collective-permute-start | bytes 983048 | tf_op jit(solution)/shard_map/ppermute | solution.py:231
  40.4 15.3 %collective-permute-start.7 = (bf16[64,2560]{1,0:T(8,128)(2,1)S(1)}, bf16[64,2560]{1,0:T(8,128)(2,1)S(1)}, u32[]{:S(2)}, u32[]{:S(2)}) collective-permute-start(bf16[64,2560]{1,0:T(8,128)(2,1)S(1)} %collective-permute-done.5.refs_7_), channel_id=1, source_target_pairs={{0,4},{1,3},{4,8},{5,1},{8,12},{9,5},{12,14},{13,9},{14,10},{15,13... | collective-permute-start | bytes 983048 | tf_op jit(solution)/shard_map/ppermute | solution.py:231
  49.4 13.2 %collective-permute-start.6 = (bf16[64,2560]{1,0:T(8,128)(2,1)S(1)}, bf16[64,2560]{1,0:T(8,128)(2,1)S(1)}, u32[]{:S(2)}, u32[]{:S(2)}) collective-permute-start(bf16[64,2560]{1,0:T(8,128)(2,1)S(1)} %collective-permute-done.4.refs_6_), channel_id=1, source_target_pairs={{0,4},{1,3},{4,8},{5,1},{8,12},{9,5},{12,14},{13,9},{14,10},{15,13... | collective-permute-start | bytes 983048 | tf_op jit(solution)/shard_map/ppermute | solution.py:231
  55.7 12.8 %collective-permute-start.9 = (bf16[64,2560]{1,0:T(8,128)(2,1)S(1)}, bf16[64,2560]{1,0:T(8,128)(2,1)}, u32[]{:S(2)}, u32[]{:S(2)}) collective-permute-start(bf16[64,2560]{1,0:T(8,128)(2,1)S(1)} %collective-permute-done.7.refs_9_), channel_id=1, source_target_pairs={{0,4},{1,3},{4,8},{5,1},{8,12},{9,5},{12,14},{13,9},{14,10},{15,13... | collective-permute-start | bytes 983048 | tf_op jit(solution)/shard_map/ppermute | solution.py:231
  75.4 21.7 %collective-permute-start.14 = (bf16[6,64,2560]{2,1,0:T(8,128)(2,1)}, bf16[6,64,2560]{2,1,0:T(8,128)(2,1)S(1)}, u32[]{:S(2)}, u32[]{:S(2)}) collective-permute-start(bf16[6,64,2560]{2,1,0:T(8,128)(2,1)} %get-tuple-element.51), channel_id=1, source_target_pairs={{0,1},{1,0},{2,3},{3,2},{4,5},{5,4},{6,7},{7,6},{8,9},{9,8},{10,11... | collective-permute-start | bytes 5898248 | tf_op jit(solution)/shard_map/ppermute | solution.py:232
  77.4 8.8 %collective-permute-start.10 = (bf16[64,2560]{1,0:T(8,128)(2,1)}, bf16[64,2560]{1,0:T(8,128)(2,1)S(1)}, u32[]{:S(2)}, u32[]{:S(2)}) collective-permute-start(bf16[64,2560]{1,0:T(8,128)(2,1)} %collective-permute-done.8.refs_10_), channel_id=1, source_target_pairs={{0,4},{1,3},{4,8},{5,1},{8,12},{9,5},{12,14},{13,9},{14,10},{15,13... | collective-permute-start | bytes 983048 | tf_op jit(solution)/shard_map/ppermute | solution.py:231
  109.3 11.3 %collective-permute-start.22 = (bf16[128,2560]{1,0:T(8,128)(2,1)S(1)}, bf16[128,2560]{1,0:T(8,128)(2,1)S(1)}, u32[]{:S(2)}, u32[]{:S(2)}) collective-permute-start(bf16[128,2560]{1,0:T(8,128)(2,1)S(1)} %get-tuple-element.63), channel_id=1, source_target_pairs={{0,1},{1,0},{2,3},{3,2},{4,5},{5,4},{6,7},{7,6},{8,9},{9,8},{10,11... | collective-permute-start | bytes 1966088 | tf_op jit(solution)/shard_map/ppermute | solution.py:232
  123.0 11.0 %collective-permute-start.21 = (bf16[128,2560]{1,0:T(8,128)(2,1)S(1)}, bf16[128,2560]{1,0:T(8,128)(2,1)S(1)}, u32[]{:S(2)}, u32[]{:S(2)}) collective-permute-start(bf16[128,2560]{1,0:T(8,128)(2,1)S(1)} %get-tuple-element.61), channel_id=1, source_target_pairs={{0,1},{1,0},{2,3},{3,2},{4,5},{5,4},{6,7},{7,6},{8,9},{9,8},{10,11... | collective-permute-start | bytes 1966088 | tf_op jit(solution)/shard_map/ppermute | solution.py:232
  135.9 16.7 %collective-permute-start.25 = (bf16[128,1280]{1,0:T(8,128)(2,1)S(1)}, bf16[128,1280]{1,0:T(8,128)(2,1)S(1)}, u32[]{:S(2)}, u32[]{:S(2)}) collective-permute-start(bf16[128,1280]{1,0:T(8,128)(2,1)S(1)} %shard_map.120), channel_id=1, source_target_pairs={{0,4},{1,3},{4,8},{5,1},{8,12},{9,5},{12,14},{13,9},{14,10},{15,13... | collective-permute-start | bytes 983048 | tf_op jit(solution)/shard_map/ppermute | solution.py:231
  139.4 15.2 %collective-permute-start.33 = (bf16[128,1280]{1,0:T(8,128)(2,1)S(1)}, bf16[128,1280]{1,0:T(8,128)(2,1)S(1)}, u32[]{:S(2)}, u32[]{:S(2)}) collective-permute-start(bf16[128,1280]{1,0:T(8,128)(2,1)S(1)} %shard_map.127), channel_id=1, source_target_pairs={{0,4},{1,3},{4,8},{5,1},{8,12},{9,5},{12,14},{13,9},{14,10},{15,13... | collective-permute-start | bytes 983048 | tf_op jit(solution)/shard_map/ppermute | solution.py:231
  152.6 15.0 %collective-permute-start.20 = (bf16[128,2560]{1,0:T(8,128)(2,1)S(1)}, bf16[128,2560]{1,0:T(8,128)(2,1)S(1)}, u32[]{:S(2)}, u32[]{:S(2)}) collective-permute-start(bf16[128,2560]{1,0:T(8,128)(2,1)S(1)} %get-tuple-element.59), channel_id=1, source_target_pairs={{0,1},{1,0},{2,3},{3,2},{4,5},{5,4},{6,7},{7,6},{8,9},{9,8},{10,11... | collective-permute-start | bytes 1966088 | tf_op jit(solution)/shard_map/ppermute | solution.py:232
  153.0 14.6 %collective-permute-start.26 = (bf16[128,1280]{1,0:T(8,128)(2,1)S(1)}, bf16[128,1280]{1,0:T(8,128)(2,1)S(1)}, u32[]{:S(2)}, u32[]{:S(2)}) collective-permute-start(bf16[128,1280]{1,0:T(8,128)(2,1)S(1)} %shard_map.121), channel_id=1, source_target_pairs={{0,4},{1,3},{4,8},{5,1},{8,12},{9,5},{12,14},{13,9},{14,10},{15,13... | collective-permute-start | bytes 983048 | tf_op jit(solution)/shard_map/ppermute | solution.py:231
  155.0 13.1 %collective-permute-start.34 = (bf16[128,1280]{1,0:T(8,128)(2,1)S(1)}, bf16[128,1280]{1,0:T(8,128)(2,1)S(1)}, u32[]{:S(2)}, u32[]{:S(2)}) collective-permute-start(bf16[128,1280]{1,0:T(8,128)(2,1)S(1)} %shard_map.128), channel_id=1, source_target_pairs={{0,4},{1,3},{4,8},{5,1},{8,12},{9,5},{12,14},{13,9},{14,10},{15,13... | collective-permute-start | bytes 983048 | tf_op jit(solution)/shard_map/ppermute | solution.py:231
  167.5 11.6 %collective-permute-start.18 = (bf16[128,2560]{1,0:T(8,128)(2,1)S(1)}, bf16[128,2560]{1,0:T(8,128)(2,1)S(1)}, u32[]{:S(2)}, u32[]{:S(2)}) collective-permute-start(bf16[128,2560]{1,0:T(8,128)(2,1)S(1)} %get-tuple-element.56), channel_id=1, source_target_pairs={{0,1},{1,0},{2,3},{3,2},{4,5},{5,4},{6,7},{7,6},{8,9},{9,8},{10,11... | collective-permute-start | bytes 1966088 | tf_op jit(solution)/shard_map/ppermute | solution.py:232
  168.5 10.1 %collective-permute-start.35 = (bf16[128,1280]{1,0:T(8,128)(2,1)S(1)}, bf16[128,1280]{1,0:T(8,128)(2,1)S(1)}, u32[]{:S(2)}, u32[]{:S(2)}) collective-permute-start(bf16[128,1280]{1,0:T(8,128)(2,1)S(1)} %shard_map.129), channel_id=1, source_target_pairs={{0,4},{1,3},{4,8},{5,1},{8,12},{9,5},{12,14},{13,9},{14,10},{15,13... | collective-permute-start | bytes 983048 | tf_op jit(solution)/shard_map/ppermute | solution.py:231
  181.6 17.7 %collective-permute-start.19 = (bf16[128,1280]{1,0:T(8,128)(2,1)S(1)}, bf16[128,1280]{1,0:T(8,128)(2,1)S(1)}, u32[]{:S(2)}, u32[]{:S(2)}) collective-permute-start(bf16[128,1280]{1,0:T(8,128)(2,1)S(1)} %get-tuple-element.57), channel_id=1, source_target_pairs={{0,16},{16,0},{1,17},{17,1},{2,18},{18,2},{3,19},{19,3},{4,20},{20... | collective-permute-start | bytes 983048 | tf_op jit(solution)/shard_map/ppermute | solution.py:236
  183.1 23.2 %collective-permute-start.30 = (bf16[128,1280]{1,0:T(8,128)(2,1)S(1)}, bf16[128,1280]{1,0:T(8,128)(2,1)S(1)}, u32[]{:S(2)}, u32[]{:S(2)}) collective-permute-start(bf16[128,1280]{1,0:T(8,128)(2,1)S(1)} %get-tuple-element.64), channel_id=1, source_target_pairs={{0,16},{16,0},{1,17},{17,1},{2,18},{18,2},{3,19},{19,3},{4,20},{20... | collective-permute-start | bytes 983048 | tf_op jit(solution)/shard_map/ppermute | solution.py:236
  184.0 24.9 %collective-permute-start.29 = (bf16[128,1280]{1,0:T(8,128)(2,1)S(1)}, bf16[128,1280]{1,0:T(8,128)(2,1)S(1)}, u32[]{:S(2)}, u32[]{:S(2)}) collective-permute-start(bf16[128,1280]{1,0:T(8,128)(2,1)S(1)} %shard_map.124), channel_id=1, source_target_pairs={{0,20},{1,19},{4,24},{5,17},{8,28},{9,21},{12,30},{13,25},{14,26},... | collective-permute-start | bytes 983048 | tf_op jit(solution)/shard_map/ppermute | solution.py:325
  187.3 25.2 %collective-permute-start.37 = (bf16[128,1280]{1,0:T(8,128)(2,1)S(1)}, bf16[128,1280]{1,0:T(8,128)(2,1)S(1)}, u32[]{:S(2)}, u32[]{:S(2)}) collective-permute-start(bf16[128,1280]{1,0:T(8,128)(2,1)S(1)} %shard_map.131), channel_id=1, source_target_pairs={{0,20},{1,19},{4,24},{5,17},{8,28},{9,21},{12,30},{13,25},{14,26},... | collective-permute-start | bytes 983048 | tf_op jit(solution)/shard_map/ppermute | solution.py:325
  (23 other events, 176.2 us)
Sparse Core Ops, SparseCore 0:
  11.9 51.1 all-gather.2

commit v2 on v1

v2 whole, which is shorter than its diff:
```python
import functools

import jax
import jax.numpy as jnp
import numpy as np
from jax import lax
from jax.experimental import pallas as pl
from jax.experimental.pallas import tpu as pltpu
from jax.sharding import PartitionSpec as P

BF = jnp.bfloat16
F32 = jnp.float32
VMEM = pl.BlockSpec(memory_space=pltpu.VMEM)
SMEM = pl.BlockSpec(memory_space=pltpu.SMEM)
MIB = 1024 * 1024


def chip_at(place, chips):
    place %= chips
    half = chips // 2
    return 2 * place if place < half else 2 * (chips - 1 - place) + 1


def call(body, outs, ins, limit=12, flops=0, moved=0):
    return pl.pallas_call(
        body,
        out_shape=outs,
        in_specs=ins,
        out_specs=jax.tree.map(lambda _: VMEM, outs),
        compiler_params=pltpu.CompilerParams(vmem_limit_bytes=limit * MIB),
        cost_estimate=pl.CostEstimate(flops=flops, transcendentals=0, bytes_accessed=moved),
    )


def dot(a, b):
    return jnp.dot(a, b, preferred_element_type=F32)


def dot_first(a, b):
    return lax.dot_general(a, b, (((0,), (0,)), ((), ())), preferred_element_type=F32)


def dot_last(a, b):
    return lax.dot_general(a, b, (((1,), (1,)), ((), ())), preferred_element_type=F32)


def slots_of(row, most):
    ids = lax.broadcasted_iota(jnp.int32, (most, row.shape[1]), 0).astype(F32)
    return jnp.where(ids == row, 1.0, 0.0)


def pack_body(routes, gates, capacity, down, out):
    top, _, rows = routes.shape
    experts = capacity.shape[1]
    expert = lax.broadcasted_iota(jnp.int32, (experts, rows), 0)
    named = jnp.zeros((experts, rows), F32)
    gate = jnp.zeros((experts, rows), F32)
    for k in range(top):
        hit = routes[k] == expert
        named = named + jnp.where(hit, 1.0, 0.0)
        gate = gate + jnp.where(hit, gates[k], 0.0)
    row = lax.broadcasted_iota(jnp.int32, (rows, rows), 0)
    col = lax.broadcasted_iota(jnp.int32, (rows, rows), 1)
    rank = dot(named.astype(BF), jnp.where(row < col, 1.0, 0.0).astype(BF))
    row = lax.broadcasted_iota(jnp.int32, (experts, experts), 0)
    col = lax.broadcasted_iota(jnp.int32, (experts, experts), 1)
    limit = jnp.sum(jnp.where(row == col, capacity[...].astype(F32), 0.0), 1, keepdims=True)
    kept = (named > 0.5) & (rank < limit)
    depth = down.shape[0]
    out[0:depth, :] = down[...]
    out[depth : depth + experts, 0:rows] = jnp.where(kept, rank, -1.0).astype(BF)
    out[depth : depth + experts, rows : 2 * rows] = jnp.where(kept, gate, 0.0).astype(BF)


def unpack_body(depth, ids, one, two, down, meta):
    chips, tall, wide = one.shape
    experts = tall - depth
    row = lax.broadcasted_iota(jnp.int32, (experts, wide), 0)
    for side, half in enumerate((one, two)):
        for k in range(chips):
            block = ids[side, k]
            down[pl.ds(pl.multiple_of(block * depth, 16), depth), :] = half[k, 0:depth, :]
            table = half[k, depth:tall, :].astype(F32)
            own = jnp.sum(jnp.where(row == ids[2, 0], table, 0.0), 0, keepdims=True)
            meta[side * chips + k : side * chips + k + 1, :] = own
            meta[pl.ds(3 * chips + block, 1), :] = own
            if side == 0:
                meta[2 * chips + k : 2 * chips + k + 1, :] = jnp.sum(
                    jnp.where(row == ids[2, 1], table, 0.0), 0, keepdims=True
                )


def arrive_body(ks, most, chips, meta, down, gain, *refs):
    count = len(ks)
    pieces, (own, other, latents) = refs[: 2 * count], refs[2 * count :]
    rows = latents.shape[1]
    half = rows // 2
    for i, k in enumerate(ks):
        x = jnp.concatenate([pieces[2 * i][...], pieces[2 * i + 1][0:half, :]], 0)
        pick = jnp.concatenate(
            [slots_of(meta[at : at + 1, 0:rows], most) for at in (k, 2 * chips + k)], 0
        ).astype(BF)
        chosen = dot(pick, x).astype(BF)
        own[i] = chosen[:most]
        other[i] = chosen[most:]
        raw = dot(x, down[...])
        scale = lax.rsqrt(jnp.mean(raw * raw, -1, keepdims=True) + 1e-06)
        latents[i] = (raw * scale * gain[...]).astype(BF)


def attend(rows, keys, masks, w_query):
    query = (dot(rows, w_query) * (rows.shape[1] ** -0.5)).astype(BF)
    scores = [dot_last(query, piece) for piece in keys]
    scores = [s if m is None else jnp.where(m, s, -1e30) for s, m in zip(scores, masks, strict=True)]
    peak = functools.reduce(jnp.maximum, [jnp.max(s, -1, keepdims=True) for s in scores])
    weights = [jnp.exp(s - peak) for s in scores]
    total = sum(jnp.sum(w, -1, keepdims=True) for w in weights)
    accum = sum(dot(w.astype(BF), piece) for w, piece in zip(weights, keys, strict=True))
    return (accum / total).astype(BF)


def reorder(attended, order):
    place = lax.broadcasted_iota(jnp.int32, (attended.shape[1], order.shape[1]), 0)
    return dot(attended, jnp.where(place == order, 1.0, 0.0).astype(BF)).astype(BF)


def expert_body(groups, most, chips, sequence, early, ids, order, meta, w_query, out_a, out_b, *refs):
    n = len(groups)
    gate_up_hbm, expert_down_hbm = refs[:2]
    own, other, lat_a, lat_b = (refs[2 + i * n : 2 + (i + 1) * n] for i in range(4))
    mine, theirs_early, theirs_late, lat, gate_up, expert_down, att, sem = refs[2 + 4 * n :]
    loads = [
        pltpu.make_async_copy(gate_up_hbm, gate_up, sem.at[0]),
        pltpu.make_async_copy(expert_down_hbm, expert_down, sem.at[1]),
    ]
    for load in loads:
        load.start()
    rows = lat_a[0].shape[1]
    hidden_width = expert_down.shape[0]
    blocks = 2 * chips
    where = {k: (g, i) for g, group in enumerate(groups) for i, k in enumerate(group)}
    for side, halves in enumerate((lat_a, lat_b)):
        for k in range(chips):
            g, i = where[k]
            lat[pl.ds(pl.multiple_of(ids[side, k] * rows, rows), rows), :] = halves[g][i]
    batch = 4
    token = lax.broadcasted_iota(jnp.int32, (most, rows), 1).astype(F32)
    for first in range(0, blocks, batch):
        latent, place = [], []
        for b in range(first, first + batch):
            pick = slots_of(meta[3 * chips + b : 3 * chips + b + 1, 0:rows], most)
            spot = jnp.sum(pick * token, -1, keepdims=True).astype(jnp.int32)
            place.append(spot + (b - first) * rows)
            latent.append(dot(pick.astype(BF), lat[b * rows : (b + 1) * rows, :]).astype(BF))
        place = jnp.concatenate(place, 0)
        key = lax.broadcasted_iota(jnp.int32, (1, batch * rows), 1)
        keys, masks = [lat[first * rows : (first + batch) * rows, :]], [key <= place]
        if first:
            keys.append(lat[0 : first * rows, :])
            masks.append(None)
        attended = attend(jnp.concatenate(latent, 0), keys, masks, w_query[...])
        attended = reorder(attended, order[...])
        for b in range(first, first + batch):
            at = pl.multiple_of(ids[3, b] * most, most)
            att[pl.ds(at, most), :] = attended[(b - first) * most : (b - first + 1) * most, :]
    for load in loads:
        load.wait()
    shard = out_a.shape[0]
    for ks in (sequence[: chips // 2], sequence[chips // 2 :]):
        chosen, attended, gate = [], [], []
        for side, xs in enumerate((own, other)):
            for k in ks:
                g, i = where[k]
                at = side * chips + k
                pick = slots_of(meta[at : at + 1, 0:rows], most)
                gate.append(jnp.sum(pick * meta[at : at + 1, rows : 2 * rows], -1, keepdims=True))
                attended.append(att[at * most : (at + 1) * most, :])
                chosen.append(xs[g][i])
        attended = jnp.concatenate(attended, 0)
        hidden = dot(attended[:, :shard], out_a[...]) + dot(attended[:, shard:], out_b[...])
        hidden = (jnp.concatenate(chosen, 0).astype(F32) + hidden).astype(BF)
        both = dot(hidden, gate_up[...])
        inner = (jax.nn.silu(both[:, :hidden_width]) * both[:, hidden_width:]).astype(BF)
        result = (dot(inner, expert_down[...]) * jnp.concatenate(gate, 0)).astype(BF)
        for i, k in enumerate(ks):
            mine[k] = result[i * most : (i + 1) * most]
            away = result[(len(ks) + i) * most : (len(ks) + i + 1) * most]
            if k in early:
                theirs_early[early.index(k)] = away
            else:
                theirs_late[[j for j in sequence if j not in early].index(k)] = away


def spread(k, most, chips, rows, meta, mine, theirs, cols):
    one = slots_of(meta[k : k + 1, 0:rows], most).astype(BF)
    two = slots_of(meta[2 * chips + k : 2 * chips + k + 1, 0:rows], most).astype(BF)
    return dot_first(one, mine[k, :, cols]) + dot_first(two, theirs[:, cols])


def combine_body(k, at, most, chips, first, size, meta, mine, theirs, *refs):
    rows = meta.shape[1] // 2
    total = spread(k, most, chips, rows, meta, mine, theirs.at[at], slice(first, first + size))
    if len(refs) > 1:
        total = total + refs[0][...].astype(F32)
    refs[-1][...] = total.astype(BF)


def own_body(at, most, chips, ids, order, meta, w_query, out_a, out_b, tokens, lat, mine, theirs, *outs):
    rows = tokens.shape[0]
    start = pl.multiple_of(ids[0, 0] * rows, rows)
    place = start + lax.broadcasted_iota(jnp.int32, (rows, 1), 0)
    key = lax.broadcasted_iota(jnp.int32, (1, lat.shape[0]), 1)
    attended = attend(lat[pl.ds(start, rows), :], [lat[...]], [key <= place], w_query[...])
    attended = reorder(attended, order[...])
    shard = out_a.shape[0]
    hidden = dot(attended[:, :shard], out_a[...]) + dot(attended[:, shard:], out_b[...])
    hidden = (tokens[...].astype(F32) + hidden).astype(BF).astype(F32)
    first = 0
    for out in outs:
        cols = slice(first, first + out.shape[1])
        total = spread(0, most, chips, rows, meta, mine, theirs.at[at], cols)
        out[...] = (hidden[:, cols] + total).astype(BF)
        first += out.shape[1]


def final_body(*refs):
    ins, out = refs[:-1], refs[-1]
    first = 0
    for one, two in zip(ins[0::2], ins[1::2], strict=True):
        size = one.shape[1]
        out[:, first : first + size] = (one[...].astype(F32) + two[...].astype(F32)).astype(BF)
        first += size


def after(x, *others):
    return lax.optimization_barrier((x, *others))[0]


def on_device(
    tokens, routes, gates, capacity, w_down_kv, kv_gain, w_query, w_out, w_gate_up, w_expert_down
):
    pipes = lax.axis_size("pipe")
    owners = lax.axis_size("expert")
    chips = owners // 2
    me = lax.axis_index("expert")
    rows, width = tokens.shape[1:]
    top = routes.shape[2]
    latent = w_query.shape[1]
    depth = w_down_kv.shape[1]
    most = max(2, 4 * rows * top // (3 * owners))
    shape = jax.ShapeDtypeStruct

    ring, blocks = [], np.zeros((owners, chips), np.int32)
    for r in range(chips):
        even, odd = 2 * chip_at(r, chips), 2 * chip_at(r, chips) + 1
        ring.append((even, 2 * chip_at(r + 1, chips)))
        ring.append((odd, 2 * chip_at(r - 1, chips) + 1))
        for k in range(chips):
            blocks[even, k] = 2 * chip_at(r - k, chips)
            blocks[odd, k] = 2 * chip_at(r + k, chips) + 1
    step = lambda x: lax.ppermute(x, "expert", ring)
    sibling = lambda x: lax.ppermute(x, "expert", [(i, i ^ 1) for i in range(owners)])
    last = [
        (p * owners + a, ((p + 1) % pipes) * owners + b) for p in range(pipes) for a, b in ring
    ]
    onward = lambda x: lax.ppermute(x, "pipe", [(p, (p + 1) % pipes) for p in range(pipes)])

    table = np.zeros((owners, 4, owners), np.int32)
    for e in range(owners):
        both = np.concatenate([blocks[e], blocks[e ^ 1]])
        table[e, 0, :chips], table[e, 1, :chips] = blocks[e], blocks[e ^ 1]
        table[e, 2, :2] = (e, e ^ 1)
        table[e, 3, both] = np.arange(owners)
    ids = lax.dynamic_index_in_dim(jnp.asarray(table), me, 0, keepdims=False)
    shard = w_out.shape[1]
    order = (ids[:2, :chips].reshape(-1)[:, None] * shard + jnp.arange(shard)[None, :]).reshape(1, -1)

    half = rows // 2
    first = [tokens[0, :half]]
    second = [jnp.concatenate([tokens[0, half:], w_out[0]], 0)]
    small = [
        call(pack_body, shape((depth + owners, latent), BF), [VMEM] * 4)(
            routes.transpose(2, 0, 1),
            gates.transpose(2, 0, 1),
            capacity,
            after(w_down_kv[0], first[0], second[0]),
        )
    ]
    arrived = []
    for _ in range(1, chips):
        for stream in (first, small, second, small):
            if len(stream) < chips:
                arrived.append(stream[-1])
                stream.append(step(after(stream[-1], *arrived[-3:-1])))
    small = jnp.stack(small)
    down, meta = call(
        functools.partial(unpack_body, depth),
        (shape((owners * depth, latent), BF), shape((5 * chips, 2 * rows), F32)),
        [SMEM, VMEM, VMEM],
    )(ids, small, sibling(small))

    groups = (tuple(range(chips - 3)), (chips - 3, chips - 2), (chips - 1,))
    own, other, lat_a, lat_b = [], [], [], []
    for group in groups:
        n = len(group)
        picked, away, lat = call(
            functools.partial(arrive_body, group, most, chips),
            (
                shape((n, most, width), BF),
                shape((n, most, width), BF),
                shape((n, rows, latent), BF),
            ),
            [VMEM] * (3 + 2 * n),
            flops=2 * n * rows * width * (latent + 2 * most),
        )(meta, down, kv_gain, *[x for k in group for x in (first[k], second[k])])
        own.append(picked)
        other.append(sibling(away))
        lat_a.append(lat)
        lat_b.append(sibling(lat))
    out_a = jnp.concatenate([x[half:] for x in second], 0)
    out_b = sibling(out_a)

    sequence = tuple(range(1, chips)) + (0,)
    early = sequence[:2]
    gate_up, expert_down = w_gate_up[0, 0], w_expert_down[0, 0]
    mine, away_early, away_late, lat = pl.pallas_call(
        functools.partial(expert_body, groups, most, chips, sequence, early),
        out_shape=(
            shape((chips, most, width), BF),
            shape((len(early), most, width), BF),
            shape((chips - len(early), most, width), BF),
            shape((owners * rows, latent), BF),
        ),
        in_specs=[SMEM] + [VMEM] * 5 + [pl.BlockSpec(memory_space=pl.ANY)] * 2 + [VMEM] * (4 * len(groups)),
        out_specs=(VMEM,) * 4,
        scratch_shapes=[
            pltpu.VMEM(gate_up.shape, BF),
            pltpu.VMEM(expert_down.shape, BF),
            pltpu.VMEM((owners * most, latent), BF),
            pltpu.SemaphoreType.DMA((2,)),
        ],
        compiler_params=pltpu.CompilerParams(vmem_limit_bytes=40 * MIB),
    )(
        ids,
        order,
        meta,
        w_query[0],
        out_a,
        out_b,
        gate_up,
        expert_down,
        *own,
        *other,
        *lat_a,
        *lat_b,
    )
    theirs_early, theirs_late = sibling(away_early), sibling(away_late)
    theirs = {}
    for i, k in enumerate(sequence):
        theirs[k] = (theirs_early, i) if i < len(early) else (theirs_late, i - len(early))

    pieces = [(0, width // 2), (width // 2, width - width // 2)]
    passing = [None] * len(pieces)
    for k in range(1, chips):
        if k == min(3, chips - 1):
            kept = call(
                functools.partial(own_body, theirs[0][1], most, chips),
                tuple(shape((rows, size), BF) for _, size in pieces),
                [SMEM] + [VMEM] * 9,
                flops=2 * rows * latent * (width + 2 * owners * rows),
            )(
                ids,
                order,
                meta,
                w_query[0],
                out_a,
                out_b,
                after(tokens[0], *passing),
                lat,
                mine,
                theirs[0][0],
            )
            passing = [after(x, *kept) for x in passing]
            kept = [onward(x) for x in kept]
        for i, (start, size) in enumerate(pieces):
            more = [] if passing[i] is None else [passing[i]]
            if k == chips - 2 and more:
                more = [after(more[0], *kept)]
            total = call(
                functools.partial(combine_body, k, theirs[k][1], most, chips, start, size),
                shape((rows, size), BF),
                [VMEM] * (3 + len(more)),
                flops=4 * rows * most * size,
            )(meta, mine, theirs[k][0], *more)
            if k < chips - 1:
                passing[i] = step(total)
            else:
                passing[i] = lax.ppermute(total, ("pipe", "expert"), last)
    output = call(final_body, shape((rows, width), BF), [VMEM] * (2 * len(pieces)))(
        *[x for pair in zip(kept, passing, strict=True) for x in pair]
    )
    return output[None]


def solution(mesh):
    return jax.shard_map(
        on_device,
        mesh=mesh,
        in_specs=(
            P("pipe", "expert", None),
            P("pipe", "expert", None),
            P("pipe", "expert", None),
            P("pipe", None),
            P("pipe", "expert", None),
            P("pipe", None),
            P("pipe", None, None),
            P("pipe", "expert", None),
            P("pipe", "expert", None, None),
            P("pipe", "expert", None, None),
        ),
        out_specs=P("pipe", "expert", None),
        check_vma=False,
    )
```

time: 221 us -> 201 us (0.910)
  Pallas kernels: 59.8 us -> 39.4 us
  waiting for transfers between devices: 78.6 us -> 92.6 us
  between operations: 13.7 us -> 0.35 us
  starting transfers between devices: 56.9 us -> 59.5 us
  local copies, waits for them, and re-layouts: 10.4 us -> 7.88 us
    pallas_call x21 -> x18, Pallas kernels: 52.7 us -> 32.5 us  [the longest x1 23.9 us: on_device(): pl.pallas_call(functools.partial(expert_body, groups, most, chips, sequen...]
    ppermute x26 -> x33, waiting for transfers between devices: 53.8 us -> 68.7 us  [on_device(): step = lambda x: lax.ppermute(x, 'expert', ring)]
    ppermute x2, waiting for transfers between devices: 18.6 us -> 5.73 us  [on_device(): lax.ppermute(x, 'pipe', [(p, (p + 1) % pipes) for p in range(pipes)])]
    ppermute x2, waiting for transfers between devices: 6.14 us -> 12.5 us  [on_device(): passing[i] = lax.ppermute(total, ('pipe', 'expert'), last)]
    ppermute x8 -> x10, waiting for transfers between devices: 0.11 us -> 5.64 us  [on_device(): lax.ppermute(x, 'expert', [(i, i ^ 1) for i in range(owners)])]
    unnamed x18 -> x50, local copies, waits for them, and re-layouts: 7.11 us -> 5.85 us
    pallas_call x2 -> x3, Pallas kernels: 6.11 us -> 5.97 us  [on_device(): call(functools.partial(arrive_body, group, most, chips), (shape((n, most,...]
    ppermute x26 -> x33, starting transfers between devices: 50.3 us -> 50.2 us  [on_device(): step = lambda x: lax.ppermute(x, 'expert', ring)]
  transfers between devices with their start and end apart: 39 -> 47, of which waited for: 24 -> 27; matrix products, arithmetic and copies ran while one was open for 2% -> 1% of each run, Pallas kernels for 19% -> 5%
where the time goes in v2:
time: 201 us
  waiting for transfers between devices  92.6 us (46%)
  starting transfers between devices  59.5 us (30%)
  Pallas kernels  39.4 us (20%)
  local copies, waits for them, and re-layouts  7.88 us (4%)
    ppermute x33, waiting for transfers between devices, on_device(): step = lambda x: lax.ppermute(x, 'expert', ring)  68.7 us
    ppermute x33, starting transfers between devices, on_device(): step = lambda x: lax.ppermute(x, 'expert', ring)  50.2 us
    pallas_call x1, Pallas kernels, on_device(): pl.pallas_call(functools.partial(expert_body, groups, most, chips, sequen...  23.9 us
    ppermute x2, waiting for transfers between devices, on_device(): passing[i] = lax.ppermute(total, ('pipe', 'expert'), last)  12.5 us
    pallas_call x3, Pallas kernels, on_device(): call(functools.partial(arrive_body, group, most, chips), (shape((n, most,...  5.97 us
    unnamed x50, local copies, waits for them, and re-layouts  5.85 us
    ppermute x2, waiting for transfers between devices, on_device(): lax.ppermute(x, 'pipe', [(p, (p + 1) % pipes) for p in range(pipes)])  5.73 us
    ppermute x10, waiting for transfers between devices, on_device(): lax.ppermute(x, 'expert', [(i, i ^ 1) for i in range(owners)])  5.64 us
  transfers between devices with their start and end apart: 47, of which 27 were waited for; matrix products, arithmetic and copies ran while one was open for 1% of the time, Pallas kernels for 5%

profile of v2, /device:TPU:0, one launch (start us, length us, event | category | flops | bytes accessed | tf_op | source)
XLA Modules:
  0.0 200.7 jit_solution(2301633023462239842)
XLA Ops:
  2.2 3.1 %collective-permute-start = (bf16[176,256]{1,0:T(8,128)(2,1)S(1)}, bf16[176,256]{1,0:T(8,128)(2,1)S(1)}, u32[]{:S(2)}, u32[]{:S(2)}) collective-permute-start(bf16[176,256]{1,0:T(8,128)(2,1)S(1)} %shard_map.109), channel_id=1, source_target_pairs={{0,4},{1,3},{4,8},{5,1},{8,12},{9,5},{12,14},{13,9},{14,10},{15,13... | collective-permute-start | bytes 270344 | tf_op jit(solution)/shard_map/ppermute | solution.py:261
  10.8 7.0 %collective-permute-done.1 = bf16[176,256]{1,0:T(8,128)(2,1)S(1)} collective-permute-done((bf16[176,256]{1,0:T(8,128)(2,1)S(1)}, bf16[176,256]{1,0:T(8,128)(2,1)S(1)}, u32[]{:S(2)}, u32[]{:S(2)}) %collective-permute-start.1) | collective-permute-done | bytes 90144 | tf_op jit(solution)/shard_map/ppermute | solution.py:261
  24.0 7.9 %collective-permute-done.5 = bf16[176,256]{1,0:T(8,128)(2,1)S(1)} collective-permute-done((bf16[176,256]{1,0:T(8,128)(2,1)S(1)}, bf16[176,256]{1,0:T(8,128)(2,1)S(1)}, u32[]{:S(2)}, u32[]{:S(2)}) %collective-permute-start.5) | collective-permute-done | bytes 90144 | tf_op jit(solution)/shard_map/ppermute | solution.py:261
  44.1 2.9 %collective-permute-done.11 = bf16[176,256]{1,0:T(8,128)(2,1)S(1)} collective-permute-done((bf16[176,256]{1,0:T(8,128)(2,1)S(1)}, bf16[176,256]{1,0:T(8,128)(2,1)S(1)}, u32[]{:S(2)}, u32[]{:S(2)}) %collective-permute-start.11) | collective-permute-done | bytes 90144 | tf_op jit(solution)/shard_map/ppermute | solution.py:261
  48.6 1.8 collective-permute-done.15.refs_8_
  52.0 6.6 %collective-permute-done.17.refs_0_ = bf16[64,2560]{1,0:T(8,128)(2,1)S(1)} collective-permute-done((bf16[64,2560]{1,0:T(8,128)(2,1)S(1)}, bf16[64,2560]{1,0:T(8,128)(2,1)S(1)}, u32[]{:S(2)}, u32[]{:S(2)}) %collective-permute-start.17) | collective-permute-done | bytes 327712 | tf_op jit(solution)/shard_map/ppermute | solution.py:261
  63.8 3.1 %shard_map.111 = (bf16[5,64,2560]{2,1,0:T(8,128)(2,1)S(1)}, bf16[5,64,2560]{2,1,0:T(8,128)(2,1)}, bf16[5,128,256]{2,1,0:T(8,128)(2,1)S(1)}) custom-call(f32[40,256]{1,0:T(8,128)S(1)} %get-tuple-element.60.meta, bf16[2560,256]{1,0:T(8,128)(2,1)S(1)} %get-tuple-element.69.down, f32[1,256]{1,0:T(1,128)S(1)} %copy-done.13, ...), custom_call_target="tpu_custom_call" | custom-call | flops 1258291200 | tf_op jit(solution)/shard_map/pallas_call | solution.py:306
  67.4 2.7 %collective-permute-done.16.refs_1_ = bf16[80,2560]{1,0:T(8,128)(2,1)S(1)} collective-permute-done((bf16[80,2560]{1,0:T(8,128)(2,1)S(1)}, bf16[80,2560]{1,0:T(8,128)(2,1)S(1)}, u32[]{:S(2)}, u32[]{:S(2)}) %collective-permute-start.16) | collective-permute-done | bytes 409632 | tf_op jit(solution)/shard_map/ppermute | solution.py:261
  72.6 9.0 %collective-permute-done.18.refs_3_ = bf16[80,2560]{1,0:T(8,128)(2,1)S(1)} collective-permute-done((bf16[80,2560]{1,0:T(8,128)(2,1)S(1)}, bf16[80,2560]{1,0:T(8,128)(2,1)S(1)}, u32[]{:S(2)}, u32[]{:S(2)}) %collective-permute-start.18) | collective-permute-done | bytes 409632 | tf_op jit(solution)/shard_map/ppermute | solution.py:261
  84.8 4.7 %collective-permute-done.20.refs_1_ = bf16[80,2560]{1,0:T(8,128)(2,1)S(1)} collective-permute-done((bf16[80,2560]{1,0:T(8,128)(2,1)S(1)}, bf16[80,2560]{1,0:T(8,128)(2,1)S(1)}, u32[]{:S(2)}, u32[]{:S(2)}) %collective-permute-start.20) | collective-permute-done | bytes 409632 | tf_op jit(solution)/shard_map/ppermute | solution.py:261
  96.9 23.9 %shard_map.114 = (bf16[8,64,2560]{2,1,0:T(8,128)(2,1)S(1)}, bf16[2,64,2560]{2,1,0:T(8,128)(2,1)S(1)}, bf16[6,64,2560]{2,1,0:T(8,128)(2,1)S(1)}, bf16[2048,256]{1,0:T(8,128)(2,1)S(1)}) custom-call(s32[4,16]{1,0:T(4,128)S(1)} %dynamic-slice_bitcast_fusion.ids, s32[1,256]{1,0:T(1,128)S(1)} %add.31.order, f32[40,256]{1,0:T(8,128)S(1)} %get-tuple-element.60.meta, ...), custom_call_target="tpu_custom_call" | custom-call | tf_op jit(solution)/shard_map/pallas_call | solution.py:326
  121.4 4.4 %collective-permute-done.29.theirs = bf16[2,64,2560]{2,1,0:T(8,128)(2,1)S(1)} collective-permute-done((bf16[2,64,2560]{2,1,0:T(8,128)(2,1)S(1)}, bf16[2,64,2560]{2,1,0:T(8,128)(2,1)S(1)}, u32[]{:S(2)}, u32[]{:S(2)}) %collective-permute-start.29) | collective-permute-done | bytes 655392 | tf_op jit(solution)/shard_map/ppermute | solution.py:262
  129.2 4.2 %collective-permute-done.30.refs_0_ = bf16[128,1280]{1,0:T(8,128)(2,1)S(1)} collective-permute-done((bf16[128,1280]{1,0:T(8,128)(2,1)S(1)}, bf16[128,1280]{1,0:T(8,128)(2,1)S(1)}, u32[]{:S(2)}, u32[]{:S(2)}) %collective-permute-start.30) | collective-permute-done | bytes 327712 | tf_op jit(solution)/shard_map/ppermute | solution.py:261
  138.8 2.1 %collective-permute-done.31.refs_0_ = bf16[128,1280]{1,0:T(8,128)(2,1)S(1)} collective-permute-done((bf16[128,1280]{1,0:T(8,128)(2,1)S(1)}, bf16[128,1280]{1,0:T(8,128)(2,1)S(1)}, u32[]{:S(2)}, u32[]{:S(2)}) %collective-permute-start.31) | collective-permute-done | bytes 327712 | tf_op jit(solution)/shard_map/ppermute | solution.py:261
  140.8 3.5 %collective-permute-done.33.refs_0_ = bf16[128,1280]{1,0:T(8,128)(2,1)S(1)} collective-permute-done((bf16[128,1280]{1,0:T(8,128)(2,1)S(1)}, bf16[128,1280]{1,0:T(8,128)(2,1)S(1)}, u32[]{:S(2)}, u32[]{:S(2)}) %collective-permute-start.33) | collective-permute-done | bytes 327712 | tf_op jit(solution)/shard_map/ppermute | solution.py:261
  144.4 2.8 %shard_map.119 = (bf16[128,1280]{1,0:T(8,128)(2,1)S(1)}, bf16[128,1280]{1,0:T(8,128)(2,1)S(1)}) custom-call(s32[4,16]{1,0:T(4,128)S(1)} %dynamic-slice_bitcast_fusion.ids, s32[1,256]{1,0:T(1,128)S(1)} %add.31.order, f32[40,256]{1,0:T(8,128)S(1)} %get-tuple-element.60.meta, bf16[256,256]{1,0:T(8,128)(2,1)S(1)} %bitcast.34, ...), custom_call_target="tpu_custom_call" | custom-call | flops 436207616 | tf_op jit(solution)/shard_map/pallas_call | solution.py:366
  150.5 4.2 %collective-permute-done.42.refs_0_ = bf16[128,1280]{1,0:T(8,128)(2,1)S(1)} collective-permute-done((bf16[128,1280]{1,0:T(8,128)(2,1)S(1)}, bf16[128,1280]{1,0:T(8,128)(2,1)S(1)}, u32[]{:S(2)}, u32[]{:S(2)}) %collective-permute-start.42) | collective-permute-done | bytes 327712 | tf_op jit(solution)/shard_map/ppermute | solution.py:261
  167.6 2.2 %collective-permute-done.35.refs_0_ = bf16[128,1280]{1,0:T(8,128)(2,1)S(1)} collective-permute-done((bf16[128,1280]{1,0:T(8,128)(2,1)S(1)}, bf16[128,1280]{1,0:T(8,128)(2,1)S(1)}, u32[]{:S(2)}, u32[]{:S(2)}) %collective-permute-start.35) | collective-permute-done | bytes 327712 | tf_op jit(solution)/shard_map/ppermute | solution.py:266
  169.8 3.5 %collective-permute-done.39.refs_2_ = bf16[128,1280]{1,0:T(8,128)(2,1)S(1)} collective-permute-done((bf16[128,1280]{1,0:T(8,128)(2,1)S(1)}, bf16[128,1280]{1,0:T(8,128)(2,1)S(1)}, u32[]{:S(2)}, u32[]{:S(2)}) %collective-permute-start.39) | collective-permute-done | bytes 327712 | tf_op jit(solution)/shard_map/ppermute | solution.py:266
  177.3 3.6 %collective-permute-done.40.refs_0_ = bf16[128,1280]{1,0:T(8,128)(2,1)S(1)} collective-permute-done((bf16[128,1280]{1,0:T(8,128)(2,1)S(1)}, bf16[128,1280]{1,0:T(8,128)(2,1)S(1)}, u32[]{:S(2)}, u32[]{:S(2)}) %collective-permute-start.40) | collective-permute-done | bytes 327712 | tf_op jit(solution)/shard_map/ppermute | solution.py:261
  181.2 2.6 %collective-permute-start.41 = (bf16[128,1280]{1,0:T(8,128)(2,1)S(1)}, bf16[128,1280]{1,0:T(8,128)(2,1)S(1)}, u32[]{:S(2)}, u32[]{:S(2)}) collective-permute-start(bf16[128,1280]{1,0:T(8,128)(2,1)S(1)} %shard_map.124), channel_id=1, source_target_pairs={{0,20},{1,19},{4,24},{5,17},{8,28},{9,21},{12,30},{13,25},{14,26},... | collective-permute-start | bytes 983048 | tf_op jit(solution)/shard_map/ppermute | solution.py:398
  184.7 2.6 %collective-permute-start.46 = (bf16[128,1280]{1,0:T(8,128)(2,1)S(1)}, bf16[128,1280]{1,0:T(8,128)(2,1)S(1)}, u32[]{:S(2)}, u32[]{:S(2)}) collective-permute-start(bf16[128,1280]{1,0:T(8,128)(2,1)S(1)} %shard_map.129), channel_id=1, source_target_pairs={{0,20},{1,19},{4,24},{5,17},{8,28},{9,21},{12,30},{13,25},{14,26},... | collective-permute-start | bytes 983048 | tf_op jit(solution)/shard_map/ppermute | solution.py:398
  187.3 9.0 %collective-permute-done.41.refs_1_ = bf16[128,1280]{1,0:T(8,128)(2,1)S(1)} collective-permute-done((bf16[128,1280]{1,0:T(8,128)(2,1)S(1)}, bf16[128,1280]{1,0:T(8,128)(2,1)S(1)}, u32[]{:S(2)}, u32[]{:S(2)}) %collective-permute-start.41) | collective-permute-done | bytes 327712 | tf_op jit(solution)/shard_map/ppermute | solution.py:398
  196.2 3.5 %collective-permute-done.46.refs_3_ = bf16[128,1280]{1,0:T(8,128)(2,1)S(1)} collective-permute-done((bf16[128,1280]{1,0:T(8,128)(2,1)S(1)}, bf16[128,1280]{1,0:T(8,128)(2,1)S(1)}, u32[]{:S(2)}, u32[]{:S(2)}) %collective-permute-start.46) | collective-permute-done | bytes 327712 | tf_op jit(solution)/shard_map/ppermute | solution.py:398
  (151 shorter events, 79.7 us)
Async XLA Ops:
  5.4 12.4 %collective-permute-start.2 = (bf16[64,2560]{1,0:T(8,128)(2,1)S(1)}, bf16[64,2560]{1,0:T(8,128)(2,1)S(1)}, u32[]{:S(2)}, u32[]{:S(2)}) collective-permute-start(bf16[64,2560]{1,0:T(8,128)(2,1)S(1)} %get-tuple-element.92.refs_0_), channel_id=1, source_target_pairs={{0,4},{1,3},{4,8},{5,1},{8,12},{9,5},{12,14},{13,9},{14,10},{15,13... | collective-permute-start | bytes 983048 | tf_op jit(solution)/shard_map/ppermute | solution.py:261
  7.0 14.1 %collective-permute-start.4 = (bf16[80,2560]{1,0:T(8,128)(2,1)S(1)}, bf16[80,2560]{1,0:T(8,128)(2,1)S(1)}, u32[]{:S(2)}, u32[]{:S(2)}) collective-permute-start(bf16[80,2560]{1,0:T(8,128)(2,1)S(1)} %pad_maximum_fusion.refs_1_), channel_id=1, source_target_pairs={{0,4},{1,3},{4,8},{5,1},{8,12},{9,5},{12,14},{13,9},{14,10},{15,13... | collective-permute-start | bytes 1228808 | tf_op jit(solution)/shard_map/ppermute | solution.py:261
  19.5 12.4 %collective-permute-start.6 = (bf16[64,2560]{1,0:T(8,128)(2,1)S(1)}, bf16[64,2560]{1,0:T(8,128)(2,1)S(1)}, u32[]{:S(2)}, u32[]{:S(2)}) collective-permute-start(bf16[64,2560]{1,0:T(8,128)(2,1)S(1)} %collective-permute-done.2.refs_2_), channel_id=1, source_target_pairs={{0,4},{1,3},{4,8},{5,1},{8,12},{9,5},{12,14},{13,9},{14,10},{15,13... | collective-permute-start | bytes 983048 | tf_op jit(solution)/shard_map/ppermute | solution.py:261
  21.0 15.4 %collective-permute-start.8 = (bf16[80,2560]{1,0:T(8,128)(2,1)S(1)}, bf16[80,2560]{1,0:T(8,128)(2,1)S(1)}, u32[]{:S(2)}, u32[]{:S(2)}) collective-permute-start(bf16[80,2560]{1,0:T(8,128)(2,1)S(1)} %collective-permute-done.4.refs_3_), channel_id=1, source_target_pairs={{0,4},{1,3},{4,8},{5,1},{8,12},{9,5},{12,14},{13,9},{14,10},{15,13... | collective-permute-start | bytes 1228808 | tf_op jit(solution)/shard_map/ppermute | solution.py:261
  22.6 9.3 %collective-permute-start.5 = (bf16[176,256]{1,0:T(8,128)(2,1)S(1)}, bf16[176,256]{1,0:T(8,128)(2,1)S(1)}, u32[]{:S(2)}, u32[]{:S(2)}) collective-permute-start(bf16[176,256]{1,0:T(8,128)(2,1)S(1)} %collective-permute-done.3), channel_id=1, source_target_pairs={{0,4},{1,3},{4,8},{5,1},{8,12},{9,5},{12,14},{13,9},{14,10},{15,13... | collective-permute-start | bytes 270344 | tf_op jit(solution)/shard_map/ppermute | solution.py:261
  38.1 9.0 %collective-permute-start.13 = (bf16[80,2560]{1,0:T(8,128)(2,1)S(1)}, bf16[80,2560]{1,0:T(8,128)(2,1)S(1)}, u32[]{:S(2)}, u32[]{:S(2)}) collective-permute-start(bf16[80,2560]{1,0:T(8,128)(2,1)S(1)} %collective-permute-done.8.refs_5_), channel_id=1, source_target_pairs={{0,4},{1,3},{4,8},{5,1},{8,12},{9,5},{12,14},{13,9},{14,10},{15,13... | collective-permute-start | bytes 1228808 | tf_op jit(solution)/shard_map/ppermute | solution.py:261
  47.0 14.1 %collective-permute-start.12 = (bf16[8,176,256]{2,1,0:T(8,128)(2,1)S(1)}, bf16[8,176,256]{2,1,0:T(8,128)(2,1)S(1)}, u32[]{:S(2)}, u32[]{:S(2)}) collective-permute-start(bf16[8,176,256]{2,1,0:T(8,128)(2,1)S(1)} %bitcast_dynamic-update-slice_fusion.one), channel_id=1, source_target_pairs={{0,1},{1,0},{2,3},{3,2},{4,5},{5,4},{6,7},{7,6},{8,9},{9,8},{10,11... | collective-permute-start | bytes 2162696 | tf_op jit(solution)/shard_map/ppermute | solution.py:262
  47.1 11.5 %collective-permute-start.14 = (bf16[80,2560]{1,0:T(8,128)(2,1)S(1)}, bf16[80,2560]{1,0:T(8,128)(2,1)S(1)}, u32[]{:S(2)}, u32[]{:S(2)}) collective-permute-start(bf16[80,2560]{1,0:T(8,128)(2,1)S(1)} %collective-permute-done.13.refs_7_), channel_id=1, source_target_pairs={{0,4},{1,3},{4,8},{5,1},{8,12},{9,5},{12,14},{13,9},{14,10},{15,13... | collective-permute-start | bytes 1228808 | tf_op jit(solution)/shard_map/ppermute | solution.py:261
  58.6 8.8 %collective-permute-start.19 = (bf16[64,2560]{1,0:T(8,128)(2,1)S(1)}, bf16[64,2560]{1,0:T(8,128)(2,1)S(1)}, u32[]{:S(2)}, u32[]{:S(2)}) collective-permute-start(bf16[64,2560]{1,0:T(8,128)(2,1)S(1)} %collective-permute-done.17.refs_0_), channel_id=1, source_target_pairs={{0,4},{1,3},{4,8},{5,1},{8,12},{9,5},{12,14},{13,9},{14,10},{15,13... | collective-permute-start | bytes 983048 | tf_op jit(solution)/shard_map/ppermute | solution.py:261
  60.1 9.9 %collective-permute-start.16 = (bf16[80,2560]{1,0:T(8,128)(2,1)S(1)}, bf16[80,2560]{1,0:T(8,128)(2,1)S(1)}, u32[]{:S(2)}, u32[]{:S(2)}) collective-permute-start(bf16[80,2560]{1,0:T(8,128)(2,1)S(1)} %collective-permute-done.14.refs_9_), channel_id=1, source_target_pairs={{0,4},{1,3},{4,8},{5,1},{8,12},{9,5},{12,14},{13,9},{14,10},{15,13... | collective-permute-start | bytes 1228808 | tf_op jit(solution)/shard_map/ppermute | solution.py:261
  66.8 25.1 %collective-permute-start.26 = (bf16[5,128,256]{2,1,0:T(8,128)(2,1)S(1)}, bf16[5,128,256]{2,1,0:T(8,128)(2,1)S(1)}, u32[]{:S(2)}, u32[]{:S(2)}) collective-permute-start(bf16[5,128,256]{2,1,0:T(8,128)(2,1)S(1)} %get-tuple-element.77.refs_8_), channel_id=1, source_target_pairs={{0,1},{1,0},{2,3},{3,2},{4,5},{5,4},{6,7},{7,6},{8,9},{9,8},{10,11... | collective-permute-start | bytes 983048 | tf_op jit(solution)/shard_map/ppermute | solution.py:262
  66.9 27.0 %collective-permute-start.23 = (bf16[5,64,2560]{2,1,0:T(8,128)(2,1)}, bf16[5,64,2560]{2,1,0:T(8,128)(2,1)}, u32[]{:S(2)}, u32[]{:S(2)}) collective-permute-start(bf16[5,64,2560]{2,1,0:T(8,128)(2,1)} %get-tuple-element.74), channel_id=1, source_target_pairs={{0,1},{1,0},{2,3},{3,2},{4,5},{5,4},{6,7},{7,6},{8,9},{9,8},{10,11... | collective-permute-start | bytes 4915208 | tf_op jit(solution)/shard_map/ppermute | solution.py:262
  70.1 19.4 %collective-permute-start.22 = (bf16[64,2560]{1,0:T(8,128)(2,1)S(1)}, bf16[64,2560]{1,0:T(8,128)(2,1)S(1)}, u32[]{:S(2)}, u32[]{:S(2)}) collective-permute-start(bf16[64,2560]{1,0:T(8,128)(2,1)S(1)} %collective-permute-done.19.refs_2_), channel_id=1, source_target_pairs={{0,4},{1,3},{4,8},{5,1},{8,12},{9,5},{12,14},{13,9},{14,10},{15,13... | collective-permute-start | bytes 983048 | tf_op jit(solution)/shard_map/ppermute | solution.py:261
  71.6 9.9 %collective-permute-start.18 = (bf16[80,2560]{1,0:T(8,128)(2,1)S(1)}, bf16[80,2560]{1,0:T(8,128)(2,1)S(1)}, u32[]{:S(2)}, u32[]{:S(2)}) collective-permute-start(bf16[80,2560]{1,0:T(8,128)(2,1)S(1)} %collective-permute-done.16.refs_1_), channel_id=1, source_target_pairs={{0,4},{1,3},{4,8},{5,1},{8,12},{9,5},{12,14},{13,9},{14,10},{15,13... | collective-permute-start | bytes 1228808 | tf_op jit(solution)/shard_map/ppermute | solution.py:261
  84.8 9.0 %collective-permute-start.24 = (bf16[2,64,2560]{2,1,0:T(8,128)(2,1)}, bf16[2,64,2560]{2,1,0:T(8,128)(2,1)}, u32[]{:S(2)}, u32[]{:S(2)}) collective-permute-start(bf16[2,64,2560]{2,1,0:T(8,128)(2,1)} %get-tuple-element.75), channel_id=1, source_target_pairs={{0,1},{1,0},{2,3},{3,2},{4,5},{5,4},{6,7},{7,6},{8,9},{9,8},{10,11... | collective-permute-start | bytes 1966088 | tf_op jit(solution)/shard_map/ppermute | solution.py:262
  120.9 23.5 %collective-permute-start.34 = (bf16[6,64,2560]{2,1,0:T(8,128)(2,1)S(1)}, bf16[6,64,2560]{2,1,0:T(8,128)(2,1)S(1)}, u32[]{:S(2)}, u32[]{:S(2)}) collective-permute-start(bf16[6,64,2560]{2,1,0:T(8,128)(2,1)S(1)} %get-tuple-element.84), channel_id=1, source_target_pairs={{0,1},{1,0},{2,3},{3,2},{4,5},{5,4},{6,7},{7,6},{8,9},{9,8},{10,11... | collective-permute-start | bytes 5898248 | tf_op jit(solution)/shard_map/ppermute | solution.py:262
  128.1 8.7 %collective-permute-start.32 = (bf16[128,1280]{1,0:T(8,128)(2,1)S(1)}, bf16[128,1280]{1,0:T(8,128)(2,1)S(1)}, u32[]{:S(2)}, u32[]{:S(2)}) collective-permute-start(bf16[128,1280]{1,0:T(8,128)(2,1)S(1)} %shard_map.117), channel_id=1, source_target_pairs={{0,4},{1,3},{4,8},{5,1},{8,12},{9,5},{12,14},{13,9},{14,10},{15,13... | collective-permute-start | bytes 983048 | tf_op jit(solution)/shard_map/ppermute | solution.py:261
  149.5 8.7 %collective-permute-start.36 = (bf16[128,1280]{1,0:T(8,128)(2,1)S(1)}, bf16[128,1280]{1,0:T(8,128)(2,1)S(1)}, u32[]{:S(2)}, u32[]{:S(2)}) collective-permute-start(bf16[128,1280]{1,0:T(8,128)(2,1)S(1)} %shard_map.120), channel_id=1, source_target_pairs={{0,4},{1,3},{4,8},{5,1},{8,12},{9,5},{12,14},{13,9},{14,10},{15,13... | collective-permute-start | bytes 983048 | tf_op jit(solution)/shard_map/ppermute | solution.py:261
  160.1 9.7 %collective-permute-start.35 = (bf16[128,1280]{1,0:T(8,128)(2,1)S(1)}, bf16[128,1280]{1,0:T(8,128)(2,1)S(1)}, u32[]{:S(2)}, u32[]{:S(2)}) collective-permute-start(bf16[128,1280]{1,0:T(8,128)(2,1)S(1)} %get-tuple-element.85), channel_id=1, source_target_pairs={{0,16},{16,0},{1,17},{17,1},{2,18},{18,2},{3,19},{19,3},{4,20},{20... | collective-permute-start | bytes 983048 | tf_op jit(solution)/shard_map/ppermute | solution.py:266
  161.6 11.7 %collective-permute-start.39 = (bf16[128,1280]{1,0:T(8,128)(2,1)S(1)}, bf16[128,1280]{1,0:T(8,128)(2,1)S(1)}, u32[]{:S(2)}, u32[]{:S(2)}) collective-permute-start(bf16[128,1280]{1,0:T(8,128)(2,1)S(1)} %get-tuple-element.86), channel_id=1, source_target_pairs={{0,16},{16,0},{1,17},{17,1},{2,18},{18,2},{3,19},{19,3},{4,20},{20... | collective-permute-start | bytes 983048 | tf_op jit(solution)/shard_map/ppermute | solution.py:266
  162.5 10.8 %collective-permute-start.44 = (bf16[128,1280]{1,0:T(8,128)(2,1)S(1)}, bf16[128,1280]{1,0:T(8,128)(2,1)S(1)}, u32[]{:S(2)}, u32[]{:S(2)}) collective-permute-start(bf16[128,1280]{1,0:T(8,128)(2,1)S(1)} %shard_map.127), channel_id=1, source_target_pairs={{0,4},{1,3},{4,8},{5,1},{8,12},{9,5},{12,14},{13,9},{14,10},{15,13... | collective-permute-start | bytes 983048 | tf_op jit(solution)/shard_map/ppermute | solution.py:261
  175.7 8.6 %collective-permute-start.45 = (bf16[128,1280]{1,0:T(8,128)(2,1)S(1)}, bf16[128,1280]{1,0:T(8,128)(2,1)S(1)}, u32[]{:S(2)}, u32[]{:S(2)}) collective-permute-start(bf16[128,1280]{1,0:T(8,128)(2,1)S(1)} %shard_map.128), channel_id=1, source_target_pairs={{0,4},{1,3},{4,8},{5,1},{8,12},{9,5},{12,14},{13,9},{14,10},{15,13... | collective-permute-start | bytes 983048 | tf_op jit(solution)/shard_map/ppermute | solution.py:261
  181.2 15.0 %collective-permute-start.41 = (bf16[128,1280]{1,0:T(8,128)(2,1)S(1)}, bf16[128,1280]{1,0:T(8,128)(2,1)S(1)}, u32[]{:S(2)}, u32[]{:S(2)}) collective-permute-start(bf16[128,1280]{1,0:T(8,128)(2,1)S(1)} %shard_map.124), channel_id=1, source_target_pairs={{0,20},{1,19},{4,24},{5,17},{8,28},{9,21},{12,30},{13,25},{14,26},... | collective-permute-start | bytes 983048 | tf_op jit(solution)/shard_map/ppermute | solution.py:398
  184.7 15.0 %collective-permute-start.46 = (bf16[128,1280]{1,0:T(8,128)(2,1)S(1)}, bf16[128,1280]{1,0:T(8,128)(2,1)S(1)}, u32[]{:S(2)}, u32[]{:S(2)}) collective-permute-start(bf16[128,1280]{1,0:T(8,128)(2,1)S(1)} %shard_map.129), channel_id=1, source_target_pairs={{0,20},{1,19},{4,24},{5,17},{8,28},{9,21},{12,30},{13,25},{14,26},... | collective-permute-start | bytes 983048 | tf_op jit(solution)/shard_map/ppermute | solution.py:398
  (41 other events, 368.6 us)

commit v3 on v2

v3 whole, which is shorter than its diff:
```python
import functools

import jax
import jax.numpy as jnp
import numpy as np
from jax import lax
from jax.experimental import pallas as pl
from jax.experimental.pallas import tpu as pltpu
from jax.sharding import PartitionSpec as P

BF = jnp.bfloat16
F32 = jnp.float32
VMEM = pl.BlockSpec(memory_space=pltpu.VMEM)
SMEM = pl.BlockSpec(memory_space=pltpu.SMEM)
MIB = 1024 * 1024
LONG = 10**11


def chip_at(place, chips):
    place %= chips
    half = chips // 2
    return 2 * place if place < half else 2 * (chips - 1 - place) + 1


def call(body, outs, ins, limit=12, flops=0):
    return pl.pallas_call(
        body,
        out_shape=outs,
        in_specs=ins,
        out_specs=jax.tree.map(lambda _: VMEM, outs),
        compiler_params=pltpu.CompilerParams(vmem_limit_bytes=limit * MIB),
        cost_estimate=pl.CostEstimate(flops=flops, transcendentals=0, bytes_accessed=flops // 100),
    )


def dot(a, b):
    return jnp.dot(a, b, preferred_element_type=F32)


def dot_first(a, b):
    return lax.dot_general(a, b, (((0,), (0,)), ((), ())), preferred_element_type=F32)


def dot_last(a, b):
    return lax.dot_general(a, b, (((1,), (1,)), ((), ())), preferred_element_type=F32)


def slots_of(row, most):
    ids = lax.broadcasted_iota(jnp.int32, (most, row.shape[1]), 0).astype(F32)
    return jnp.where(ids == row, 1.0, 0.0)


def pack_body(routes, gates, capacity, down, out):
    top, _, rows = routes.shape
    experts = capacity.shape[1]
    expert = lax.broadcasted_iota(jnp.int32, (experts, rows), 0)
    named = jnp.zeros((experts, rows), F32)
    gate = jnp.zeros((experts, rows), F32)
    for k in range(top):
        hit = routes[k] == expert
        named = named + jnp.where(hit, 1.0, 0.0)
        gate = gate + jnp.where(hit, gates[k], 0.0)
    row = lax.broadcasted_iota(jnp.int32, (rows, rows), 0)
    col = lax.broadcasted_iota(jnp.int32, (rows, rows), 1)
    rank = dot(named.astype(BF), jnp.where(row < col, 1.0, 0.0).astype(BF))
    row = lax.broadcasted_iota(jnp.int32, (experts, experts), 0)
    col = lax.broadcasted_iota(jnp.int32, (experts, experts), 1)
    limit = jnp.sum(jnp.where(row == col, capacity[...].astype(F32), 0.0), 1, keepdims=True)
    kept = (named > 0.5) & (rank < limit)
    depth = down.shape[0]
    out[0:depth, :] = down[...]
    out[depth : depth + experts, 0:rows] = jnp.where(kept, rank, -1.0).astype(BF)
    out[depth : depth + experts, rows : 2 * rows] = jnp.where(kept, gate, 0.0).astype(BF)


def unpack_body(depth, ids, *refs):
    halves, (down, meta) = refs[:-2], refs[-2:]
    chips = len(halves) // 2
    tall, wide = halves[0].shape
    experts = tall - depth
    row = lax.broadcasted_iota(jnp.int32, (experts, wide), 0)
    for i, half in enumerate(halves):
        side, k = divmod(i, chips)
        block = ids[side, k]
        down[pl.ds(pl.multiple_of(block * depth, 16), depth), :] = half[0:depth, :]
        table = half[depth:tall, :].astype(F32)
        own = jnp.sum(jnp.where(row == ids[2, 0], table, 0.0), 0, keepdims=True)
        meta[i : i + 1, :] = own
        meta[pl.ds(3 * chips + block, 1), :] = own
        if side == 0:
            meta[2 * chips + k : 2 * chips + k + 1, :] = jnp.sum(
                jnp.where(row == ids[2, 1], table, 0.0), 0, keepdims=True
            )


def arrive_body(packs, most, chips, meta, down, gain, *refs):
    count = sum(len(ks) for ks in packs)
    pieces, outs = refs[: 2 * count], refs[2 * count :]
    latents = outs[-1]
    rows = latents.shape[1]
    half = rows // 2
    at = 0
    for g, ks in enumerate(packs):
        for i, k in enumerate(ks):
            x = jnp.concatenate([pieces[2 * at][...], pieces[2 * at + 1][0:half, :]], 0)
            pick = jnp.concatenate(
                [slots_of(meta[j : j + 1, 0:rows], most) for j in (k, 2 * chips + k)], 0
            ).astype(BF)
            chosen = dot(pick, x).astype(BF)
            outs[2 * g][i] = chosen[:most]
            outs[2 * g + 1][i] = chosen[most:]
            raw = dot(x, down[...])
            scale = lax.rsqrt(jnp.mean(raw * raw, -1, keepdims=True) + 1e-06)
            latents[at] = (raw * scale * gain[...]).astype(BF)
            at += 1


def attend(rows, keys, masks, w_query):
    query = (dot(rows, w_query) * (rows.shape[1] ** -0.5)).astype(BF)
    scores = [dot_last(query, piece) for piece in keys]
    scores = [s if m is None else jnp.where(m, s, -1e30) for s, m in zip(scores, masks, strict=True)]
    peak = functools.reduce(jnp.maximum, [jnp.max(s, -1, keepdims=True) for s in scores])
    weights = [jnp.exp(s - peak) for s in scores]
    total = sum(jnp.sum(w, -1, keepdims=True) for w in weights)
    accum = sum(dot(w.astype(BF), piece) for w, piece in zip(weights, keys, strict=True))
    return (accum / total).astype(BF)


def reorder(attended, order):
    place = lax.broadcasted_iota(jnp.int32, (attended.shape[1], order.shape[1]), 0)
    return dot(attended, jnp.where(place == order, 1.0, 0.0).astype(BF)).astype(BF)


def attend_body(most, chips, counts, packs, ids, order, meta, w_query, *refs):
    latents, (att, lat) = refs[:-2], refs[-2:]
    rows = latents[0].shape[1]
    blocks = 2 * chips
    for side in (0, 1):
        for group, ks in enumerate(packs):
            for i, k in enumerate(ks):
                block = pl.multiple_of(ids[side, k] * rows, rows)
                lat[pl.ds(block, rows), :] = latents[side * len(packs) + group][i]
    token = lax.broadcasted_iota(jnp.int32, (most, rows), 1).astype(F32)
    for first in range(0, blocks, counts):
        latent, place = [], []
        for b in range(first, first + counts):
            pick = slots_of(meta[3 * chips + b : 3 * chips + b + 1, 0:rows], most)
            spot = jnp.sum(pick * token, -1, keepdims=True).astype(jnp.int32)
            place.append(spot + (b - first) * rows)
            latent.append(dot(pick.astype(BF), lat[b * rows : (b + 1) * rows, :]).astype(BF))
        place = jnp.concatenate(place, 0)
        key = lax.broadcasted_iota(jnp.int32, (1, counts * rows), 1)
        keys, masks = [lat[first * rows : (first + counts) * rows, :]], [key <= place]
        if first:
            keys.append(lat[0 : first * rows, :])
            masks.append(None)
        attended = attend(jnp.concatenate(latent, 0), keys, masks, w_query[...])
        attended = reorder(attended, order[...])
        for b in range(first, first + counts):
            at = pl.multiple_of(ids[3, b] * most, most)
            att[pl.ds(at, most), :] = attended[(b - first) * most : (b - first + 1) * most, :]


def expert_body(ks, most, chips, meta, att, out_a, out_b, gate_up, expert_down, *refs):
    chosen_refs, outs = refs[:-2], refs[-2:]
    rows = meta.shape[1] // 2
    hidden_width = expert_down.shape[0]
    shard = out_a.shape[0]
    attended, gate = [], []
    for side in (0, 1):
        for k in ks:
            at = side * chips + k
            pick = slots_of(meta[at : at + 1, 0:rows], most)
            gate.append(jnp.sum(pick * meta[at : at + 1, rows : 2 * rows], -1, keepdims=True))
            attended.append(att[at * most : (at + 1) * most, :])
    chosen = jnp.concatenate([ref[i] for ref in chosen_refs for i in range(ref.shape[0])], 0)
    attended = jnp.concatenate(attended, 0)
    hidden = dot(attended[:, :shard], out_a[...]) + dot(attended[:, shard:], out_b[...])
    hidden = (chosen.astype(F32) + hidden).astype(BF)
    both = dot(hidden, gate_up[...])
    inner = (jax.nn.silu(both[:, :hidden_width]) * both[:, hidden_width:]).astype(BF)
    result = (dot(inner, expert_down[...]) * jnp.concatenate(gate, 0)).astype(BF)
    for i in range(2 * len(ks)):
        outs[i // len(ks)][i % len(ks)] = result[i * most : (i + 1) * most]


def spread(k, at, most, chips, meta, mine, theirs, cols):
    rows = meta.shape[1] // 2
    one = slots_of(meta[k : k + 1, 0:rows], most).astype(BF)
    two = slots_of(meta[2 * chips + k : 2 * chips + k + 1, 0:rows], most).astype(BF)
    return dot_first(one, mine[at, :, cols]) + dot_first(two, theirs[at, :, cols])


def combine_body(k, at, most, chips, first, size, meta, mine, theirs, *refs):
    total = spread(k, at, most, chips, meta, mine, theirs, slice(first, first + size))
    if len(refs) > 1:
        total = total + refs[0][...].astype(F32)
    refs[-1][...] = total.astype(BF)


def own_body(at, most, chips, ids, order, meta, w_query, out_a, out_b, tokens, lat, mine, theirs, *outs):
    rows = tokens.shape[0]
    start = pl.multiple_of(ids[0, 0] * rows, rows)
    place = start + lax.broadcasted_iota(jnp.int32, (rows, 1), 0)
    key = lax.broadcasted_iota(jnp.int32, (1, lat.shape[0]), 1)
    attended = attend(lat[pl.ds(start, rows), :], [lat[...]], [key <= place], w_query[...])
    attended = reorder(attended, order[...])
    shard = out_a.shape[0]
    hidden = dot(attended[:, :shard], out_a[...]) + dot(attended[:, shard:], out_b[...])
    hidden = (tokens[...].astype(F32) + hidden).astype(BF).astype(F32)
    first = 0
    for out in outs:
        cols = slice(first, first + out.shape[1])
        total = spread(0, at, most, chips, meta, mine, theirs, cols)
        out[...] = (hidden[:, cols] + total).astype(BF)
        first += out.shape[1]


def final_body(*refs):
    ins, out = refs[:-1], refs[-1]
    first = 0
    for one, two in zip(ins[0::2], ins[1::2], strict=True):
        size = one.shape[1]
        out[:, first : first + size] = (one[...].astype(F32) + two[...].astype(F32)).astype(BF)
        first += size


def after(x, *others):
    return lax.optimization_barrier((x, *others))[0]


def on_device(
    tokens, routes, gates, capacity, w_down_kv, kv_gain, w_query, w_out, w_gate_up, w_expert_down
):
    pipes = lax.axis_size("pipe")
    owners = lax.axis_size("expert")
    chips = owners // 2
    me = lax.axis_index("expert")
    rows, width = tokens.shape[1:]
    top = routes.shape[2]
    latent = w_query.shape[1]
    depth = w_down_kv.shape[1]
    most = max(2, 4 * rows * top // (3 * owners))
    shape = jax.ShapeDtypeStruct

    ring, blocks = [], np.zeros((owners, chips), np.int32)
    for r in range(chips):
        even, odd = 2 * chip_at(r, chips), 2 * chip_at(r, chips) + 1
        ring.append((even, 2 * chip_at(r + 1, chips)))
        ring.append((odd, 2 * chip_at(r - 1, chips) + 1))
        for k in range(chips):
            blocks[even, k] = 2 * chip_at(r - k, chips)
            blocks[odd, k] = 2 * chip_at(r + k, chips) + 1
    step = lambda x: lax.ppermute(x, "expert", ring)
    sibling = lambda x: lax.ppermute(x, "expert", [(i, i ^ 1) for i in range(owners)])
    last = [
        (p * owners + a, ((p + 1) % pipes) * owners + b) for p in range(pipes) for a, b in ring
    ]
    onward = lambda x: lax.ppermute(x, "pipe", [(p, (p + 1) % pipes) for p in range(pipes)])

    table = np.zeros((owners, 4, owners), np.int32)
    for e in range(owners):
        both = np.concatenate([blocks[e], blocks[e ^ 1]])
        table[e, 0, :chips], table[e, 1, :chips] = blocks[e], blocks[e ^ 1]
        table[e, 2, :2] = (e, e ^ 1)
        table[e, 3, both] = np.arange(owners)
    ids = lax.dynamic_index_in_dim(jnp.asarray(table), me, 0, keepdims=False)
    shard = w_out.shape[1]
    order = (ids[:2, :chips].reshape(-1)[:, None] * shard + jnp.arange(shard)[None, :]).reshape(1, -1)

    half = rows // 2
    small = [
        call(pack_body, shape((depth + owners, latent), BF), [VMEM] * 4)(
            routes.transpose(2, 0, 1), gates.transpose(2, 0, 1), capacity, w_down_kv[0]
        )
    ]
    first = [tokens[0, :half]]
    second = [jnp.concatenate([tokens[0, half:], w_out[0]], 0)]
    arrived = []
    for _ in range(1, chips):
        for stream in (small, first, second):
            arrived.append(stream[-1])
            stream.append(step(after(stream[-1], *arrived[-3:-1])))
    down, meta = call(
        functools.partial(unpack_body, depth),
        (shape((owners * depth, latent), BF), shape((5 * chips, 2 * rows), F32)),
        [SMEM] + [VMEM] * owners,
        flops=LONG,
    )(ids, *small, *[sibling(x) for x in small])

    chunks = [(1, 2), (3, 0)] + [(k, k + 1) for k in range(4, chips, 2)]
    chosen = {}
    lat_a, lat_b, groups = [], [], []
    for whole in (range(chips - 1), (chips - 1,)):
        packs = [tuple(k for k in ks if k in whole) for ks in chunks]
        packs = [ks for ks in packs if ks]
        flat = [k for ks in packs for k in ks]
        *picked, lat = call(
            functools.partial(arrive_body, packs, most, chips),
            tuple(shape((len(ks), most, width), BF) for ks in packs for _ in (0, 1))
            + (shape((len(flat), rows, latent), BF),),
            [VMEM] * (3 + 2 * len(flat)),
            flops=LONG,
            limit=16,
        )(meta, down, kv_gain, *[x for k in flat for x in (first[k], second[k])])
        for i, ks in enumerate(packs):
            chosen[ks] = (picked[2 * i], sibling(picked[2 * i + 1]))
        lat_a.append(lat)
        lat_b.append(sibling(lat))
        groups.append(tuple(flat))
    out_a = jnp.concatenate([x[half:] for x in second], 0)
    out_b = sibling(out_a)
    att, lat = call(
        functools.partial(attend_body, most, chips, 4, groups),
        (shape((owners * most, latent), BF), shape((owners * rows, latent), BF)),
        [SMEM] + [VMEM] * (3 + 4),
        flops=LONG,
        limit=16,
    )(ids, order, meta, w_query[0], *lat_a, *lat_b)

    gate_up, expert_down = w_gate_up[0, 0], w_expert_down[0, 0]
    mine, theirs = {}, {}

    def expert(ks, *waits):
        packs = [part for part in chosen if set(part) <= set(ks)]
        packs = [part for k in ks for part in packs if part[0] == k]
        picked = [chosen[part][side] for side in (0, 1) for part in packs]
        result, away = call(
            functools.partial(expert_body, ks, most, chips),
            (shape((len(ks), most, width), BF),) * 2,
            [VMEM] * (6 + len(picked)),
            flops=LONG // 10,
            limit=16,
        )(after(meta, *waits), att, out_a, out_b, gate_up, expert_down, *picked)
        back = sibling(away)
        for i, k in enumerate(ks):
            mine[k], theirs[k] = (result, i), back

    pieces = [(0, width // 2), (width // 2, width - width // 2)]
    passing = [None] * len(pieces)
    expert(chunks[0])
    waiting = list(chunks[1:])
    for k in range(1, chips):
        totals = []
        for i, (start, size) in enumerate(pieces):
            more = [] if passing[i] is None else [passing[i]]
            if k == chips - 2 and more:
                more = [after(more[0], *kept)]
            total = call(
                functools.partial(combine_body, k, mine[k][1], most, chips, start, size),
                shape((rows, size), BF),
                [VMEM] * (3 + len(more)),
            )(meta, mine[k][0], theirs[k], *more)
            totals.append(total)
            if k < chips - 1:
                passing[i] = step(total)
            else:
                passing[i] = lax.ppermute(total, ("pipe", "expert"), last)
        if waiting and k + 2 >= waiting[0][0]:
            expert(waiting.pop(0), totals[0])
        if k == 2:
            kept = call(
                functools.partial(own_body, mine[0][1], most, chips),
                tuple(shape((rows, size), BF) for _, size in pieces),
                [SMEM] + [VMEM] * 9,
            )(
                ids,
                order,
                meta,
                w_query[0],
                out_a,
                out_b,
                after(tokens[0], *totals),
                lat,
                mine[0][0],
                theirs[0],
            )
            passing = [after(x, *kept) for x in passing]
            kept = [onward(x) for x in kept]
    output = call(final_body, shape((rows, width), BF), [VMEM] * (2 * len(pieces)))(
        *[x for pair in zip(kept, passing, strict=True) for x in pair]
    )
    return output[None]


def solution(mesh):
    return jax.shard_map(
        on_device,
        mesh=mesh,
        in_specs=(
            P("pipe", "expert", None),
            P("pipe", "expert", None),
            P("pipe", "expert", None),
            P("pipe", None),
            P("pipe", "expert", None),
            P("pipe", None),
            P("pipe", None, None),
            P("pipe", "expert", None),
            P("pipe", "expert", None, None),
            P("pipe", "expert", None, None),
        ),
        out_specs=P("pipe", "expert", None),
        check_vma=False,
    )
```

time: 201 us -> 179 us (0.89)
  waiting for transfers between devices: 92.6 us -> 70.8 us
  starting transfers between devices: 59.5 us -> 64 us
  Pallas kernels: 39.4 us -> 36.9 us
  local copies, waits for them, and re-layouts: 7.88 us -> 5.84 us
    ppermute x33, waiting for transfers between devices: 68.7 us -> 48 us  [on_device(): step = lambda x: lax.ppermute(x, 'expert', ring)]
    ppermute x10 -> x20, waiting for transfers between devices: 5.64 us -> 2.21 us  [on_device(): lax.ppermute(x, 'expert', [(i, i ^ 1) for i in range(owners)])]
    ppermute x33, starting transfers between devices: 50.2 us -> 53.2 us  [on_device(): step = lambda x: lax.ppermute(x, 'expert', ring)]
    pallas_call x19 -> x22, Pallas kernels: 37.7 us -> 35.1 us  [the longest x4 16.6 us: expert(): call(functools.partial(expert_body, ks, most, chips), (shape((len(ks), mo...]
    ppermute x2, waiting for transfers between devices: 5.73 us -> 8.24 us  [on_device(): lax.ppermute(x, 'pipe', [(p, (p + 1) % pipes) for p in range(pipes)])]
    unnamed x50 -> x29, local copies, waits for them, and re-layouts: 5.85 us -> 3.87 us
  transfers between devices with their start and end apart: 47 -> 57, of which waited for: 27 -> 26; matrix products, arithmetic and copies ran while one was open for 1% -> 2% of each run, Pallas kernels for 5% -> 17%
where the time goes in v3:
time: 179 us
  waiting for transfers between devices  70.8 us (40%)
  starting transfers between devices  64 us (36%)
  Pallas kernels  36.9 us (21%)
  local copies, waits for them, and re-layouts  5.84 us (3%)
    ppermute x33, starting transfers between devices, on_device(): step = lambda x: lax.ppermute(x, 'expert', ring)  53.2 us
    ppermute x33, waiting for transfers between devices, on_device(): step = lambda x: lax.ppermute(x, 'expert', ring)  48 us
    pallas_call x4, Pallas kernels, expert(): call(functools.partial(expert_body, ks, most, chips), (shape((len(ks), mo...  16.6 us
    ppermute x2, waiting for transfers between devices, on_device(): passing[i] = lax.ppermute(total, ('pipe', 'expert'), last)  12.4 us
    ppermute x2, waiting for transfers between devices, on_device(): lax.ppermute(x, 'pipe', [(p, (p + 1) % pipes) for p in range(pipes)])  8.24 us
    pallas_call x1, Pallas kernels, on_device(): call(functools.partial(attend_body, most, chips, 4, groups), (shape((owne...  5.47 us
    pallas_call x2, Pallas kernels, on_device(): call(functools.partial(arrive_body, packs, most, chips), tuple((shape((le...  5.23 us
    ppermute x2, starting transfers between devices, on_device(): passing[i] = lax.ppermute(total, ('pipe', 'expert'), last)  5.11 us
  transfers between devices with their start and end apart: 57, of which 26 were waited for; matrix products, arithmetic and copies ran while one was open for 2% of the time, Pallas kernels for 17%

profile of v3, /device:TPU:0, one launch (start us, length us, event | category | flops | bytes accessed | tf_op | source)
XLA Modules:
  0.0 179.0 jit_solution(13673924284665888045)
XLA Ops:
  4.6 2.6 %collective-permute-start.2 = (bf16[64,2560]{1,0:T(8,128)(2,1)S(1)}, bf16[64,2560]{1,0:T(8,128)(2,1)S(1)}, u32[]{:S(2)}, u32[]{:S(2)}) collective-permute-start(bf16[64,2560]{1,0:T(8,128)(2,1)S(1)} %get-tuple-element.60.refs_6_), channel_id=1, source_target_pairs={{0,4},{1,3},{4,8},{5,1},{8,12},{9,5},{12,14},{13,9},{14,10},{15,13... | collective-permute-start | bytes 983048 | tf_op jit(solution)/shard_map/ppermute | solution.py:254
  24.2 3.6 %collective-permute-done.4.refs_3_ = bf16[176,256]{1,0:T(8,128)(2,1)S(1)} collective-permute-done((bf16[176,256]{1,0:T(8,128)(2,1)S(1)}, bf16[176,256]{1,0:T(8,128)(2,1)S(1)}, u32[]{:S(2)}, u32[]{:S(2)}) %collective-permute-start.4) | collective-permute-done | bytes 90144 | tf_op jit(solution)/shard_map/ppermute | solution.py:254
  33.0 4.4 %collective-permute-done.9.refs_5_ = bf16[80,2560]{1,0:T(8,128)(2,1)S(1)} collective-permute-done((bf16[80,2560]{1,0:T(8,128)(2,1)S(1)}, bf16[80,2560]{1,0:T(8,128)(2,1)S(1)}, u32[]{:S(2)}, u32[]{:S(2)}) %collective-permute-start.9) | collective-permute-done | bytes 409632 | tf_op jit(solution)/shard_map/ppermute | solution.py:254
  42.6 4.4 %collective-permute-done.12.refs_9_ = bf16[80,2560]{1,0:T(8,128)(2,1)S(1)} collective-permute-done((bf16[80,2560]{1,0:T(8,128)(2,1)S(1)}, bf16[80,2560]{1,0:T(8,128)(2,1)S(1)}, u32[]{:S(2)}, u32[]{:S(2)}) %collective-permute-start.12) | collective-permute-done | bytes 409632 | tf_op jit(solution)/shard_map/ppermute | solution.py:254
  50.5 5.4 %collective-permute-done.13.refs_6_ = bf16[176,256]{1,0:T(8,128)(2,1)S(1)} collective-permute-done((bf16[176,256]{1,0:T(8,128)(2,1)S(1)}, bf16[176,256]{1,0:T(8,128)(2,1)S(1)}, u32[]{:S(2)}, u32[]{:S(2)}) %collective-permute-start.13) | collective-permute-done | bytes 90144 | tf_op jit(solution)/shard_map/ppermute | solution.py:254
  59.7 3.4 %collective-permute-done.26.refs_12_ = bf16[64,2560]{1,0:T(8,128)(2,1)} collective-permute-done((bf16[64,2560]{1,0:T(8,128)(2,1)S(1)}, bf16[64,2560]{1,0:T(8,128)(2,1)}, u32[]{:S(2)}, u32[]{:S(2)}) %collective-permute-start.26) | collective-permute-done | bytes 327712 | tf_op jit(solution)/shard_map/ppermute | solution.py:254
  67.9 7.9 %collective-permute-done.25.refs_13_ = bf16[80,2560]{1,0:T(8,128)(2,1)S(1)} collective-permute-done((bf16[80,2560]{1,0:T(8,128)(2,1)S(1)}, bf16[80,2560]{1,0:T(8,128)(2,1)S(1)}, u32[]{:S(2)}, u32[]{:S(2)}) %collective-permute-start.25) | collective-permute-done | bytes 409632 | tf_op jit(solution)/shard_map/ppermute | solution.py:254
  77.3 3.7 %shard_map.111 = (bf16[2,64,2560]{2,1,0:T(8,128)(2,1)S(1)}, bf16[2,64,2560]{2,1,0:T(8,128)(2,1)}, bf16[2,64,2560]{2,1,0:T(8,128)(2,1)S(1)}, bf16[2,64,2560]{2,1,...) custom-call(f32[40,256]{1,0:T(8,128)S(1)} %get-tuple-element.103.met, ...), custom_call_target="tpu_custom_call" | custom-call | flops 99999997952 | bytes 1000000000 | tf_op jit(solution)/shard_map/pallas_call | solution.py:298
  81.6 2.1 %collective-permute-done.27.refs_1_ = bf16[80,2560]{1,0:T(8,128)(2,1)S(1)} collective-permute-done((bf16[80,2560]{1,0:T(8,128)(2,1)S(1)}, bf16[80,2560]{1,0:T(8,128)(2,1)S(1)}, u32[]{:S(2)}, u32[]{:S(2)}) %collective-permute-start.27) | collective-permute-done | bytes 409632 | tf_op jit(solution)/shard_map/ppermute | solution.py:254
  86.6 5.5 %shard_map.113 = (bf16[1024,256]{1,0:T(8,128)(2,1)S(1)}, bf16[2048,256]{1,0:T(8,128)(2,1)S(1)}) custom-call(s32[4,16]{1,0:T(4,128)S(1)} %dynamic-slice_bitcast_fusion.ids, s32[1,256]{1,0:T(1,128)S(1)} %add.31.order, f32[40,256]{1,0:T(8,128)S(1)} %get-tuple-element.103.meta, bf16[256,256]{1,0:T(8,128)(2,1)S(1)} %bitcast.17, ...), custom_call_target="tpu_custom_call" | custom-call | flops 99999997952 | bytes 1000000000 | tf_op jit(solution)/shard_map/pallas_call | solution.py:313
  92.1 5.0 %shard_map.114 = (bf16[2,64,2560]{2,1,0:T(8,128)(2,1)S(1)}, bf16[2,64,2560]{2,1,0:T(8,128)(2,1)S(1)}) custom-call(f32[40,256]{1,0:T(8,128)S(1)} %get-tuple-element.103.meta, bf16[1024,256]{1,0:T(8,128)(2,1)S(1)} %get-tuple-element.83.att, bf16[128,2560]{1,0:T(8,128)(2,1)S(1)} %slice_dynamic-update-slice_fusion.out_a, ...), custom_call_target="tpu_custom_call" | custom-call | flops 10000000000 | bytes 100000000 | tf_op jit(solution)/shard_map/pallas_call | solution.py:328
  103.4 3.9 %shard_map.119 = (bf16[2,64,2560]{2,1,0:T(8,128)(2,1)S(1)}, bf16[2,64,2560]{2,1,0:T(8,128)(2,1)S(1)}) custom-call(f32[40,256]{1,0:T(8,128)S(1)} %get-tuple-element.103.meta, bf16[1024,256]{1,0:T(8,128)(2,1)S(1)} %get-tuple-element.83.att, bf16[128,2560]{1,0:T(8,128)(2,1)S(1)} %slice_dynamic-update-slice_fusion.out_a, ...), custom_call_target="tpu_custom_call" | custom-call | flops 10000000000 | bytes 100000000 | tf_op jit(solution)/shard_map/pallas_call | solution.py:328
  112.2 3.9 %shard_map.121 = (bf16[2,64,2560]{2,1,0:T(8,128)(2,1)S(1)}, bf16[2,64,2560]{2,1,0:T(8,128)(2,1)S(1)}) custom-call(f32[40,256]{1,0:T(8,128)S(1)} %get-tuple-element.103.meta, bf16[1024,256]{1,0:T(8,128)(2,1)S(1)} %get-tuple-element.83.att, bf16[128,2560]{1,0:T(8,128)(2,1)S(1)} %slice_dynamic-update-slice_fusion.out_a, ...), custom_call_target="tpu_custom_call" | custom-call | flops 10000000000 | bytes 100000000 | tf_op jit(solution)/shard_map/pallas_call | solution.py:328
  116.2 2.8 %shard_map.120 = (bf16[128,1280]{1,0:T(8,128)(2,1)S(1)}, bf16[128,1280]{1,0:T(8,128)(2,1)S(1)}) custom-call(s32[4,16]{1,0:T(4,128)S(1)} %dynamic-slice_bitcast_fusion.ids, s32[1,256]{1,0:T(1,128)S(1)} %add.31.order, f32[40,256]{1,0:T(8,128)S(1)} %get-tuple-element.103.meta, bf16[256,256]{1,0:T(8,128)(2,1)S(1)} %bitcast.18, ...), custom_call_target="tpu_custom_call" | custom-call | tf_op jit(solution)/shard_map/pallas_call | solution.py:362
  122.9 3.7 %collective-permute-done.52.refs_0_ = bf16[128,1280]{1,0:T(8,128)(2,1)S(1)} collective-permute-done((bf16[128,1280]{1,0:T(8,128)(2,1)S(1)}, bf16[128,1280]{1,0:T(8,128)(2,1)S(1)}, u32[]{:S(2)}, u32[]{:S(2)}) %collective-permute-start.52) | collective-permute-done | bytes 327712 | tf_op jit(solution)/shard_map/ppermute | solution.py:254
  130.4 3.9 %shard_map.124 = (bf16[2,64,2560]{2,1,0:T(8,128)(2,1)S(1)}, bf16[2,64,2560]{2,1,0:T(8,128)(2,1)S(1)}) custom-call(f32[40,256]{1,0:T(8,128)S(1)} %get-tuple-element.103.meta, bf16[1024,256]{1,0:T(8,128)(2,1)S(1)} %get-tuple-element.83.att, bf16[128,2560]{1,0:T(8,128)(2,1)S(1)} %slice_dynamic-update-slice_fusion.out_a, ...), custom_call_target="tpu_custom_call" | custom-call | flops 10000000000 | bytes 100000000 | tf_op jit(solution)/shard_map/pallas_call | solution.py:328
  139.4 2.1 %collective-permute-done.46.refs_0_ = bf16[128,1280]{1,0:T(8,128)(2,1)S(1)} collective-permute-done((bf16[128,1280]{1,0:T(8,128)(2,1)S(1)}, bf16[128,1280]{1,0:T(8,128)(2,1)S(1)}, u32[]{:S(2)}, u32[]{:S(2)}) %collective-permute-start.46) | collective-permute-done | bytes 327712 | tf_op jit(solution)/shard_map/ppermute | solution.py:254
  143.5 3.2 %collective-permute-done.38.refs_0_ = bf16[128,1280]{1,0:T(8,128)(2,1)S(1)} collective-permute-done((bf16[128,1280]{1,0:T(8,128)(2,1)S(1)}, bf16[128,1280]{1,0:T(8,128)(2,1)S(1)}, u32[]{:S(2)}, u32[]{:S(2)}) %collective-permute-start.38) | collective-permute-done | bytes 327712 | tf_op jit(solution)/shard_map/ppermute | solution.py:259
  146.6 5.1 %collective-permute-done.48.refs_2_ = bf16[128,1280]{1,0:T(8,128)(2,1)S(1)} collective-permute-done((bf16[128,1280]{1,0:T(8,128)(2,1)S(1)}, bf16[128,1280]{1,0:T(8,128)(2,1)S(1)}, u32[]{:S(2)}, u32[]{:S(2)}) %collective-permute-start.48) | collective-permute-done | bytes 327712 | tf_op jit(solution)/shard_map/ppermute | solution.py:259
  155.6 3.6 %collective-permute-done.55.refs_0_ = bf16[128,1280]{1,0:T(8,128)(2,1)S(1)} collective-permute-done((bf16[128,1280]{1,0:T(8,128)(2,1)S(1)}, bf16[128,1280]{1,0:T(8,128)(2,1)S(1)}, u32[]{:S(2)}, u32[]{:S(2)}) %collective-permute-start.55) | collective-permute-done | bytes 327712 | tf_op jit(solution)/shard_map/ppermute | solution.py:254
  159.6 2.6 %collective-permute-start.56 = (bf16[128,1280]{1,0:T(8,128)(2,1)S(1)}, bf16[128,1280]{1,0:T(8,128)(2,1)S(1)}, u32[]{:S(2)}, u32[]{:S(2)}) collective-permute-start(bf16[128,1280]{1,0:T(8,128)(2,1)S(1)} %shard_map.132), channel_id=1, source_target_pairs={{0,20},{1,19},{4,24},{5,17},{8,28},{9,21},{12,30},{13,25},{14,26},... | collective-permute-start | bytes 983048 | tf_op jit(solution)/shard_map/ppermute | solution.py:358
  163.1 2.6 %collective-permute-start.50 = (bf16[128,1280]{1,0:T(8,128)(2,1)S(1)}, bf16[128,1280]{1,0:T(8,128)(2,1)S(1)}, u32[]{:S(2)}, u32[]{:S(2)}) collective-permute-start(bf16[128,1280]{1,0:T(8,128)(2,1)S(1)} %shard_map.127), channel_id=1, source_target_pairs={{0,20},{1,19},{4,24},{5,17},{8,28},{9,21},{12,30},{13,25},{14,26},... | collective-permute-start | bytes 983048 | tf_op jit(solution)/shard_map/ppermute | solution.py:358
  165.6 8.9 %collective-permute-done.56.refs_3_ = bf16[128,1280]{1,0:T(8,128)(2,1)S(1)} collective-permute-done((bf16[128,1280]{1,0:T(8,128)(2,1)S(1)}, bf16[128,1280]{1,0:T(8,128)(2,1)S(1)}, u32[]{:S(2)}, u32[]{:S(2)}) %collective-permute-start.56) | collective-permute-done | bytes 327712 | tf_op jit(solution)/shard_map/ppermute | solution.py:358
  174.5 3.5 %collective-permute-done.50.refs_1_ = bf16[128,1280]{1,0:T(8,128)(2,1)S(1)} collective-permute-done((bf16[128,1280]{1,0:T(8,128)(2,1)S(1)}, bf16[128,1280]{1,0:T(8,128)(2,1)S(1)}, u32[]{:S(2)}, u32[]{:S(2)}) %collective-permute-start.50) | collective-permute-done | bytes 327712 | tf_op jit(solution)/shard_map/ppermute | solution.py:358
  (152 shorter events, 81.1 us)
Async XLA Ops:
  3.0 56.0 %collective-permute-start.17 = (bf16[176,256]{1,0:T(8,128)(2,1)S(1)}, bf16[176,256]{1,0:T(8,128)(2,1)S(1)}, u32[]{:S(2)}, u32[]{:S(2)}) collective-permute-start(bf16[176,256]{1,0:T(8,128)(2,1)S(1)} %shard_map.109.refs_0_), channel_id=1, source_target_pairs={{0,1},{1,0},{2,3},{3,2},{4,5},{5,4},{6,7},{7,6},{8,9},{9,8},{10,11... | collective-permute-start | bytes 270344 | tf_op jit(solution)/shard_map/ppermute | solution.py:255
  4.6 10.7 %collective-permute-start.2 = (bf16[64,2560]{1,0:T(8,128)(2,1)S(1)}, bf16[64,2560]{1,0:T(8,128)(2,1)S(1)}, u32[]{:S(2)}, u32[]{:S(2)}) collective-permute-start(bf16[64,2560]{1,0:T(8,128)(2,1)S(1)} %get-tuple-element.60.refs_6_), channel_id=1, source_target_pairs={{0,4},{1,3},{4,8},{5,1},{8,12},{9,5},{12,14},{13,9},{14,10},{15,13... | collective-permute-start | bytes 983048 | tf_op jit(solution)/shard_map/ppermute | solution.py:254
  17.7 10.0 %collective-permute-start.6 = (bf16[80,2560]{1,0:T(8,128)(2,1)S(1)}, bf16[80,2560]{1,0:T(8,128)(2,1)S(1)}, u32[]{:S(2)}, u32[]{:S(2)}) collective-permute-start(bf16[80,2560]{1,0:T(8,128)(2,1)S(1)} %collective-permute-done.3.refs_1_), channel_id=1, source_target_pairs={{0,4},{1,3},{4,8},{5,1},{8,12},{9,5},{12,14},{13,9},{14,10},{15,13... | collective-permute-start | bytes 1228808 | tf_op jit(solution)/shard_map/ppermute | solution.py:254
  21.5 37.6 %collective-permute-start.18 = (bf16[176,256]{1,0:T(8,128)(2,1)S(1)}, bf16[176,256]{1,0:T(8,128)(2,1)S(1)}, u32[]{:S(2)}, u32[]{:S(2)}) collective-permute-start(bf16[176,256]{1,0:T(8,128)(2,1)S(1)} %collective-permute-done.refs_1_), channel_id=1, source_target_pairs={{0,1},{1,0},{2,3},{3,2},{4,5},{5,4},{6,7},{7,6},{8,9},{9,8},{10,11... | collective-permute-start | bytes 270344 | tf_op jit(solution)/shard_map/ppermute | solution.py:255
  22.4 8.9 %collective-permute-start.8 = (bf16[64,2560]{1,0:T(8,128)(2,1)S(1)}, bf16[64,2560]{1,0:T(8,128)(2,1)S(1)}, u32[]{:S(2)}, u32[]{:S(2)}) collective-permute-start(bf16[64,2560]{1,0:T(8,128)(2,1)S(1)} %collective-permute-done.5.refs_2_), channel_id=1, source_target_pairs={{0,4},{1,3},{4,8},{5,1},{8,12},{9,5},{12,14},{13,9},{14,10},{15,13... | collective-permute-start | bytes 983048 | tf_op jit(solution)/shard_map/ppermute | solution.py:254
  31.2 9.7 %collective-permute-start.11 = (bf16[64,2560]{1,0:T(8,128)(2,1)S(1)}, bf16[64,2560]{1,0:T(8,128)(2,1)S(1)}, u32[]{:S(2)}, u32[]{:S(2)}) collective-permute-start(bf16[64,2560]{1,0:T(8,128)(2,1)S(1)} %collective-permute-done.8.refs_4_), channel_id=1, source_target_pairs={{0,4},{1,3},{4,8},{5,1},{8,12},{9,5},{12,14},{13,9},{14,10},{15,13... | collective-permute-start | bytes 983048 | tf_op jit(solution)/shard_map/ppermute | solution.py:254
  37.5 11.1 %collective-permute-start.10 = (bf16[176,256]{1,0:T(8,128)(2,1)S(1)}, bf16[176,256]{1,0:T(8,128)(2,1)S(1)}, u32[]{:S(2)}, u32[]{:S(2)}) collective-permute-start(bf16[176,256]{1,0:T(8,128)(2,1)S(1)} %collective-permute-done.7.refs_4_), channel_id=1, source_target_pairs={{0,4},{1,3},{4,8},{5,1},{8,12},{9,5},{12,14},{13,9},{14,10},{15,13... | collective-permute-start | bytes 270344 | tf_op jit(solution)/shard_map/ppermute | solution.py:254
  41.0 9.5 %collective-permute-start.14 = (bf16[64,2560]{1,0:T(8,128)(2,1)S(1)}, bf16[64,2560]{1,0:T(8,128)(2,1)S(1)}, u32[]{:S(2)}, u32[]{:S(2)}) collective-permute-start(bf16[64,2560]{1,0:T(8,128)(2,1)S(1)} %collective-permute-done.11.refs_8_), channel_id=1, source_target_pairs={{0,4},{1,3},{4,8},{5,1},{8,12},{9,5},{12,14},{13,9},{14,10},{15,13... | collective-permute-start | bytes 983048 | tf_op jit(solution)/shard_map/ppermute | solution.py:254
  47.0 10.5 %collective-permute-start.15 = (bf16[80,2560]{1,0:T(8,128)(2,1)S(1)}, bf16[80,2560]{1,0:T(8,128)(2,1)S(1)}, u32[]{:S(2)}, u32[]{:S(2)}) collective-permute-start(bf16[80,2560]{1,0:T(8,128)(2,1)S(1)} %collective-permute-done.12.refs_9_), channel_id=1, source_target_pairs={{0,4},{1,3},{4,8},{5,1},{8,12},{9,5},{12,14},{13,9},{14,10},{15,13... | collective-permute-start | bytes 1228808 | tf_op jit(solution)/shard_map/ppermute | solution.py:254
  50.5 9.1 %collective-permute-start.19 = (bf16[176,256]{1,0:T(8,128)(2,1)S(1)}, bf16[176,256]{1,0:T(8,128)(2,1)S(1)}, u32[]{:S(2)}, u32[]{:S(2)}) collective-permute-start(bf16[176,256]{1,0:T(8,128)(2,1)S(1)} %collective-permute-done.1.refs_2_), channel_id=1, source_target_pairs={{0,1},{1,0},{2,3},{3,2},{4,5},{5,4},{6,7},{7,6},{8,9},{9,8},{10,11... | collective-permute-start | bytes 270344 | tf_op jit(solution)/shard_map/ppermute | solution.py:255
  64.0 17.6 %collective-permute-start.29 = (bf16[64,2560]{1,0:T(8,128)(2,1)}, bf16[64,2560]{1,0:T(8,128)(2,1)}, u32[]{:S(2)}, u32[]{:S(2)}) collective-permute-start(bf16[64,2560]{1,0:T(8,128)(2,1)} %collective-permute-done.26.refs_12_), channel_id=1, source_target_pairs={{0,4},{1,3},{4,8},{5,1},{8,12},{9,5},{12,14},{13,9},{14,10},{15,13... | collective-permute-start | bytes 983048 | tf_op jit(solution)/shard_map/ppermute | solution.py:254
  65.6 10.1 %collective-permute-start.25 = (bf16[80,2560]{1,0:T(8,128)(2,1)S(1)}, bf16[80,2560]{1,0:T(8,128)(2,1)S(1)}, u32[]{:S(2)}, u32[]{:S(2)}) collective-permute-start(bf16[80,2560]{1,0:T(8,128)(2,1)S(1)} %collective-permute-done.15.refs_11_), channel_id=1, source_target_pairs={{0,4},{1,3},{4,8},{5,1},{8,12},{9,5},{12,14},{13,9},{14,10},{15,13... | collective-permute-start | bytes 1228808 | tf_op jit(solution)/shard_map/ppermute | solution.py:254
  81.1 11.0 %collective-permute-start.32 = (bf16[2,64,2560]{2,1,0:T(8,128)(2,1)}, bf16[2,64,2560]{2,1,0:T(8,128)(2,1)}, u32[]{:S(2)}, u32[]{:S(2)}) collective-permute-start(bf16[2,64,2560]{2,1,0:T(8,128)(2,1)} %get-tuple-element.85), channel_id=1, source_target_pairs={{0,1},{1,0},{2,3},{3,2},{4,5},{5,4},{6,7},{7,6},{8,9},{9,8},{10,11... | collective-permute-start | bytes 1966088 | tf_op jit(solution)/shard_map/ppermute | solution.py:255
  97.6 14.6 %collective-permute-start.39 = (bf16[2,64,2560]{2,1,0:T(8,128)(2,1)S(1)}, bf16[2,64,2560]{2,1,0:T(8,128)(2,1)S(1)}, u32[]{:S(2)}, u32[]{:S(2)}) collective-permute-start(bf16[2,64,2560]{2,1,0:T(8,128)(2,1)S(1)} %get-tuple-element.98), channel_id=1, source_target_pairs={{0,1},{1,0},{2,3},{3,2},{4,5},{5,4},{6,7},{7,6},{8,9},{9,8},{10,11... | collective-permute-start | bytes 1966088 | tf_op jit(solution)/shard_map/ppermute | solution.py:255
  107.3 8.9 %collective-permute-start.37 = (bf16[2,64,2560]{2,1,0:T(8,128)(2,1)S(1)}, bf16[2,64,2560]{2,1,0:T(8,128)(2,1)S(1)}, u32[]{:S(2)}, u32[]{:S(2)}) collective-permute-start(bf16[2,64,2560]{2,1,0:T(8,128)(2,1)S(1)} %get-tuple-element.94), channel_id=1, source_target_pairs={{0,1},{1,0},{2,3},{3,2},{4,5},{5,4},{6,7},{7,6},{8,9},{9,8},{10,11... | collective-permute-start | bytes 1966088 | tf_op jit(solution)/shard_map/ppermute | solution.py:255
  107.7 13.3 %collective-permute-start.41 = (bf16[128,1280]{1,0:T(8,128)(2,1)S(1)}, bf16[128,1280]{1,0:T(8,128)(2,1)S(1)}, u32[]{:S(2)}, u32[]{:S(2)}) collective-permute-start(bf16[128,1280]{1,0:T(8,128)(2,1)S(1)} %shard_map.116), channel_id=1, source_target_pairs={{0,4},{1,3},{4,8},{5,1},{8,12},{9,5},{12,14},{13,9},{14,10},{15,13... | collective-permute-start | bytes 983048 | tf_op jit(solution)/shard_map/ppermute | solution.py:254
  126.9 11.1 %collective-permute-start.53 = (bf16[128,1280]{1,0:T(8,128)(2,1)S(1)}, bf16[128,1280]{1,0:T(8,128)(2,1)S(1)}, u32[]{:S(2)}, u32[]{:S(2)}) collective-permute-start(bf16[128,1280]{1,0:T(8,128)(2,1)S(1)} %shard_map.129), channel_id=1, source_target_pairs={{0,4},{1,3},{4,8},{5,1},{8,12},{9,5},{12,14},{13,9},{14,10},{15,13... | collective-permute-start | bytes 983048 | tf_op jit(solution)/shard_map/ppermute | solution.py:254
  134.3 17.4 %collective-permute-start.45 = (bf16[2,64,2560]{2,1,0:T(8,128)(2,1)S(1)}, bf16[2,64,2560]{2,1,0:T(8,128)(2,1)S(1)}, u32[]{:S(2)}, u32[]{:S(2)}) collective-permute-start(bf16[2,64,2560]{2,1,0:T(8,128)(2,1)S(1)} %get-tuple-element.109), channel_id=1, source_target_pairs={{0,1},{1,0},{2,3},{3,2},{4,5},{5,4},{6,7},{7,6},{8,9},{9,8},{10,11... | collective-permute-start | bytes 1966088 | tf_op jit(solution)/shard_map/ppermute | solution.py:255
  136.0 10.6 %collective-permute-start.38 = (bf16[128,1280]{1,0:T(8,128)(2,1)S(1)}, bf16[128,1280]{1,0:T(8,128)(2,1)S(1)}, u32[]{:S(2)}, u32[]{:S(2)}) collective-permute-start(bf16[128,1280]{1,0:T(8,128)(2,1)S(1)} %get-tuple-element.95), channel_id=1, source_target_pairs={{0,16},{16,0},{1,17},{17,1},{2,18},{18,2},{3,19},{19,3},{4,20},{20... | collective-permute-start | bytes 983048 | tf_op jit(solution)/shard_map/ppermute | solution.py:259
  137.5 14.2 %collective-permute-start.48 = (bf16[128,1280]{1,0:T(8,128)(2,1)S(1)}, bf16[128,1280]{1,0:T(8,128)(2,1)S(1)}, u32[]{:S(2)}, u32[]{:S(2)}) collective-permute-start(bf16[128,1280]{1,0:T(8,128)(2,1)S(1)} %get-tuple-element.101), channel_id=1, source_target_pairs={{0,16},{16,0},{1,17},{17,1},{2,18},{18,2},{3,19},{19,3},{4,20},{20... | collective-permute-start | bytes 983048 | tf_op jit(solution)/shard_map/ppermute | solution.py:259
  138.4 13.3 %collective-permute-start.54 = (bf16[128,1280]{1,0:T(8,128)(2,1)S(1)}, bf16[128,1280]{1,0:T(8,128)(2,1)S(1)}, u32[]{:S(2)}, u32[]{:S(2)}) collective-permute-start(bf16[128,1280]{1,0:T(8,128)(2,1)S(1)} %shard_map.130), channel_id=1, source_target_pairs={{0,4},{1,3},{4,8},{5,1},{8,12},{9,5},{12,14},{13,9},{14,10},{15,13... | collective-permute-start | bytes 983048 | tf_op jit(solution)/shard_map/ppermute | solution.py:254
  141.9 11.8 %collective-permute-start.47 = (bf16[128,1280]{1,0:T(8,128)(2,1)S(1)}, bf16[128,1280]{1,0:T(8,128)(2,1)S(1)}, u32[]{:S(2)}, u32[]{:S(2)}) collective-permute-start(bf16[128,1280]{1,0:T(8,128)(2,1)S(1)} %shard_map.125), channel_id=1, source_target_pairs={{0,4},{1,3},{4,8},{5,1},{8,12},{9,5},{12,14},{13,9},{14,10},{15,13... | collective-permute-start | bytes 983048 | tf_op jit(solution)/shard_map/ppermute | solution.py:254
  159.6 14.9 %collective-permute-start.56 = (bf16[128,1280]{1,0:T(8,128)(2,1)S(1)}, bf16[128,1280]{1,0:T(8,128)(2,1)S(1)}, u32[]{:S(2)}, u32[]{:S(2)}) collective-permute-start(bf16[128,1280]{1,0:T(8,128)(2,1)S(1)} %shard_map.132), channel_id=1, source_target_pairs={{0,20},{1,19},{4,24},{5,17},{8,28},{9,21},{12,30},{13,25},{14,26},... | collective-permute-start | bytes 983048 | tf_op jit(solution)/shard_map/ppermute | solution.py:358
  163.1 14.9 %collective-permute-start.50 = (bf16[128,1280]{1,0:T(8,128)(2,1)S(1)}, bf16[128,1280]{1,0:T(8,128)(2,1)S(1)}, u32[]{:S(2)}, u32[]{:S(2)}) collective-permute-start(bf16[128,1280]{1,0:T(8,128)(2,1)S(1)} %shard_map.127), channel_id=1, source_target_pairs={{0,20},{1,19},{4,24},{5,17},{8,28},{9,21},{12,30},{13,25},{14,26},... | collective-permute-start | bytes 983048 | tf_op jit(solution)/shard_map/ppermute | solution.py:358
  (44 other events, 263.9 us)

commit v4 on v3

--- a/solution.py
+++ b/solution.py
@@ -14,6 +14,7 @@
 SMEM = pl.BlockSpec(memory_space=pltpu.SMEM)
 MIB = 1024 * 1024
 LONG = 10**11
+SHORT = 3 * 10**9
 
 
 def chip_at(place, chips):
@@ -22,14 +23,16 @@
     return 2 * place if place < half else 2 * (chips - 1 - place) + 1
 
 
-def call(body, outs, ins, limit=12, flops=0):
+def call(body, outs, ins, limit=12, flops=0, moved=None):
     return pl.pallas_call(
         body,
         out_shape=outs,
         in_specs=ins,
         out_specs=jax.tree.map(lambda _: VMEM, outs),
         compiler_params=pltpu.CompilerParams(vmem_limit_bytes=limit * MIB),
-        cost_estimate=pl.CostEstimate(flops=flops, transcendentals=0, bytes_accessed=flops // 100),
+        cost_estimate=pl.CostEstimate(
+            flops=flops, transcendentals=0, bytes_accessed=flops // 100 if moved is None else moved
+        ),
     )
 
 
@@ -50,9 +53,15 @@
     return jnp.where(ids == row, 1.0, 0.0)
 
 
-def pack_body(routes, gates, capacity, down, out):
+def pack_body(tokens, routes, gates, capacity, down, out, first, second):
     top, _, rows = routes.shape
     experts = capacity.shape[1]
+    latent = down.shape[1]
+    half = rows // 2
+    for j in range(tokens.shape[1] // latent):
+        first[j * half : (j + 1) * half, :] = tokens[0:half, j * latent : (j + 1) * latent]
+    second[0:half, :] = tokens[half:rows, :]
+    second[half : half + out.shape[0], :] = out[...]
     expert = lax.broadcasted_iota(jnp.int32, (experts, rows), 0)
     named = jnp.zeros((experts, rows), F32)
     gate = jnp.zeros((experts, rows), F32)
@@ -67,14 +76,26 @@
     col = lax.broadcasted_iota(jnp.int32, (experts, experts), 1)
     limit = jnp.sum(jnp.where(row == col, capacity[...].astype(F32), 0.0), 1, keepdims=True)
     kept = (named > 0.5) & (rank < limit)
-    depth = down.shape[0]
-    out[0:depth, :] = down[...]
-    out[depth : depth + experts, 0:rows] = jnp.where(kept, rank, -1.0).astype(BF)
-    out[depth : depth + experts, rows : 2 * rows] = jnp.where(kept, gate, 0.0).astype(BF)
+    start = tokens.shape[1] // latent * half
+    first[start : start + down.shape[0], :] = down[...]
+    start += down.shape[0]
+    first[start : start + experts, 0:rows] = jnp.where(kept, rank, -1.0).astype(BF)
+    first[start : start + experts, rows : 2 * rows] = jnp.where(kept, gate, 0.0).astype(BF)
+
+
+def tail_body(piece, out):
+    out[...] = piece[piece.shape[0] - out.shape[0] :, :]
+
+
+def stack_body(*refs):
+    ins, out = refs[:-1], refs[-1]
+    for i, piece in enumerate(ins):
+        out[i] = piece[...]
 
 
 def unpack_body(depth, ids, *refs):
-    halves, (down, meta) = refs[:-2], refs[-2:]
+    arrays, (down, meta) = refs[:-2], refs[-2:]
+    halves = [ref.at[i] for ref in arrays for i in range(ref.shape[0])]
     chips = len(halves) // 2
     tall, wide = halves[0].shape
     experts = tall - depth
@@ -97,12 +118,15 @@
     count = sum(len(ks) for ks in packs)
     pieces, outs = refs[: 2 * count], refs[2 * count :]
     latents = outs[-1]
-    rows = latents.shape[1]
+    rows, latent = latents.shape[1:]
     half = rows // 2
     at = 0
     for g, ks in enumerate(packs):
         for i, k in enumerate(ks):
-            x = jnp.concatenate([pieces[2 * at][...], pieces[2 * at + 1][0:half, :]], 0)
+            one, two = pieces[2 * at], pieces[2 * at + 1]
+            blocks = range(two.shape[1] // latent)
+            one = jnp.concatenate([one[j * half : (j + 1) * half, :] for j in blocks], 1)
+            x = jnp.concatenate([one, two[0:half, :]], 0)
             pick = jnp.concatenate(
                 [slots_of(meta[j : j + 1, 0:rows], most) for j in (k, 2 * chips + k)], 0
             ).astype(BF)
@@ -269,22 +293,41 @@
     order = (ids[:2, :chips].reshape(-1)[:, None] * shard + jnp.arange(shard)[None, :]).reshape(1, -1)
 
     half = rows // 2
-    small = [
-        call(pack_body, shape((depth + owners, latent), BF), [VMEM] * 4)(
-            routes.transpose(2, 0, 1), gates.transpose(2, 0, 1), capacity, w_down_kv[0]
+    tall = depth + owners
+    one, two = call(
+        pack_body,
+        (
+            shape((width // latent * half + tall, latent), BF),
+            shape((half + shard, width), BF),
+        ),
+        [VMEM] * 6,
+    )(
+        tokens[0],
+        routes.transpose(2, 0, 1),
+        gates.transpose(2, 0, 1),
+        capacity,
+        w_down_kv[0],
+        w_out[0],
+    )
+    def tail(x, rows, *others):
+        return call(tail_body, shape((rows, x.shape[1]), BF), [VMEM], flops=SHORT, moved=0)(
+            after(x, *others)
         )
-    ]
-    first = [tokens[0, :half]]
-    second = [jnp.concatenate([tokens[0, half:], w_out[0]], 0)]
-    arrived = []
-    for _ in range(1, chips):
-        for stream in (small, first, second):
-            arrived.append(stream[-1])
-            stream.append(step(after(stream[-1], *arrived[-3:-1])))
+
+    first, second = [one], [two]
+    small = [tail(one, tall)]
+    outs = [tail(two, shard, small[0])]
+    for k in range(1, chips):
+        first.append(step(after(first[-1], *outs[k - 2 : k - 1])))
+        second.append(step(after(second[-1], small[k - 1])))
+        small.append(tail(first[k], tall, outs[k - 1]))
+        outs.append(tail(second[k], shard, small[k]))
+    stack = lambda xs: call(stack_body, shape((len(xs), *xs[0].shape), BF), [VMEM] * len(xs))(*xs)
+    small = [stack(small[:-1]), stack(small[-1:])]
     down, meta = call(
         functools.partial(unpack_body, depth),
         (shape((owners * depth, latent), BF), shape((5 * chips, 2 * rows), F32)),
-        [SMEM] + [VMEM] * owners,
+        [SMEM] + [VMEM] * 4,
         flops=LONG,
     )(ids, *small, *[sibling(x) for x in small])
 
@@ -308,7 +351,7 @@
         lat_a.append(lat)
         lat_b.append(sibling(lat))
         groups.append(tuple(flat))
-    out_a = jnp.concatenate([x[half:] for x in second], 0)
+    out_a = stack(outs).reshape(-1, width)
     out_b = sibling(out_a)
     att, lat = call(
         functools.partial(attend_body, most, chips, 4, groups),
@@ -340,23 +383,24 @@
     passing = [None] * len(pieces)
     expert(chunks[0])
     waiting = list(chunks[1:])
+    def combine(k, i, *more):
+        start, size = pieces[i]
+        return call(
+            functools.partial(combine_body, k, mine[k][1], most, chips, start, size),
+            shape((rows, size), BF),
+            [VMEM] * (3 + len(more)),
+        )(meta, mine[k][0], theirs[k], *more)
+
+    cross = lambda x: lax.ppermute(x, ("pipe", "expert"), last)
     for k in range(1, chips):
         totals = []
-        for i, (start, size) in enumerate(pieces):
-            more = [] if passing[i] is None else [passing[i]]
-            if k == chips - 2 and more:
-                more = [after(more[0], *kept)]
-            total = call(
-                functools.partial(combine_body, k, mine[k][1], most, chips, start, size),
-                shape((rows, size), BF),
-                [VMEM] * (3 + len(more)),
-            )(meta, mine[k][0], theirs[k], *more)
-            totals.append(total)
-            if k < chips - 1:
-                passing[i] = step(total)
-            else:
-                passing[i] = lax.ppermute(total, ("pipe", "expert"), last)
-        if waiting and k + 2 >= waiting[0][0]:
+        for i in range(len(pieces)):
+            more = [] if k == 1 else [passing[i]]
+            if i == 0 and chips - 3 <= k < chips - 1:
+                more = [after(more[0], kept[k - (chips - 3)])]
+            totals.append(combine(k, i, *more))
+            passing[i] = (cross if k == chips - 1 else step)(totals[i])
+        if waiting and k + 3 >= waiting[0][0]:
             expert(waiting.pop(0), totals[0])
         if k == 2:
             kept = call(

time: 179 us -> 164 us (0.916)
  waiting for transfers between devices: 70.8 us -> 60.6 us
  starting transfers between devices: 64 us -> 57.2 us
    ppermute x2, waiting for transfers between devices: 8.24 us -> 1.85 us  [on_device(): lax.ppermute(x, 'pipe', [(p, (p + 1) % pipes) for p in range(pipes)])]
    ppermute x33 -> x26, starting transfers between devices: 53.2 us -> 46.9 us  [on_device(): step = lambda x: lax.ppermute(x, 'expert', ring)]
    ppermute x33 -> x26, waiting for transfers between devices: 48 us -> 44.8 us  [on_device(): step = lambda x: lax.ppermute(x, 'expert', ring)]
    pallas_call x15 -> x34, Pallas kernels: 5.08 us -> 7.46 us  [the longest x14 5 us: combine(): call(functools.partial(combine_body, k, mine[k][1], most, chips, start, s...]
    unnamed x29 -> x68, local copies, waits for them, and re-layouts: 3.87 us -> 5.75 us
    ppermute x20 -> x14, starting transfers between devices: 3.75 us -> 2.58 us  [on_device(): lax.ppermute(x, 'expert', [(i, i ^ 1) for i in range(owners)])]
  transfers between devices with their start and end apart: 57 -> 44, of which waited for: 26 -> 24; matrix products, arithmetic and copies ran while one was open for 2% -> 1% of each run, Pallas kernels for 17% -> 18%
where the time goes in v4:
time: 164 us; the launch traced here: 163 us
  waiting for transfers between devices  60.6 us (37%)
  starting transfers between devices  57.2 us (35%)
  Pallas kernels  38.2 us (23%)
  local copies, waits for them, and re-layouts  6.6 us (4%)
    ppermute x26, starting transfers between devices, on_device(): step = lambda x: lax.ppermute(x, 'expert', ring)  46.9 us
    ppermute x26, waiting for transfers between devices, on_device(): step = lambda x: lax.ppermute(x, 'expert', ring)  44.8 us
    pallas_call x4, Pallas kernels, expert(): call(functools.partial(expert_body, ks, most, chips), (shape((len(ks), mo...  15.5 us
    ppermute x2, waiting for transfers between devices, on_device(): cross = lambda x: lax.ppermute(x, ('pipe', 'expert'), last)  12.4 us
    unnamed x68, local copies, waits for them, and re-layouts  5.75 us
    pallas_call x1, Pallas kernels, on_device(): call(functools.partial(attend_body, most, chips, 4, groups), (shape((owne...  5.47 us
    pallas_call x2, Pallas kernels, on_device(): call(functools.partial(arrive_body, packs, most, chips), tuple((shape((le...  5.31 us
    pallas_call x14, Pallas kernels, combine(): call(functools.partial(combine_body, k, mine[k][1], most, chips, start, s...  5 us
  transfers between devices with their start and end apart: 44, of which 24 were waited for; matrix products, arithmetic and copies ran while one was open for 1% of the time, Pallas kernels for 18%

profile of v4, /device:TPU:0, one launch (start us, length us, event | category | flops | bytes accessed | tf_op | source)
XLA Modules:
  0.0 163.2 jit_solution(9752849335655570726)
XLA Ops:
  5.0 3.1 %collective-permute-start = (bf16[816,256]{1,0:T(8,128)(2,1)S(1)}, bf16[816,256]{1,0:T(8,128)(2,1)S(1)}, u32[]{:S(2)}, u32[]{:S(2)}) collective-permute-start(bf16[816,256]{1,0:T(8,128)(2,1)S(1)} %get-tuple-element.56.piece.refs_6_), channel_id=1, source_target_pairs={{0,4},{1,3},{4,8},{5,1},{8,12},{9,5},{12,14},{13,9},{14,10},{15,13... | collective-permute-start | bytes 1253384 | tf_op jit(solution)/shard_map/ppermute | solution.py:278
  10.4 3.6 %collective-permute-done.piece.refs_0_ = bf16[816,256]{1,0:T(8,128)(2,1)S(1)} collective-permute-done((bf16[816,256]{1,0:T(8,128)(2,1)S(1)}, bf16[816,256]{1,0:T(8,128)(2,1)S(1)}, u32[]{:S(2)}, u32[]{:S(2)}) %collective-permute-start) | collective-permute-done | bytes 417824 | tf_op jit(solution)/shard_map/ppermute | solution.py:278
  16.1 2.3 %collective-permute-done.2.piece.refs_1_ = bf16[80,2560]{1,0:T(8,128)(2,1)S(1)} collective-permute-done((bf16[80,2560]{1,0:T(8,128)(2,1)S(1)}, bf16[80,2560]{1,0:T(8,128)(2,1)S(1)}, u32[]{:S(2)}, u32[]{:S(2)}) %collective-permute-start.2) | collective-permute-done | bytes 409632 | tf_op jit(solution)/shard_map/ppermute | solution.py:278
  20.5 2.4 %collective-permute-done.1.piece.refs_2_ = bf16[816,256]{1,0:T(8,128)(2,1)S(1)} collective-permute-done((bf16[816,256]{1,0:T(8,128)(2,1)S(1)}, bf16[816,256]{1,0:T(8,128)(2,1)S(1)}, u32[]{:S(2)}, u32[]{:S(2)}) %collective-permute-start.1) | collective-permute-done | bytes 417824 | tf_op jit(solution)/shard_map/ppermute | solution.py:278
  25.0 2.3 %collective-permute-done.4.piece.refs_3_ = bf16[80,2560]{1,0:T(8,128)(2,1)S(1)} collective-permute-done((bf16[80,2560]{1,0:T(8,128)(2,1)S(1)}, bf16[80,2560]{1,0:T(8,128)(2,1)S(1)}, u32[]{:S(2)}, u32[]{:S(2)}) %collective-permute-start.4) | collective-permute-done | bytes 409632 | tf_op jit(solution)/shard_map/ppermute | solution.py:278
  29.4 2.4 %collective-permute-done.3.piece.refs_4_ = bf16[816,256]{1,0:T(8,128)(2,1)S(1)} collective-permute-done((bf16[816,256]{1,0:T(8,128)(2,1)S(1)}, bf16[816,256]{1,0:T(8,128)(2,1)S(1)}, u32[]{:S(2)}, u32[]{:S(2)}) %collective-permute-start.3) | collective-permute-done | bytes 417824 | tf_op jit(solution)/shard_map/ppermute | solution.py:278
  38.2 2.4 %collective-permute-done.5.piece.refs_8_ = bf16[816,256]{1,0:T(8,128)(2,1)S(1)} collective-permute-done((bf16[816,256]{1,0:T(8,128)(2,1)S(1)}, bf16[816,256]{1,0:T(8,128)(2,1)S(1)}, u32[]{:S(2)}, u32[]{:S(2)}) %collective-permute-start.5) | collective-permute-done | bytes 417824 | tf_op jit(solution)/shard_map/ppermute | solution.py:278
  42.7 2.3 %collective-permute-done.8.piece.refs_9_ = bf16[80,2560]{1,0:T(8,128)(2,1)S(1)} collective-permute-done((bf16[80,2560]{1,0:T(8,128)(2,1)S(1)}, bf16[80,2560]{1,0:T(8,128)(2,1)S(1)}, u32[]{:S(2)}, u32[]{:S(2)}) %collective-permute-start.8) | collective-permute-done | bytes 409632 | tf_op jit(solution)/shard_map/ppermute | solution.py:278
  47.1 2.4 %collective-permute-done.7.piece.refs_10_ = bf16[816,256]{1,0:T(8,128)(2,1)S(1)} collective-permute-done((bf16[816,256]{1,0:T(8,128)(2,1)S(1)}, bf16[816,256]{1,0:T(8,128)(2,1)S(1)}, u32[]{:S(2)}, u32[]{:S(2)}) %collective-permute-start.7) | collective-permute-done | bytes 417824 | tf_op jit(solution)/shard_map/ppermute | solution.py:278
  51.6 2.3 %collective-permute-done.10.piece.refs_11_ = bf16[80,2560]{1,0:T(8,128)(2,1)S(1)} collective-permute-done((bf16[80,2560]{1,0:T(8,128)(2,1)S(1)}, bf16[80,2560]{1,0:T(8,128)(2,1)S(1)}, u32[]{:S(2)}, u32[]{:S(2)}) %collective-permute-start.10) | collective-permute-done | bytes 409632 | tf_op jit(solution)/shard_map/ppermute | solution.py:278
  56.0 2.4 %collective-permute-done.9.piece.refs_12_ = bf16[816,256]{1,0:T(8,128)(2,1)S(1)} collective-permute-done((bf16[816,256]{1,0:T(8,128)(2,1)S(1)}, bf16[816,256]{1,0:T(8,128)(2,1)S(1)}, u32[]{:S(2)}, u32[]{:S(2)}) %collective-permute-start.9) | collective-permute-done | bytes 417824 | tf_op jit(solution)/shard_map/ppermute | solution.py:278
  60.5 2.3 %collective-permute-done.12.piece.refs_13_ = bf16[80,2560]{1,0:T(8,128)(2,1)} collective-permute-done((bf16[80,2560]{1,0:T(8,128)(2,1)S(1)}, bf16[80,2560]{1,0:T(8,128)(2,1)}, u32[]{:S(2)}, u32[]{:S(2)}) %collective-permute-start.12) | collective-permute-done | bytes 409632 | tf_op jit(solution)/shard_map/ppermute | solution.py:278
  68.2 3.9 %collective-permute-done.15.piece.refs_1_ = bf16[80,2560]{1,0:T(8,128)(2,1)} collective-permute-done((bf16[80,2560]{1,0:T(8,128)(2,1)}, bf16[80,2560]{1,0:T(8,128)(2,1)}, u32[]{:S(2)}, u32[]{:S(2)}) %collective-permute-start.15) | collective-permute-done | bytes 409632 | tf_op jit(solution)/shard_map/ppermute | solution.py:278
  72.9 3.7 %shard_map.130 = (bf16[2,64,2560]{2,1,0:T(8,128)(2,1)S(1)}, bf16[2,64,2560]{2,1,0:T(8,128)(2,1)S(1)}, bf16[2,64,2560]{2,1,0:T(8,128)(2,1)S(1)}, bf16[2,64,2560]{...) custom-call(f32[40,256]{1,0:T(8,128)S(1)} %get-tuple-element.99.meta, ...), custom_call_target="tpu_custom_call" | custom-call | flops 99999997952 | bytes 1000000000 | tf_op jit(solution)/shard_map/pallas_call | solution.py:341
  80.7 5.5 %shard_map.132 = (bf16[1024,256]{1,0:T(8,128)(2,1)S(1)}, bf16[2048,256]{1,0:T(8,128)(2,1)S(1)}) custom-call(s32[4,16]{1,0:T(4,128)S(1)} %dynamic-slice_bitcast_fusion.ids, s32[1,256]{1,0:T(1,128)S(1)} %add.31.order, f32[40,256]{1,0:T(8,128)S(1)} %get-tuple-element.99.meta, bf16[256,256]{1,0:T(8,128)(2,1)S(1)} %bitcast.20, ...), custom_call_target="tpu_custom_call" | custom-call | flops 99999997952 | bytes 1000000000 | tf_op jit(solution)/shard_map/pallas_call | solution.py:356
  86.2 3.9 %shard_map.133 = (bf16[2,64,2560]{2,1,0:T(8,128)(2,1)S(1)}, bf16[2,64,2560]{2,1,0:T(8,128)(2,1)S(1)}) custom-call(f32[40,256]{1,0:T(8,128)S(1)} %get-tuple-element.99.meta, bf16[1024,256]{1,0:T(8,128)(2,1)S(1)} %get-tuple-element.77.att, bf16[128,2560]{1,0:T(8,128)(2,1)S(1)} %bitcast.15, bf16[128,2560]{1,0:T(8,128)(2,1)S(1)} %collective-permute-done.16.out_b, ...), custom_call_target="tpu_custom_call" | custom-call | flops 10000000000 | bytes 100000000 | tf_op jit(solution)/shard_map/pallas_call | solution.py:371
  97.0 3.9 %shard_map.138 = (bf16[2,64,2560]{2,1,0:T(8,128)(2,1)S(1)}, bf16[2,64,2560]{2,1,0:T(8,128)(2,1)S(1)}) custom-call(f32[40,256]{1,0:T(8,128)S(1)} %get-tuple-element.99.meta, bf16[1024,256]{1,0:T(8,128)(2,1)S(1)} %get-tuple-element.77.att, bf16[128,2560]{1,0:T(8,128)(2,1)S(1)} %bitcast.16, bf16[128,2560]{1,0:T(8,128)(2,1)S(1)} %collective-permute-done.16.out_b, ...), custom_call_target="tpu_custom_call" | custom-call | flops 10000000000 | bytes 100000000 | tf_op jit(solution)/shard_map/pallas_call | solution.py:371
  102.9 3.9 %shard_map.142 = (bf16[2,64,2560]{2,1,0:T(8,128)(2,1)S(1)}, bf16[2,64,2560]{2,1,0:T(8,128)(2,1)S(1)}) custom-call(f32[40,256]{1,0:T(8,128)S(1)} %get-tuple-element.99.meta, bf16[1024,256]{1,0:T(8,128)(2,1)S(1)} %get-tuple-element.77.att, bf16[128,2560]{1,0:T(8,128)(2,1)S(1)} %bitcast.17, bf16[128,2560]{1,0:T(8,128)(2,1)S(1)} %collective-permute-done.16.out_b, ...), custom_call_target="tpu_custom_call" | custom-call | flops 10000000000 | bytes 100000000 | tf_op jit(solution)/shard_map/pallas_call | solution.py:371
  108.9 2.8 %shard_map.139 = (bf16[128,1280]{1,0:T(8,128)(2,1)S(1)}, bf16[128,1280]{1,0:T(8,128)(2,1)S(1)}) custom-call(s32[4,16]{1,0:T(4,128)S(1)} %dynamic-slice_bitcast_fusion.ids, s32[1,256]{1,0:T(1,128)S(1)} %add.31.order, f32[40,256]{1,0:T(8,128)S(1)} %get-tuple-element.99.meta, bf16[256,256]{1,0:T(8,128)(2,1)S(1)} %bitcast.21, bf16[128,2560]{1,0:T(8,128)(2,1)S(1)} %bitcast.18, ...), custom_call_target="tpu_custom_call" | custom-call | tf_op jit(solution)/shard_map/pallas_call | solution.py:406
  120.6 3.9 %shard_map.141 = (bf16[2,64,2560]{2,1,0:T(8,128)(2,1)S(1)}, bf16[2,64,2560]{2,1,0:T(8,128)(2,1)S(1)}) custom-call(f32[40,256]{1,0:T(8,128)S(1)} %get-tuple-element.99.meta, bf16[1024,256]{1,0:T(8,128)(2,1)S(1)} %get-tuple-element.77.att, bf16[128,2560]{1,0:T(8,128)(2,1)S(1)} %bitcast.19, bf16[128,2560]{1,0:T(8,128)(2,1)S(1)} %collective-permute-done.16.out_b, ...), custom_call_target="tpu_custom_call" | custom-call | flops 10000000000 | bytes 100000000 | tf_op jit(solution)/shard_map/pallas_call | solution.py:371
  128.9 3.2 %collective-permute-done.40.refs_0_ = bf16[128,1280]{1,0:T(8,128)(2,1)S(1)} collective-permute-done((bf16[128,1280]{1,0:T(8,128)(2,1)S(1)}, bf16[128,1280]{1,0:T(8,128)(2,1)S(1)}, u32[]{:S(2)}, u32[]{:S(2)}) %collective-permute-start.40) | collective-permute-done | bytes 327712 | tf_op jit(solution)/shard_map/ppermute | solution.py:278
  147.4 2.5 %collective-permute-start.43 = (bf16[128,1280]{1,0:T(8,128)(2,1)S(1)}, bf16[128,1280]{1,0:T(8,128)(2,1)S(1)}, u32[]{:S(2)}, u32[]{:S(2)}) collective-permute-start(bf16[128,1280]{1,0:T(8,128)(2,1)S(1)} %shard_map.151), channel_id=1, source_target_pairs={{0,20},{1,19},{4,24},{5,17},{8,28},{9,21},{12,30},{13,25},{14,26},... | collective-permute-start | bytes 983048 | tf_op jit(solution)/shard_map/ppermute | solution.py:394
  149.9 8.8 %collective-permute-done.37.refs_1_ = bf16[128,1280]{1,0:T(8,128)(2,1)S(1)} collective-permute-done((bf16[128,1280]{1,0:T(8,128)(2,1)S(1)}, bf16[128,1280]{1,0:T(8,128)(2,1)S(1)}, u32[]{:S(2)}, u32[]{:S(2)}) %collective-permute-start.37) | collective-permute-done | bytes 327712 | tf_op jit(solution)/shard_map/ppermute | solution.py:394
  158.8 3.5 %collective-permute-done.43.refs_3_ = bf16[128,1280]{1,0:T(8,128)(2,1)S(1)} collective-permute-done((bf16[128,1280]{1,0:T(8,128)(2,1)S(1)}, bf16[128,1280]{1,0:T(8,128)(2,1)S(1)}, u32[]{:S(2)}, u32[]{:S(2)}) %collective-permute-start.43) | collective-permute-done | bytes 327712 | tf_op jit(solution)/shard_map/ppermute | solution.py:394
  (182 shorter events, 83.1 us)
Async XLA Ops:
  5.0 9.0 %collective-permute-start = (bf16[816,256]{1,0:T(8,128)(2,1)S(1)}, bf16[816,256]{1,0:T(8,128)(2,1)S(1)}, u32[]{:S(2)}, u32[]{:S(2)}) collective-permute-start(bf16[816,256]{1,0:T(8,128)(2,1)S(1)} %get-tuple-element.56.piece.refs_6_), channel_id=1, source_target_pairs={{0,4},{1,3},{4,8},{5,1},{8,12},{9,5},{12,14},{13,9},{14,10},{15,13... | collective-permute-start | bytes 1253384 | tf_op jit(solution)/shard_map/ppermute | solution.py:278
  8.1 10.3 %collective-permute-start.2 = (bf16[80,2560]{1,0:T(8,128)(2,1)S(1)}, bf16[80,2560]{1,0:T(8,128)(2,1)S(1)}, u32[]{:S(2)}, u32[]{:S(2)}) collective-permute-start(bf16[80,2560]{1,0:T(8,128)(2,1)S(1)} %get-tuple-element.58.piece.refs_7_), channel_id=1, source_target_pairs={{0,4},{1,3},{4,8},{5,1},{8,12},{9,5},{12,14},{13,9},{14,10},{15,13... | collective-permute-start | bytes 1228808 | tf_op jit(solution)/shard_map/ppermute | solution.py:278
  14.0 8.9 %collective-permute-start.1 = (bf16[816,256]{1,0:T(8,128)(2,1)S(1)}, bf16[816,256]{1,0:T(8,128)(2,1)S(1)}, u32[]{:S(2)}, u32[]{:S(2)}) collective-permute-start(bf16[816,256]{1,0:T(8,128)(2,1)S(1)} %collective-permute-done.piece.refs_0_), channel_id=1, source_target_pairs={{0,4},{1,3},{4,8},{5,1},{8,12},{9,5},{12,14},{13,9},{14,10},{15,13... | collective-permute-start | bytes 1253384 | tf_op jit(solution)/shard_map/ppermute | solution.py:278
  18.4 8.9 %collective-permute-start.4 = (bf16[80,2560]{1,0:T(8,128)(2,1)S(1)}, bf16[80,2560]{1,0:T(8,128)(2,1)S(1)}, u32[]{:S(2)}, u32[]{:S(2)}) collective-permute-start(bf16[80,2560]{1,0:T(8,128)(2,1)S(1)} %collective-permute-done.2.piece.refs_1_), channel_id=1, source_target_pairs={{0,4},{1,3},{4,8},{5,1},{8,12},{9,5},{12,14},{13,9},{14,10},{15,13... | collective-permute-start | bytes 1228808 | tf_op jit(solution)/shard_map/ppermute | solution.py:278
  22.9 8.9 %collective-permute-start.3 = (bf16[816,256]{1,0:T(8,128)(2,1)S(1)}, bf16[816,256]{1,0:T(8,128)(2,1)S(1)}, u32[]{:S(2)}, u32[]{:S(2)}) collective-permute-start(bf16[816,256]{1,0:T(8,128)(2,1)S(1)} %collective-permute-done.1.piece.refs_2_), channel_id=1, source_target_pairs={{0,4},{1,3},{4,8},{5,1},{8,12},{9,5},{12,14},{13,9},{14,10},{15,13... | collective-permute-start | bytes 1253384 | tf_op jit(solution)/shard_map/ppermute | solution.py:278
  27.3 8.9 %collective-permute-start.6 = (bf16[80,2560]{1,0:T(8,128)(2,1)S(1)}, bf16[80,2560]{1,0:T(8,128)(2,1)S(1)}, u32[]{:S(2)}, u32[]{:S(2)}) collective-permute-start(bf16[80,2560]{1,0:T(8,128)(2,1)S(1)} %collective-permute-done.4.piece.refs_3_), channel_id=1, source_target_pairs={{0,4},{1,3},{4,8},{5,1},{8,12},{9,5},{12,14},{13,9},{14,10},{15,13... | collective-permute-start | bytes 1228808 | tf_op jit(solution)/shard_map/ppermute | solution.py:278
  31.7 8.9 %collective-permute-start.5 = (bf16[816,256]{1,0:T(8,128)(2,1)S(1)}, bf16[816,256]{1,0:T(8,128)(2,1)S(1)}, u32[]{:S(2)}, u32[]{:S(2)}) collective-permute-start(bf16[816,256]{1,0:T(8,128)(2,1)S(1)} %collective-permute-done.3.piece.refs_4_), channel_id=1, source_target_pairs={{0,4},{1,3},{4,8},{5,1},{8,12},{9,5},{12,14},{13,9},{14,10},{15,13... | collective-permute-start | bytes 1253384 | tf_op jit(solution)/shard_map/ppermute | solution.py:278
  36.1 8.9 %collective-permute-start.8 = (bf16[80,2560]{1,0:T(8,128)(2,1)S(1)}, bf16[80,2560]{1,0:T(8,128)(2,1)S(1)}, u32[]{:S(2)}, u32[]{:S(2)}) collective-permute-start(bf16[80,2560]{1,0:T(8,128)(2,1)S(1)} %collective-permute-done.6.piece.refs_5_), channel_id=1, source_target_pairs={{0,4},{1,3},{4,8},{5,1},{8,12},{9,5},{12,14},{13,9},{14,10},{15,13... | collective-permute-start | bytes 1228808 | tf_op jit(solution)/shard_map/ppermute | solution.py:278
  40.6 8.9 %collective-permute-start.7 = (bf16[816,256]{1,0:T(8,128)(2,1)S(1)}, bf16[816,256]{1,0:T(8,128)(2,1)S(1)}, u32[]{:S(2)}, u32[]{:S(2)}) collective-permute-start(bf16[816,256]{1,0:T(8,128)(2,1)S(1)} %collective-permute-done.5.piece.refs_8_), channel_id=1, source_target_pairs={{0,4},{1,3},{4,8},{5,1},{8,12},{9,5},{12,14},{13,9},{14,10},{15,13... | collective-permute-start | bytes 1253384 | tf_op jit(solution)/shard_map/ppermute | solution.py:278
  45.0 8.9 %collective-permute-start.10 = (bf16[80,2560]{1,0:T(8,128)(2,1)S(1)}, bf16[80,2560]{1,0:T(8,128)(2,1)S(1)}, u32[]{:S(2)}, u32[]{:S(2)}) collective-permute-start(bf16[80,2560]{1,0:T(8,128)(2,1)S(1)} %collective-permute-done.8.piece.refs_9_), channel_id=1, source_target_pairs={{0,4},{1,3},{4,8},{5,1},{8,12},{9,5},{12,14},{13,9},{14,10},{15,13... | collective-permute-start | bytes 1228808 | tf_op jit(solution)/shard_map/ppermute | solution.py:278
  49.5 8.9 %collective-permute-start.9 = (bf16[816,256]{1,0:T(8,128)(2,1)S(1)}, bf16[816,256]{1,0:T(8,128)(2,1)S(1)}, u32[]{:S(2)}, u32[]{:S(2)}) collective-permute-start(bf16[816,256]{1,0:T(8,128)(2,1)S(1)} %collective-permute-done.7.piece.refs_10_), channel_id=1, source_target_pairs={{0,4},{1,3},{4,8},{5,1},{8,12},{9,5},{12,14},{13,9},{14,10},{15,13... | collective-permute-start | bytes 1253384 | tf_op jit(solution)/shard_map/ppermute | solution.py:278
  53.9 9.0 %collective-permute-start.12 = (bf16[80,2560]{1,0:T(8,128)(2,1)S(1)}, bf16[80,2560]{1,0:T(8,128)(2,1)}, u32[]{:S(2)}, u32[]{:S(2)}) collective-permute-start(bf16[80,2560]{1,0:T(8,128)(2,1)S(1)} %collective-permute-done.10.piece.refs_11_), channel_id=1, source_target_pairs={{0,4},{1,3},{4,8},{5,1},{8,12},{9,5},{12,14},{13,9},{14,10},{15,13... | collective-permute-start | bytes 1228808 | tf_op jit(solution)/shard_map/ppermute | solution.py:278
  58.3 8.9 %collective-permute-start.11 = (bf16[816,256]{1,0:T(8,128)(2,1)S(1)}, bf16[816,256]{1,0:T(8,128)(2,1)S(1)}, u32[]{:S(2)}, u32[]{:S(2)}) collective-permute-start(bf16[816,256]{1,0:T(8,128)(2,1)S(1)} %collective-permute-done.9.piece.refs_12_), channel_id=1, source_target_pairs={{0,4},{1,3},{4,8},{5,1},{8,12},{9,5},{12,14},{13,9},{14,10},{15,13... | collective-permute-start | bytes 1253384 | tf_op jit(solution)/shard_map/ppermute | solution.py:278
  62.8 9.3 %collective-permute-start.13 = (bf16[7,176,256]{2,1,0:T(8,128)(2,1)S(1)}, bf16[7,176,256]{2,1,0:T(8,128)(2,1)S(1)}, u32[]{:S(2)}, u32[]{:S(2)}) collective-permute-start(bf16[7,176,256]{2,1,0:T(8,128)(2,1)S(1)} %shard_map.123.refs_0_), channel_id=1, source_target_pairs={{0,1},{1,0},{2,3},{3,2},{4,5},{5,4},{6,7},{7,6},{8,9},{9,8},{10,11... | collective-permute-start | bytes 1892360 | tf_op jit(solution)/shard_map/ppermute | solution.py:279
  90.7 12.2 %collective-permute-start.30 = (bf16[2,64,2560]{2,1,0:T(8,128)(2,1)S(1)}, bf16[2,64,2560]{2,1,0:T(8,128)(2,1)S(1)}, u32[]{:S(2)}, u32[]{:S(2)}) collective-permute-start(bf16[2,64,2560]{2,1,0:T(8,128)(2,1)S(1)} %get-tuple-element.101), channel_id=1, source_target_pairs={{0,1},{1,0},{2,3},{3,2},{4,5},{5,4},{6,7},{7,6},{8,9},{9,8},{10,11... | collective-permute-start | bytes 1966088 | tf_op jit(solution)/shard_map/ppermute | solution.py:279
  95.2 11.8 %collective-permute-start.22 = (bf16[128,1280]{1,0:T(8,128)(2,1)S(1)}, bf16[128,1280]{1,0:T(8,128)(2,1)S(1)}, u32[]{:S(2)}, u32[]{:S(2)}) collective-permute-start(bf16[128,1280]{1,0:T(8,128)(2,1)S(1)} %shard_map.136), channel_id=1, source_target_pairs={{0,4},{1,3},{4,8},{5,1},{8,12},{9,5},{12,14},{13,9},{14,10},{15,13... | collective-permute-start | bytes 983048 | tf_op jit(solution)/shard_map/ppermute | solution.py:278
  101.3 10.4 %collective-permute-start.26 = (bf16[128,1280]{1,0:T(8,128)(2,1)S(1)}, bf16[128,1280]{1,0:T(8,128)(2,1)S(1)}, u32[]{:S(2)}, u32[]{:S(2)}) collective-permute-start(bf16[128,1280]{1,0:T(8,128)(2,1)S(1)} %shard_map.135), channel_id=1, source_target_pairs={{0,4},{1,3},{4,8},{5,1},{8,12},{9,5},{12,14},{13,9},{14,10},{15,13... | collective-permute-start | bytes 983048 | tf_op jit(solution)/shard_map/ppermute | solution.py:278
  106.8 9.4 %collective-permute-start.31 = (bf16[2,64,2560]{2,1,0:T(8,128)(2,1)S(1)}, bf16[2,64,2560]{2,1,0:T(8,128)(2,1)S(1)}, u32[]{:S(2)}, u32[]{:S(2)}) collective-permute-start(bf16[2,64,2560]{2,1,0:T(8,128)(2,1)S(1)} %get-tuple-element.103), channel_id=1, source_target_pairs={{0,1},{1,0},{2,3},{3,2},{4,5},{5,4},{6,7},{7,6},{8,9},{9,8},{10,11... | collective-permute-start | bytes 1966088 | tf_op jit(solution)/shard_map/ppermute | solution.py:279
  114.4 13.6 %collective-permute-start.25 = (bf16[128,1280]{1,0:T(8,128)(2,1)S(1)}, bf16[128,1280]{1,0:T(8,128)(2,1)S(1)}, u32[]{:S(2)}, u32[]{:S(2)}) collective-permute-start(bf16[128,1280]{1,0:T(8,128)(2,1)S(1)} %get-tuple-element.89), channel_id=1, source_target_pairs={{0,16},{16,0},{1,17},{17,1},{2,18},{18,2},{3,19},{19,3},{4,20},{20... | collective-permute-start | bytes 983048 | tf_op jit(solution)/shard_map/ppermute | solution.py:283
  119.5 8.5 %collective-permute-start.33 = (bf16[128,1280]{1,0:T(8,128)(2,1)S(1)}, bf16[128,1280]{1,0:T(8,128)(2,1)S(1)}, u32[]{:S(2)}, u32[]{:S(2)}) collective-permute-start(bf16[128,1280]{1,0:T(8,128)(2,1)S(1)} %shard_map.143), channel_id=1, source_target_pairs={{0,4},{1,3},{4,8},{5,1},{8,12},{9,5},{12,14},{13,9},{14,10},{15,13... | collective-permute-start | bytes 983048 | tf_op jit(solution)/shard_map/ppermute | solution.py:278
  124.5 11.4 %collective-permute-start.29 = (bf16[2,64,2560]{2,1,0:T(8,128)(2,1)S(1)}, bf16[2,64,2560]{2,1,0:T(8,128)(2,1)S(1)}, u32[]{:S(2)}, u32[]{:S(2)}) collective-permute-start(bf16[2,64,2560]{2,1,0:T(8,128)(2,1)S(1)} %get-tuple-element.98), channel_id=1, source_target_pairs={{0,1},{1,0},{2,3},{3,2},{4,5},{5,4},{6,7},{7,6},{8,9},{9,8},{10,11... | collective-permute-start | bytes 1966088 | tf_op jit(solution)/shard_map/ppermute | solution.py:279
  126.5 9.3 %collective-permute-start.35 = (bf16[128,1280]{1,0:T(8,128)(2,1)S(1)}, bf16[128,1280]{1,0:T(8,128)(2,1)S(1)}, u32[]{:S(2)}, u32[]{:S(2)}) collective-permute-start(bf16[128,1280]{1,0:T(8,128)(2,1)S(1)} %get-tuple-element.90), channel_id=1, source_target_pairs={{0,16},{16,0},{1,17},{17,1},{2,18},{18,2},{3,19},{19,3},{4,20},{20... | collective-permute-start | bytes 983048 | tf_op jit(solution)/shard_map/ppermute | solution.py:283
  143.7 15.0 %collective-permute-start.37 = (bf16[128,1280]{1,0:T(8,128)(2,1)S(1)}, bf16[128,1280]{1,0:T(8,128)(2,1)S(1)}, u32[]{:S(2)}, u32[]{:S(2)}) collective-permute-start(bf16[128,1280]{1,0:T(8,128)(2,1)S(1)} %shard_map.146), channel_id=1, source_target_pairs={{0,20},{1,19},{4,24},{5,17},{8,28},{9,21},{12,30},{13,25},{14,26},... | collective-permute-start | bytes 983048 | tf_op jit(solution)/shard_map/ppermute | solution.py:394
  147.4 14.9 %collective-permute-start.43 = (bf16[128,1280]{1,0:T(8,128)(2,1)S(1)}, bf16[128,1280]{1,0:T(8,128)(2,1)S(1)}, u32[]{:S(2)}, u32[]{:S(2)}) collective-permute-start(bf16[128,1280]{1,0:T(8,128)(2,1)S(1)} %shard_map.151), channel_id=1, source_target_pairs={{0,20},{1,19},{4,24},{5,17},{8,28},{9,21},{12,30},{13,25},{14,26},... | collective-permute-start | bytes 983048 | tf_op jit(solution)/shard_map/ppermute | solution.py:394
  (54 other events, 240.6 us)

commit v5 on v4

--- a/solution.py
+++ b/solution.py
@@ -13,7 +13,7 @@
 VMEM = pl.BlockSpec(memory_space=pltpu.VMEM)
 SMEM = pl.BlockSpec(memory_space=pltpu.SMEM)
 MIB = 1024 * 1024
-LONG = 10**11
+LONG = 10**10
 SHORT = 3 * 10**9
 
 
@@ -23,7 +23,7 @@
     return 2 * place if place < half else 2 * (chips - 1 - place) + 1
 
 
-def call(body, outs, ins, limit=12, flops=0, moved=None):
+def call(body, outs, ins, limit=8, flops=0, moved=None):
     return pl.pallas_call(
         body,
         out_shape=outs,
@@ -53,15 +53,43 @@
     return jnp.where(ids == row, 1.0, 0.0)
 
 
-def pack_body(tokens, routes, gates, capacity, down, out, first, second):
+def blocks_of(x, out, first, latent):
+    size = x.shape[0]
+    for j in range(x.shape[1] // latent):
+        out[first + j * size : first + (j + 1) * size, :] = x[:, j * latent : (j + 1) * latent]
+
+
+def joined(piece, first, size, count):
+    return jnp.concatenate(
+        [piece[first + j * size : first + (j + 1) * size, :] for j in range(count)], 1
+    )
+
+
+def pack_weights_body(down, out, weights):
+    weights[0 : down.shape[0], :] = down[...]
+    blocks_of(out[...], weights, down.shape[0], down.shape[1])
+
+
+def pack_first_body(tokens, weights, first):
+    latent = weights.shape[1]
+    blocks_of(tokens[0 : tokens.shape[0] // 2, :], first, 0, latent)
+    first[first.shape[0] - weights.shape[0] :, :] = weights[...]
+
+
+def head_body(piece, out):
+    out[...] = piece[0 : out.shape[0], :]
+
+
+def last_body(piece, out):
+    out[...] = piece[piece.shape[0] - out.shape[0] :, :]
+
+
+def pack_second_body(tokens, routes, gates, capacity, second):
     top, _, rows = routes.shape
     experts = capacity.shape[1]
-    latent = down.shape[1]
     half = rows // 2
-    for j in range(tokens.shape[1] // latent):
-        first[j * half : (j + 1) * half, :] = tokens[0:half, j * latent : (j + 1) * latent]
-    second[0:half, :] = tokens[half:rows, :]
-    second[half : half + out.shape[0], :] = out[...]
+    latent = second.shape[1]
+    blocks_of(tokens[half:rows, :], second, 0, latent)
     expert = lax.broadcasted_iota(jnp.int32, (experts, rows), 0)
     named = jnp.zeros((experts, rows), F32)
     gate = jnp.zeros((experts, rows), F32)
@@ -76,15 +104,16 @@
     col = lax.broadcasted_iota(jnp.int32, (experts, experts), 1)
     limit = jnp.sum(jnp.where(row == col, capacity[...].astype(F32), 0.0), 1, keepdims=True)
     kept = (named > 0.5) & (rank < limit)
-    start = tokens.shape[1] // latent * half
-    first[start : start + down.shape[0], :] = down[...]
-    start += down.shape[0]
-    first[start : start + experts, 0:rows] = jnp.where(kept, rank, -1.0).astype(BF)
-    first[start : start + experts, rows : 2 * rows] = jnp.where(kept, gate, 0.0).astype(BF)
-
-
-def tail_body(piece, out):
-    out[...] = piece[piece.shape[0] - out.shape[0] :, :]
+    start = half * (tokens.shape[1] // latent)
+    second[start : start + experts, 0:rows] = jnp.where(kept, rank, -1.0).astype(BF)
+    second[start : start + experts, rows : 2 * rows] = jnp.where(kept, gate, 0.0).astype(BF)
+
+
+def tail_body(piece, down, out):
+    count = out.shape[1] // piece.shape[1]
+    end = piece.shape[0] - out.shape[0] * count
+    down[...] = piece[end - down.shape[0] : end, :]
+    out[...] = joined(piece, end, out.shape[0], count)
 
 
 def stack_body(*refs):
@@ -93,50 +122,74 @@
         out[i] = piece[...]
 
 
-def unpack_body(depth, ids, *refs):
-    arrays, (down, meta) = refs[:-2], refs[-2:]
+def unpack_body(ids, *refs):
+    arrays, down = refs[:-1], refs[-1]
     halves = [ref.at[i] for ref in arrays for i in range(ref.shape[0])]
     chips = len(halves) // 2
-    tall, wide = halves[0].shape
-    experts = tall - depth
-    row = lax.broadcasted_iota(jnp.int32, (experts, wide), 0)
+    depth = halves[0].shape[0]
     for i, half in enumerate(halves):
         side, k = divmod(i, chips)
-        block = ids[side, k]
-        down[pl.ds(pl.multiple_of(block * depth, 16), depth), :] = half[0:depth, :]
-        table = half[depth:tall, :].astype(F32)
+        down[pl.ds(pl.multiple_of(ids[side, k] * depth, 16), depth), :] = half[...]
+
+
+def table_body(ids, *refs):
+    arrays, meta = refs[:-1], refs[-1]
+    halves = [ref.at[i] for ref in arrays for i in range(ref.shape[0])]
+    chips = len(halves) // 2
+    row = lax.broadcasted_iota(jnp.int32, halves[0].shape, 0)
+    for i, half in enumerate(halves):
+        side, k = divmod(i, chips)
+        table = half[...].astype(F32)
         own = jnp.sum(jnp.where(row == ids[2, 0], table, 0.0), 0, keepdims=True)
         meta[i : i + 1, :] = own
-        meta[pl.ds(3 * chips + block, 1), :] = own
+        meta[pl.ds(3 * chips + ids[side, k], 1), :] = own
         if side == 0:
             meta[2 * chips + k : 2 * chips + k + 1, :] = jnp.sum(
                 jnp.where(row == ids[2, 1], table, 0.0), 0, keepdims=True
             )
 
 
-def arrive_body(packs, most, chips, meta, down, gain, *refs):
-    count = sum(len(ks) for ks in packs)
-    pieces, outs = refs[: 2 * count], refs[2 * count :]
-    latents = outs[-1]
+def whole(one, two, rows, count):
+    half = rows // 2
+    return jnp.concatenate([joined(one, 0, half, count), joined(two, 0, half, count)], 0)
+
+
+def choose_body(most, ids, small, one, two, *refs):
+    lines, (own, other) = refs[:-2], refs[-2:]
+    latent = two.shape[1]
+    rows = latent // 2
+    table = small[...].astype(F32)
+    row = lax.broadcasted_iota(jnp.int32, (small.shape[0], rows), 0)
+    picks = []
+    for which in (0, 1):
+        mine = jnp.where(row == ids[2, which], table[:, 0:rows], 0.0)
+        picks.append(slots_of(jnp.sum(mine, 0, keepdims=True), most))
+    tokens = whole(one, two, rows, own.shape[1] // latent)
+    chosen = dot(jnp.concatenate(picks, 0).astype(BF), tokens)
+    own[...] = chosen[:most].astype(BF)
+    other[0:most, :] = chosen[most:].astype(BF)
+    start = most
+    for line in lines:
+        other[start : start + line.shape[0], :] = line[...]
+        start += line.shape[0]
+
+
+def gate_up_body(count, gate_up, *refs):
+    result = dot(jnp.concatenate([ref[...] for ref in refs[:count]], 0), gate_up[...]).astype(BF)
+    start = 0
+    for out in refs[count:]:
+        out[...] = result[start : start + out.shape[0]]
+        start += out.shape[0]
+
+
+def latent_body(down, gain, *refs):
+    pieces, latents = refs[:-1], refs[-1]
     rows, latent = latents.shape[1:]
-    half = rows // 2
-    at = 0
-    for g, ks in enumerate(packs):
-        for i, k in enumerate(ks):
-            one, two = pieces[2 * at], pieces[2 * at + 1]
-            blocks = range(two.shape[1] // latent)
-            one = jnp.concatenate([one[j * half : (j + 1) * half, :] for j in blocks], 1)
-            x = jnp.concatenate([one, two[0:half, :]], 0)
-            pick = jnp.concatenate(
-                [slots_of(meta[j : j + 1, 0:rows], most) for j in (k, 2 * chips + k)], 0
-            ).astype(BF)
-            chosen = dot(pick, x).astype(BF)
-            outs[2 * g][i] = chosen[:most]
-            outs[2 * g + 1][i] = chosen[most:]
-            raw = dot(x, down[...])
-            scale = lax.rsqrt(jnp.mean(raw * raw, -1, keepdims=True) + 1e-06)
-            latents[at] = (raw * scale * gain[...]).astype(BF)
-            at += 1
+    for i in range(latents.shape[0]):
+        x = whole(pieces[2 * i], pieces[2 * i + 1], rows, down.shape[0] // latent)
+        raw = dot(x, down[...])
+        scale = lax.rsqrt(jnp.mean(raw * raw, -1, keepdims=True) + 1e-06)
+        latents[i] = (raw * scale * gain[...]).astype(BF)
 
 
 def attend(rows, keys, masks, w_query):
@@ -152,7 +205,7 @@
 
 def reorder(attended, order):
     place = lax.broadcasted_iota(jnp.int32, (attended.shape[1], order.shape[1]), 0)
-    return dot(attended, jnp.where(place == order, 1.0, 0.0).astype(BF)).astype(BF)
+    return dot(attended, jnp.where(place == order[4:5, :], 1.0, 0.0).astype(BF)).astype(BF)
 
 
 def attend_body(most, chips, counts, packs, ids, order, meta, w_query, *refs):
@@ -185,11 +238,11 @@
             att[pl.ds(at, most), :] = attended[(b - first) * most : (b - first + 1) * most, :]
 
 
-def expert_body(ks, most, chips, meta, att, out_a, out_b, gate_up, expert_down, *refs):
-    chosen_refs, outs = refs[:-2], refs[-2:]
+def expert_body(ks, most, chips, meta, att, wide_a, wide_b, expert_down, *refs):
+    chosen, outs = refs[:-2], refs[-2:]
     rows = meta.shape[1] // 2
     hidden_width = expert_down.shape[0]
-    shard = out_a.shape[0]
+    shard = wide_a.shape[0]
     attended, gate = [], []
     for side in (0, 1):
         for k in ks:
@@ -197,11 +250,9 @@
             pick = slots_of(meta[at : at + 1, 0:rows], most)
             gate.append(jnp.sum(pick * meta[at : at + 1, rows : 2 * rows], -1, keepdims=True))
             attended.append(att[at * most : (at + 1) * most, :])
-    chosen = jnp.concatenate([ref[i] for ref in chosen_refs for i in range(ref.shape[0])], 0)
     attended = jnp.concatenate(attended, 0)
-    hidden = dot(attended[:, :shard], out_a[...]) + dot(attended[:, shard:], out_b[...])
-    hidden = (chosen.astype(F32) + hidden).astype(BF)
-    both = dot(hidden, gate_up[...])
+    both = dot(attended[:, :shard], wide_a[...]) + dot(attended[:, shard:], wide_b[...])
+    both = both + jnp.concatenate([ref[...] for ref in chosen], 0).astype(F32)
     inner = (jax.nn.silu(both[:, :hidden_width]) * both[:, hidden_width:]).astype(BF)
     result = (dot(inner, expert_down[...]) * jnp.concatenate(gate, 0)).astype(BF)
     for i in range(2 * len(ks)):
@@ -240,13 +291,14 @@
         first += out.shape[1]
 
 
-def final_body(*refs):
-    ins, out = refs[:-1], refs[-1]
-    first = 0
-    for one, two in zip(ins[0::2], ins[1::2], strict=True):
-        size = one.shape[1]
-        out[:, first : first + size] = (one[...].astype(F32) + two[...].astype(F32)).astype(BF)
-        first += size
+def add_body(one, two, out):
+    out[...] = (one[...].astype(F32) + two[...].astype(F32)).astype(BF)
+
+
+def final_body(first, one, two, out):
+    size = first.shape[1]
+    out[:, :size] = first[...]
+    out[:, size:] = (one[...].astype(F32) + two[...].astype(F32)).astype(BF)
 
 
 def after(x, *others):
@@ -288,93 +340,138 @@
         table[e, 0, :chips], table[e, 1, :chips] = blocks[e], blocks[e ^ 1]
         table[e, 2, :2] = (e, e ^ 1)
         table[e, 3, both] = np.arange(owners)
-    ids = lax.dynamic_index_in_dim(jnp.asarray(table), me, 0, keepdims=False)
     shard = w_out.shape[1]
-    order = (ids[:2, :chips].reshape(-1)[:, None] * shard + jnp.arange(shard)[None, :]).reshape(1, -1)
+    columns = table[:, :2, :chips].reshape(owners, owners, 1) * shard + np.arange(shard)
+    numbers = np.zeros((owners, 8, owners * shard), np.int32)
+    numbers[:, :4, :owners] = table
+    numbers[:, 4] = columns.reshape(owners, -1)
+    ids = lax.dynamic_slice(
+        jnp.asarray(numbers.reshape(owners * 8, -1)), (8 * me, 0), (8, owners * shard)
+    )
 
     half = rows // 2
-    tall = depth + owners
-    one, two = call(
-        pack_body,
-        (
-            shape((width // latent * half + tall, latent), BF),
-            shape((half + shard, width), BF),
-        ),
-        [VMEM] * 6,
-    )(
-        tokens[0],
-        routes.transpose(2, 0, 1),
-        gates.transpose(2, 0, 1),
-        capacity,
-        w_down_kv[0],
-        w_out[0],
-    )
-    def tail(x, rows, *others):
-        return call(tail_body, shape((rows, x.shape[1]), BF), [VMEM], flops=SHORT, moved=0)(
+    count = width // latent
+    gate_up, expert_down = w_gate_up[0, 0], w_expert_down[0, 0]
+
+    def weights_of(x):
+        return call(tail_body, (shape((depth, latent), BF), shape((shard, width), BF)), [VMEM])(x)
+
+    def routes_of(x, *others):
+        return call(last_body, shape((owners, latent), BF), [VMEM], flops=SHORT, moved=0)(
             after(x, *others)
         )
 
-    first, second = [one], [two]
-    small = [tail(one, tall)]
-    outs = [tail(two, shard, small[0])]
+    def choose(listed, first, second, lines, *others):
+        return call(
+            functools.partial(choose_body, most),
+            (shape((most, width), BF), shape((most + len(lines) * shard, width), BF)),
+            [SMEM] + [VMEM] * (3 + len(lines)),
+            flops=SHORT,
+            moved=0,
+        )(ids, after(listed, *others), first, second, *lines)
+
+    def project(own, lines, other):
+        parts = [own, *lines, other]
+        sizes = ([most] + [shard] * len(lines)) * 2
+        results = call(
+            functools.partial(gate_up_body, len(parts)),
+            tuple(shape((n, gate_up.shape[1]), BF) for n in sizes),
+            [VMEM] * (1 + len(parts)),
+        )(gate_up, *parts)
+        half = len(lines) + 1
+        wide.append((results[0], results[half]))
+        thin_a.extend(results[1:half])
+        thin_b.extend(results[half + 1 :])
+
+    block = half * count
+    weights = [
+        call(pack_weights_body, shape((depth + shard * count, latent), BF), [VMEM] * 2)(
+            w_down_kv[0], w_out[0]
+        )
+    ]
+    weights.append(step(weights[0]))
+    small = [weights_of(x) for x in weights]
+    second = [
+        call(pack_second_body, shape((block + owners, latent), BF), [VMEM] * 4)(
+            after(tokens[0], weights[0]),
+            routes.transpose(2, 0, 1),
+            gates.transpose(2, 0, 1),
+            capacity,
+        )
+    ]
+    first = [
+        call(pack_first_body, shape((block + depth + shard * count, latent), BF), [VMEM] * 2)(
+            after(tokens[0], second[0]), weights[1]
+        )
+    ]
+    listed = [routes_of(second[0])]
+    chosen = [choose(listed[0], first[0], second[0], [x[1] for x in small])]
+    other = [sibling(chosen[0][1])]
+    wide, thin_a, thin_b = [], [], []
     for k in range(1, chips):
-        first.append(step(after(first[-1], *outs[k - 2 : k - 1])))
-        second.append(step(after(second[-1], small[k - 1])))
-        small.append(tail(first[k], tall, outs[k - 1]))
-        outs.append(tail(second[k], shard, small[k]))
+        second.append(step(after(second[-1], *[x[0] for x in chosen[k - 2 : k - 1]])))
+        passed = first[-1]
+        if k == chips - 1:
+            passed = call(head_body, shape((block, latent), BF), [VMEM])(passed)
+        first.append(step(after(passed, listed[k - 1], *[x[0] for x in wide[k - 2 : k - 1]])))
+        listed.append(routes_of(second[k], chosen[k - 1][0]))
+        project(
+            after(chosen[k - 1][0], listed[k]),
+            [x[1] for x in (small[:2] if k == 1 else small[k:])],
+            other[k - 1],
+        )
+        if k < chips - 1:
+            small.append(weights_of(first[k]))
+            chosen.append(choose(listed[k], first[k], second[k], [small[-1][1]], wide[k - 1][0]))
+            other.append(sibling(chosen[k][1]))
     stack = lambda xs: call(stack_body, shape((len(xs), *xs[0].shape), BF), [VMEM] * len(xs))(*xs)
-    small = [stack(small[:-1]), stack(small[-1:])]
-    down, meta = call(
-        functools.partial(unpack_body, depth),
-        (shape((owners * depth, latent), BF), shape((5 * chips, 2 * rows), F32)),
-        [SMEM] + [VMEM] * 4,
-        flops=LONG,
-    )(ids, *small, *[sibling(x) for x in small])
-
-    chunks = [(1, 2), (3, 0)] + [(k, k + 1) for k in range(4, chips, 2)]
-    chosen = {}
-    lat_a, lat_b, groups = [], [], []
-    for whole in (range(chips - 1), (chips - 1,)):
-        packs = [tuple(k for k in ks if k in whole) for ks in chunks]
-        packs = [ks for ks in packs if ks]
-        flat = [k for ks in packs for k in ks]
-        *picked, lat = call(
-            functools.partial(arrive_body, packs, most, chips),
-            tuple(shape((len(ks), most, width), BF) for ks in packs for _ in (0, 1))
-            + (shape((len(flat), rows, latent), BF),),
-            [VMEM] * (3 + 2 * len(flat)),
-            flops=LONG,
-            limit=16,
-        )(meta, down, kv_gain, *[x for k in flat for x in (first[k], second[k])])
-        for i, ks in enumerate(packs):
-            chosen[ks] = (picked[2 * i], sibling(picked[2 * i + 1]))
+    parts = [stack([x[0] for x in part]) for part in (small[:-1], small[-1:])]
+    down = call(unpack_body, shape((owners * depth, latent), BF), [SMEM] + [VMEM] * 4)(
+        ids, *parts, *[sibling(x) for x in parts]
+    )
+    wide_a, wide_b = (stack(thin).reshape(-1, gate_up.shape[1]) for thin in (thin_a, thin_b))
+
+    lat_a, lat_b, groups = [], [], (tuple(range(chips - 1)), (chips - 1,))
+    for group in groups:
+        lat = call(
+            latent_body,
+            shape((len(group), rows, latent), BF),
+            [VMEM] * (2 + 2 * len(group)),
+            flops=0 if lat_a else 2 * SHORT,
+            moved=0,
+        )(
+            after(down, chosen[-1][0], *lat_a),
+            kv_gain,
+            *[x for k in group for x in (first[k], second[k])],
+        )
         lat_a.append(lat)
         lat_b.append(sibling(lat))
-        groups.append(tuple(flat))
-    out_a = stack(outs).reshape(-1, width)
-    out_b = sibling(out_a)
+    chosen.append(choose(listed[-1], first[-1], second[-1], [], lat_a[1]))
+    other.append(sibling(chosen[-1][1]))
+    parts = [stack(listed[:-1]), stack(listed[-1:])]
+    meta = call(table_body, shape((5 * chips, latent), F32), [SMEM] + [VMEM] * 4)(
+        ids, *parts, *[sibling(x) for x in parts]
+    )
     att, lat = call(
         functools.partial(attend_body, most, chips, 4, groups),
         (shape((owners * most, latent), BF), shape((owners * rows, latent), BF)),
         [SMEM] + [VMEM] * (3 + 4),
         flops=LONG,
-        limit=16,
-    )(ids, order, meta, w_query[0], *lat_a, *lat_b)
-
-    gate_up, expert_down = w_gate_up[0, 0], w_expert_down[0, 0]
+    )(ids, ids, meta, w_query[0], *lat_a, *lat_b)
+    out_a = stack([after(x[1], att) for x in small]).reshape(-1, width)
+    out_b = sibling(out_a)
+
+    chunks = [(1, 2), (3, 0)] + [(k, k + 1) for k in range(4, chips, 2)]
     mine, theirs = {}, {}
 
     def expert(ks, *waits):
-        packs = [part for part in chosen if set(part) <= set(ks)]
-        packs = [part for k in ks for part in packs if part[0] == k]
-        picked = [chosen[part][side] for side in (0, 1) for part in packs]
+        picked = [wide[k][side] for side in (0, 1) for k in ks]
         result, away = call(
             functools.partial(expert_body, ks, most, chips),
             (shape((len(ks), most, width), BF),) * 2,
-            [VMEM] * (6 + len(picked)),
+            [VMEM] * (5 + len(picked)),
             flops=LONG // 10,
-            limit=16,
-        )(after(meta, *waits), att, out_a, out_b, gate_up, expert_down, *picked)
+        )(after(meta, *waits), att, wide_a, wide_b, expert_down, *picked)
         back = sibling(away)
         for i, k in enumerate(ks):
             mine[k], theirs[k] = (result, i), back
@@ -383,33 +480,39 @@
     passing = [None] * len(pieces)
     expert(chunks[0])
     waiting = list(chunks[1:])
-    def combine(k, i, *more):
+    def combine(k, i, previous, *more):
         start, size = pieces[i]
         return call(
             functools.partial(combine_body, k, mine[k][1], most, chips, start, size),
             shape((rows, size), BF),
             [VMEM] * (3 + len(more)),
-        )(meta, mine[k][0], theirs[k], *more)
+            flops=2 * SHORT,
+            moved=0,
+        )(after(meta, *previous), mine[k][0], theirs[k], *more)
 
     cross = lambda x: lax.ppermute(x, ("pipe", "expert"), last)
+    done = []
     for k in range(1, chips):
         totals = []
         for i in range(len(pieces)):
             more = [] if k == 1 else [passing[i]]
             if i == 0 and chips - 3 <= k < chips - 1:
                 more = [after(more[0], kept[k - (chips - 3)])]
-            totals.append(combine(k, i, *more))
+            totals.append(combine(k, i, done[-1:], *more))
+            done.append(totals[i])
             passing[i] = (cross if k == chips - 1 else step)(totals[i])
-        if waiting and k + 3 >= waiting[0][0]:
+        if k == min(2, chips - 2):
+            project(after(chosen[-1][0], totals[0]), [], other[-1])
+        if waiting and k + 2 >= waiting[0][0]:
             expert(waiting.pop(0), totals[0])
-        if k == 2:
+        if k == 3:
             kept = call(
                 functools.partial(own_body, mine[0][1], most, chips),
                 tuple(shape((rows, size), BF) for _, size in pieces),
                 [SMEM] + [VMEM] * 9,
             )(
                 ids,
-                order,
+                ids,
                 meta,
                 w_query[0],
                 out_a,
@@ -421,8 +524,11 @@
             )
             passing = [after(x, *kept) for x in passing]
             kept = [onward(x) for x in kept]
-    output = call(final_body, shape((rows, width), BF), [VMEM] * (2 * len(pieces)))(
-        *[x for pair in zip(kept, passing, strict=True) for x in pair]
+    output = call(add_body, shape((rows, pieces[0][1]), BF), [VMEM] * 2, flops=2 * SHORT, moved=0)(
+        kept[0], passing[0]
+    )
+    output = call(final_body, shape((rows, width), BF), [VMEM] * 3)(
+        output, after(kept[1], output), after(passing[1], output)
     )
     return output[None]
 

time: 164 us -> 155 us (0.945)
  waiting for transfers between devices: 60.6 us -> 49.3 us
  Pallas kernels: 38.2 us -> 44.1 us
  starting transfers between devices: 57.2 us -> 55.2 us
    pallas_call x21 -> x42, Pallas kernels: 9.34 us -> 24.1 us  [the longest x8 11.5 us: project(): call(functools.partial(gate_up_body, len(parts)), tuple((shape((n, gate_u...]
    ppermute x26 -> x27, waiting for transfers between devices: 44.8 us -> 32.9 us  [on_device(): step = lambda x: lax.ppermute(x, 'expert', ring)]
    pallas_call x4, Pallas kernels: 15.5 us -> 6.38 us  [expert(): call(functools.partial(expert_body, ks, most, chips), (shape((len(ks), mo...]
    ppermute x26 -> x27, starting transfers between devices: 46.9 us -> 44.8 us  [on_device(): step = lambda x: lax.ppermute(x, 'expert', ring)]
    ppermute x14 -> x19, starting transfers between devices: 2.58 us -> 3.51 us  [on_device(): lax.ppermute(x, 'expert', [(i, i ^ 1) for i in range(owners)])]
    unnamed x68 -> x24, local copies, waits for them, and re-layouts: 5.75 us -> 4.92 us
  transfers between devices with their start and end apart: 44 -> 50, of which waited for: 24 -> 26; matrix products, arithmetic and copies ran while one was open for 1% -> 0% of each run, Pallas kernels for 18% -> 23%
where the time goes in v5:
time: 155 us
  starting transfers between devices  55.2 us (36%)
  waiting for transfers between devices  49.3 us (32%)
  Pallas kernels  44.1 us (28%)
  local copies, waits for them, and re-layouts  5.62 us (4%)
    ppermute x27, starting transfers between devices, on_device(): step = lambda x: lax.ppermute(x, 'expert', ring)  44.8 us
    ppermute x27, waiting for transfers between devices, on_device(): step = lambda x: lax.ppermute(x, 'expert', ring)  32.9 us
    ppermute x2, waiting for transfers between devices, on_device(): cross = lambda x: lax.ppermute(x, ('pipe', 'expert'), last)  12.4 us
    pallas_call x8, Pallas kernels, project(): call(functools.partial(gate_up_body, len(parts)), tuple((shape((n, gate_u...  11.5 us
    pallas_call x8, Pallas kernels, choose(): call(functools.partial(choose_body, most), (shape((most, width), BF), sha...  7.89 us
    pallas_call x4, Pallas kernels, expert(): call(functools.partial(expert_body, ks, most, chips), (shape((len(ks), mo...  6.38 us
    pallas_call x1, Pallas kernels, on_device(): call(functools.partial(attend_body, most, chips, 4, groups), (shape((owne...  5.57 us
    pallas_call x14, Pallas kernels, combine(): call(functools.partial(combine_body, k, mine[k][1], most, chips, start, s...  5.04 us
  transfers between devices with their start and end apart: 50, of which 26 were waited for; matrix products, arithmetic and copies ran while one was open for 0% of the time, Pallas kernels for 23%

profile of v5, /device:TPU:0, one launch (start us, length us, event | category | flops | bytes accessed | tf_op | source)
XLA Modules:
  0.0 155.0 jit_solution(2042904219035942032)
XLA Ops:
  1.8 3.1 %collective-permute-start.1 = (bf16[320,256]{1,0:T(8,128)(2,1)S(1)}, bf16[320,256]{1,0:T(8,128)(2,1)S(1)}, u32[]{:S(2)}, u32[]{:S(2)}) collective-permute-start(bf16[320,256]{1,0:T(8,128)(2,1)S(1)} %shard_map.109.piece), channel_id=1, source_target_pairs={{0,4},{1,3},{4,8},{5,1},{8,12},{9,5},{12,14},{13,9},{14,10},{15,13... | collective-permute-start | bytes 491528 | tf_op jit(solution)/shard_map/ppermute | solution.py:330
  13.2 2.1 %collective-permute-done.piece.two.refs_3_ = bf16[656,256]{1,0:T(8,128)(2,1)S(1)} collective-permute-done((bf16[656,256]{1,0:T(8,128)(2,1)S(1)}, bf16[656,256]{1,0:T(8,128)(2,1)S(1)}, u32[]{:S(2)}, u32[]{:S(2)}) %collective-permute-start) | collective-permute-done | bytes 335904 | tf_op jit(solution)/shard_map/ppermute | solution.py:330
  16.9 1.7 %shard_map.117 = (bf16[64,1536]{1,0:T(8,128)(2,1)S(1)}, bf16[16,1536]{1,0:T(8,128)(2,1)S(1)}, bf16[16,1536]{1,0:T(8,128)(2,1)S(1)}, bf16[64,1536]{1,0:T(8,128)(2...) custom-call(bf16[2560,1536]{1,0:T(8,128)(2,1)S(1)} %bitcast.14, ...), custom_call_target="tpu_custom_call" | custom-call | tf_op jit(solution)/shard_map/pallas_call | solution.py:376
  18.6 2.0 %collective-permute-done.4.piece.one.refs_2_ = bf16[960,256]{1,0:T(8,128)(2,1)S(1)} collective-permute-done((bf16[960,256]{1,0:T(8,128)(2,1)S(1)}, bf16[960,256]{1,0:T(8,128)(2,1)S(1)}, u32[]{:S(2)}, u32[]{:S(2)}) %collective-permute-start.4) | collective-permute-done | bytes 491552 | tf_op jit(solution)/shard_map/ppermute | solution.py:330
  27.2 2.2 %collective-permute-done.7.piece.one.refs_4_ = bf16[960,256]{1,0:T(8,128)(2,1)S(1)} collective-permute-done((bf16[960,256]{1,0:T(8,128)(2,1)S(1)}, bf16[960,256]{1,0:T(8,128)(2,1)S(1)}, u32[]{:S(2)}, u32[]{:S(2)}) %collective-permute-start.7) | collective-permute-done | bytes 491552 | tf_op jit(solution)/shard_map/ppermute | solution.py:330
  36.0 2.2 %collective-permute-done.10.piece.one.refs_6_ = bf16[960,256]{1,0:T(8,128)(2,1)S(1)} collective-permute-done((bf16[960,256]{1,0:T(8,128)(2,1)S(1)}, bf16[960,256]{1,0:T(8,128)(2,1)S(1)}, u32[]{:S(2)}, u32[]{:S(2)}) %collective-permute-start.10) | collective-permute-done | bytes 491552 | tf_op jit(solution)/shard_map/ppermute | solution.py:330
  44.9 2.2 %collective-permute-done.13.piece.one.refs_8_ = bf16[960,256]{1,0:T(8,128)(2,1)S(1)} collective-permute-done((bf16[960,256]{1,0:T(8,128)(2,1)S(1)}, bf16[960,256]{1,0:T(8,128)(2,1)S(1)}, u32[]{:S(2)}, u32[]{:S(2)}) %collective-permute-start.13) | collective-permute-done | bytes 491552 | tf_op jit(solution)/shard_map/ppermute | solution.py:330
  53.8 2.2 %collective-permute-done.16.piece.one.refs_10_ = bf16[960,256]{1,0:T(8,128)(2,1)S(1)} collective-permute-done((bf16[960,256]{1,0:T(8,128)(2,1)S(1)}, bf16[960,256]{1,0:T(8,128)(2,1)S(1)}, u32[]{:S(2)}, u32[]{:S(2)}) %collective-permute-start.16) | collective-permute-done | bytes 491552 | tf_op jit(solution)/shard_map/ppermute | solution.py:330
  62.6 2.2 %collective-permute-done.19.piece.one.refs_12_ = bf16[960,256]{1,0:T(8,128)(2,1)S(1)} collective-permute-done((bf16[960,256]{1,0:T(8,128)(2,1)S(1)}, bf16[960,256]{1,0:T(8,128)(2,1)S(1)}, u32[]{:S(2)}, u32[]{:S(2)}) %collective-permute-start.19) | collective-permute-done | bytes 491552 | tf_op jit(solution)/shard_map/ppermute | solution.py:330
  65.0 1.8 %collective-permute-start.24 = (bf16[640,256]{1,0:T(8,128)(2,1)S(1)}, bf16[640,256]{1,0:T(8,128)(2,1)S(1)}, u32[]{:S(2)}, u32[]{:S(2)}) collective-permute-start(bf16[640,256]{1,0:T(8,128)(2,1)S(1)} %shard_map.148), channel_id=1, source_target_pairs={{0,4},{1,3},{4,8},{5,1},{8,12},{9,5},{12,14},{13,9},{14,10},{15,13... | collective-permute-start | bytes 983048 | tf_op jit(solution)/shard_map/ppermute | solution.py:330
  76.5 5.6 %shard_map.150 = (bf16[1024,256]{1,0:T(8,128)(2,1)S(1)}, bf16[2048,256]{1,0:T(8,128)(2,1)S(1)}) custom-call(s32[8,256]{1,0:T(8,128)S(1)} %constant_dynamic-slice_fusion.ids.order, s32[8,256]{1,0:T(8,128)S(1)} %constant_dynamic-slice_fusion.ids.order, f32[40,256]{1,0:T(8,128)S(1)} %shard_map.143.meta, bf16[256,256]{1,0:T(8,128)(2,1)S(1)} %bitcast.39, ...), custom_call_target="tpu_custom_call" | custom-call | flops 10000000000 | bytes 100000000 | tf_op jit(solution)/shard_map/pallas_call | solution.py:455
  91.6 1.8 %collective-permute-done.30.refs_0_ = bf16[128,1280]{1,0:T(8,128)(2,1)S(1)} collective-permute-done((bf16[128,1280]{1,0:T(8,128)(2,1)S(1)}, bf16[128,1280]{1,0:T(8,128)(2,1)S(1)}, u32[]{:S(2)}, u32[]{:S(2)}) %collective-permute-start.30) | collective-permute-done | bytes 327712 | tf_op jit(solution)/shard_map/ppermute | solution.py:330
  97.3 1.9 %collective-permute-start.34 = (bf16[128,1280]{1,0:T(8,128)(2,1)S(1)}, bf16[128,1280]{1,0:T(8,128)(2,1)S(1)}, u32[]{:S(2)}, u32[]{:S(2)}) collective-permute-start(bf16[128,1280]{1,0:T(8,128)(2,1)S(1)} %shard_map.159), channel_id=1, source_target_pairs={{0,4},{1,3},{4,8},{5,1},{8,12},{9,5},{12,14},{13,9},{14,10},{15,13... | collective-permute-start | bytes 983048 | tf_op jit(solution)/shard_map/ppermute | solution.py:330
  106.6 2.9 %shard_map.163 = (bf16[128,1280]{1,0:T(8,128)(2,1)S(1)}, bf16[128,1280]{1,0:T(8,128)(2,1)S(1)}) custom-call(s32[8,256]{1,0:T(8,128)S(1)} %constant_dynamic-slice_fusion.ids.order, s32[8,256]{1,0:T(8,128)S(1)} %constant_dynamic-slice_fusion.ids.order, f32[40,256]{1,0:T(8,128)S(1)} %shard_map.143.meta, bf16[256,256]{1,0:T(8,128)(2,1)S(1)} %bitcast.40, ...), custom_call_target="tpu_custom_call" | custom-call | tf_op jit(solution)/shard_map/pallas_call | solution.py:509
  112.0 1.6 %collective-permute-start.39 = (bf16[128,1280]{1,0:T(8,128)(2,1)S(1)}, bf16[128,1280]{1,0:T(8,128)(2,1)S(1)}, u32[]{:S(2)}, u32[]{:S(2)}) collective-permute-start(bf16[128,1280]{1,0:T(8,128)(2,1)S(1)} %shard_map.165), channel_id=1, source_target_pairs={{0,4},{1,3},{4,8},{5,1},{8,12},{9,5},{12,14},{13,9},{14,10},{15,13... | collective-permute-start | bytes 983048 | tf_op jit(solution)/shard_map/ppermute | solution.py:330
  117.2 3.0 %collective-permute-done.35.one = bf16[128,1280]{1,0:T(8,128)(2,1)S(1)} collective-permute-done((bf16[128,1280]{1,0:T(8,128)(2,1)S(1)}, bf16[128,1280]{1,0:T(8,128)(2,1)S(1)}, u32[]{:S(2)}, u32[]{:S(2)}) %collective-permute-start.35) | collective-permute-done | bytes 327712 | tf_op jit(solution)/shard_map/ppermute | solution.py:335
  123.0 1.6 %collective-permute-start.45 = (bf16[128,1280]{1,0:T(8,128)(2,1)S(1)}, bf16[128,1280]{1,0:T(8,128)(2,1)S(1)}, u32[]{:S(2)}, u32[]{:S(2)}) collective-permute-start(bf16[128,1280]{1,0:T(8,128)(2,1)S(1)} %shard_map.168), channel_id=1, source_target_pairs={{0,4},{1,3},{4,8},{5,1},{8,12},{9,5},{12,14},{13,9},{14,10},{15,13... | collective-permute-start | bytes 983048 | tf_op jit(solution)/shard_map/ppermute | solution.py:330
  124.6 3.1 %collective-permute-done.43.refs_0_ = bf16[128,1280]{1,0:T(8,128)(2,1)S(1)} collective-permute-done((bf16[128,1280]{1,0:T(8,128)(2,1)S(1)}, bf16[128,1280]{1,0:T(8,128)(2,1)S(1)}, u32[]{:S(2)}, u32[]{:S(2)}) %collective-permute-start.43) | collective-permute-done | bytes 327712 | tf_op jit(solution)/shard_map/ppermute | solution.py:330
  129.6 1.7 %collective-permute-done.45.refs_0_ = bf16[128,1280]{1,0:T(8,128)(2,1)S(1)} collective-permute-done((bf16[128,1280]{1,0:T(8,128)(2,1)S(1)}, bf16[128,1280]{1,0:T(8,128)(2,1)S(1)}, u32[]{:S(2)}, u32[]{:S(2)}) %collective-permute-start.45) | collective-permute-done | bytes 327712 | tf_op jit(solution)/shard_map/ppermute | solution.py:330
  133.1 2.1 %collective-permute-done.46.refs_0_ = bf16[128,1280]{1,0:T(8,128)(2,1)S(1)} collective-permute-done((bf16[128,1280]{1,0:T(8,128)(2,1)S(1)}, bf16[128,1280]{1,0:T(8,128)(2,1)S(1)}, u32[]{:S(2)}, u32[]{:S(2)}) %collective-permute-start.46) | collective-permute-done | bytes 327712 | tf_op jit(solution)/shard_map/ppermute | solution.py:330
  135.6 2.4 %collective-permute-start.47 = (bf16[128,1280]{1,0:T(8,128)(2,1)S(1)}, bf16[128,1280]{1,0:T(8,128)(2,1)S(1)}, u32[]{:S(2)}, u32[]{:S(2)}) collective-permute-start(bf16[128,1280]{1,0:T(8,128)(2,1)S(1)} %shard_map.174), channel_id=1, source_target_pairs={{0,20},{1,19},{4,24},{5,17},{8,28},{9,21},{12,30},{13,25},{14,26},... | collective-permute-start | bytes 983048 | tf_op jit(solution)/shard_map/ppermute | solution.py:493
  139.1 2.4 %collective-permute-start.49 = (bf16[128,1280]{1,0:T(8,128)(2,1)S(1)}, bf16[128,1280]{1,0:T(8,128)(2,1)S(1)}, u32[]{:S(2)}, u32[]{:S(2)}) collective-permute-start(bf16[128,1280]{1,0:T(8,128)(2,1)S(1)} %shard_map.176), channel_id=1, source_target_pairs={{0,20},{1,19},{4,24},{5,17},{8,28},{9,21},{12,30},{13,25},{14,26},... | collective-permute-start | bytes 983048 | tf_op jit(solution)/shard_map/ppermute | solution.py:493
  141.5 9.0 %collective-permute-done.47.two = bf16[128,1280]{1,0:T(8,128)(2,1)S(1)} collective-permute-done((bf16[128,1280]{1,0:T(8,128)(2,1)S(1)}, bf16[128,1280]{1,0:T(8,128)(2,1)S(1)}, u32[]{:S(2)}, u32[]{:S(2)}) %collective-permute-start.47) | collective-permute-done | bytes 327712 | tf_op jit(solution)/shard_map/ppermute | solution.py:493
  150.6 3.4 %collective-permute-done.49.two = bf16[128,1280]{1,0:T(8,128)(2,1)S(1)} collective-permute-done((bf16[128,1280]{1,0:T(8,128)(2,1)S(1)}, bf16[128,1280]{1,0:T(8,128)(2,1)S(1)}, u32[]{:S(2)}, u32[]{:S(2)}) %collective-permute-start.49) | collective-permute-done | bytes 327712 | tf_op jit(solution)/shard_map/ppermute | solution.py:493
  (171 shorter events, 89.9 us)
Async XLA Ops:
  11.6 9.0 %collective-permute-start.4 = (bf16[960,256]{1,0:T(8,128)(2,1)S(1)}, bf16[960,256]{1,0:T(8,128)(2,1)S(1)}, u32[]{:S(2)}, u32[]{:S(2)}) collective-permute-start(bf16[960,256]{1,0:T(8,128)(2,1)S(1)} %shard_map.112.one.refs_0_), channel_id=1, source_target_pairs={{0,4},{1,3},{4,8},{5,1},{8,12},{9,5},{12,14},{13,9},{14,10},{15,13... | collective-permute-start | bytes 1474568 | tf_op jit(solution)/shard_map/ppermute | solution.py:330
  15.3 8.9 %collective-permute-start.2 = (bf16[656,256]{1,0:T(8,128)(2,1)S(1)}, bf16[656,256]{1,0:T(8,128)(2,1)S(1)}, u32[]{:S(2)}, u32[]{:S(2)}) collective-permute-start(bf16[656,256]{1,0:T(8,128)(2,1)S(1)} %collective-permute-done.piece.two.refs_3_), channel_id=1, source_target_pairs={{0,4},{1,3},{4,8},{5,1},{8,12},{9,5},{12,14},{13,9},{14,10},{15,13... | collective-permute-start | bytes 1007624 | tf_op jit(solution)/shard_map/ppermute | solution.py:330
  20.6 8.9 %collective-permute-start.7 = (bf16[960,256]{1,0:T(8,128)(2,1)S(1)}, bf16[960,256]{1,0:T(8,128)(2,1)S(1)}, u32[]{:S(2)}, u32[]{:S(2)}) collective-permute-start(bf16[960,256]{1,0:T(8,128)(2,1)S(1)} %collective-permute-done.4.piece.one.refs_2_), channel_id=1, source_target_pairs={{0,4},{1,3},{4,8},{5,1},{8,12},{9,5},{12,14},{13,9},{14,10},{15,13... | collective-permute-start | bytes 1474568 | tf_op jit(solution)/shard_map/ppermute | solution.py:330
  24.2 8.9 %collective-permute-start.5 = (bf16[656,256]{1,0:T(8,128)(2,1)S(1)}, bf16[656,256]{1,0:T(8,128)(2,1)S(1)}, u32[]{:S(2)}, u32[]{:S(2)}) collective-permute-start(bf16[656,256]{1,0:T(8,128)(2,1)S(1)} %collective-permute-done.2.piece.two.refs_5_), channel_id=1, source_target_pairs={{0,4},{1,3},{4,8},{5,1},{8,12},{9,5},{12,14},{13,9},{14,10},{15,13... | collective-permute-start | bytes 1007624 | tf_op jit(solution)/shard_map/ppermute | solution.py:330
  29.4 8.9 %collective-permute-start.10 = (bf16[960,256]{1,0:T(8,128)(2,1)S(1)}, bf16[960,256]{1,0:T(8,128)(2,1)S(1)}, u32[]{:S(2)}, u32[]{:S(2)}) collective-permute-start(bf16[960,256]{1,0:T(8,128)(2,1)S(1)} %collective-permute-done.7.piece.one.refs_4_), channel_id=1, source_target_pairs={{0,4},{1,3},{4,8},{5,1},{8,12},{9,5},{12,14},{13,9},{14,10},{15,13... | collective-permute-start | bytes 1474568 | tf_op jit(solution)/shard_map/ppermute | solution.py:330
  33.0 8.9 %collective-permute-start.8 = (bf16[656,256]{1,0:T(8,128)(2,1)S(1)}, bf16[656,256]{1,0:T(8,128)(2,1)S(1)}, u32[]{:S(2)}, u32[]{:S(2)}) collective-permute-start(bf16[656,256]{1,0:T(8,128)(2,1)S(1)} %collective-permute-done.5.piece.two.refs_7_), channel_id=1, source_target_pairs={{0,4},{1,3},{4,8},{5,1},{8,12},{9,5},{12,14},{13,9},{14,10},{15,13... | collective-permute-start | bytes 1007624 | tf_op jit(solution)/shard_map/ppermute | solution.py:330
  38.3 8.9 %collective-permute-start.13 = (bf16[960,256]{1,0:T(8,128)(2,1)S(1)}, bf16[960,256]{1,0:T(8,128)(2,1)S(1)}, u32[]{:S(2)}, u32[]{:S(2)}) collective-permute-start(bf16[960,256]{1,0:T(8,128)(2,1)S(1)} %collective-permute-done.10.piece.one.refs_6_), channel_id=1, source_target_pairs={{0,4},{1,3},{4,8},{5,1},{8,12},{9,5},{12,14},{13,9},{14,10},{15,13... | collective-permute-start | bytes 1474568 | tf_op jit(solution)/shard_map/ppermute | solution.py:330
  41.9 8.9 %collective-permute-start.11 = (bf16[656,256]{1,0:T(8,128)(2,1)S(1)}, bf16[656,256]{1,0:T(8,128)(2,1)S(1)}, u32[]{:S(2)}, u32[]{:S(2)}) collective-permute-start(bf16[656,256]{1,0:T(8,128)(2,1)S(1)} %collective-permute-done.8.piece.two.refs_9_), channel_id=1, source_target_pairs={{0,4},{1,3},{4,8},{5,1},{8,12},{9,5},{12,14},{13,9},{14,10},{15,13... | collective-permute-start | bytes 1007624 | tf_op jit(solution)/shard_map/ppermute | solution.py:330
  47.1 8.9 %collective-permute-start.16 = (bf16[960,256]{1,0:T(8,128)(2,1)S(1)}, bf16[960,256]{1,0:T(8,128)(2,1)S(1)}, u32[]{:S(2)}, u32[]{:S(2)}) collective-permute-start(bf16[960,256]{1,0:T(8,128)(2,1)S(1)} %collective-permute-done.13.piece.one.refs_8_), channel_id=1, source_target_pairs={{0,4},{1,3},{4,8},{5,1},{8,12},{9,5},{12,14},{13,9},{14,10},{15,13... | collective-permute-start | bytes 1474568 | tf_op jit(solution)/shard_map/ppermute | solution.py:330
  50.7 8.9 %collective-permute-start.14 = (bf16[656,256]{1,0:T(8,128)(2,1)S(1)}, bf16[656,256]{1,0:T(8,128)(2,1)S(1)}, u32[]{:S(2)}, u32[]{:S(2)}) collective-permute-start(bf16[656,256]{1,0:T(8,128)(2,1)S(1)} %collective-permute-done.11.piece.two.refs_11_), channel_id=1, source_target_pairs={{0,4},{1,3},{4,8},{5,1},{8,12},{9,5},{12,14},{13,9},{14,10},{15,13... | collective-permute-start | bytes 1007624 | tf_op jit(solution)/shard_map/ppermute | solution.py:330
  56.0 8.9 %collective-permute-start.19 = (bf16[960,256]{1,0:T(8,128)(2,1)S(1)}, bf16[960,256]{1,0:T(8,128)(2,1)S(1)}, u32[]{:S(2)}, u32[]{:S(2)}) collective-permute-start(bf16[960,256]{1,0:T(8,128)(2,1)S(1)} %collective-permute-done.16.piece.one.refs_10_), channel_id=1, source_target_pairs={{0,4},{1,3},{4,8},{5,1},{8,12},{9,5},{12,14},{13,9},{14,10},{15,13... | collective-permute-start | bytes 1474568 | tf_op jit(solution)/shard_map/ppermute | solution.py:330
  58.7 9.1 %collective-permute-start.22 = (bf16[7,160,256]{2,1,0:T(8,128)(2,1)S(1)}, bf16[7,160,256]{2,1,0:T(8,128)(2,1)S(1)}, u32[]{:S(2)}, u32[]{:S(2)}) collective-permute-start(bf16[7,160,256]{2,1,0:T(8,128)(2,1)S(1)} %shard_map.144.refs_0_), channel_id=1, source_target_pairs={{0,1},{1,0},{2,3},{3,2},{4,5},{5,4},{6,7},{7,6},{8,9},{9,8},{10,11... | collective-permute-start | bytes 1720328 | tf_op jit(solution)/shard_map/ppermute | solution.py:331
  59.6 11.2 %collective-permute-start.17 = (bf16[656,256]{1,0:T(8,128)(2,1)S(1)}, bf16[656,256]{1,0:T(8,128)(2,1)S(1)}, u32[]{:S(2)}, u32[]{:S(2)}) collective-permute-start(bf16[656,256]{1,0:T(8,128)(2,1)S(1)} %collective-permute-done.14.piece.two.refs_13_), channel_id=1, source_target_pairs={{0,4},{1,3},{4,8},{5,1},{8,12},{9,5},{12,14},{13,9},{14,10},{15,13... | collective-permute-start | bytes 1007624 | tf_op jit(solution)/shard_map/ppermute | solution.py:330
  85.1 15.6 %collective-permute-start.41 = (bf16[64,2560]{1,0:T(8,128)(2,1)S(1)}, bf16[64,2560]{1,0:T(8,128)(2,1)S(1)}, u32[]{:S(2)}, u32[]{:S(2)}) collective-permute-start(bf16[64,2560]{1,0:T(8,128)(2,1)S(1)} %get-tuple-element.267), channel_id=1, source_target_pairs={{0,1},{1,0},{2,3},{3,2},{4,5},{5,4},{6,7},{7,6},{8,9},{9,8},{10,11... | collective-permute-start | bytes 983048 | tf_op jit(solution)/shard_map/ppermute | solution.py:331
  85.4 21.2 %collective-permute-start.27 = (bf16[128,2560]{1,0:T(8,128)(2,1)S(1)}, bf16[128,2560]{1,0:T(8,128)(2,1)S(1)}, u32[]{:S(2)}, u32[]{:S(2)}) collective-permute-start(bf16[128,2560]{1,0:T(8,128)(2,1)S(1)} %bitcast.37), channel_id=1, source_target_pairs={{0,1},{1,0},{2,3},{3,2},{4,5},{5,4},{6,7},{7,6},{8,9},{9,8},{10,11... | collective-permute-start | bytes 1966088 | tf_op jit(solution)/shard_map/ppermute | solution.py:331
  91.5 10.5 %collective-permute-start.32 = (bf16[2,64,2560]{2,1,0:T(8,128)(2,1)S(1)}, bf16[2,64,2560]{2,1,0:T(8,128)(2,1)S(1)}, u32[]{:S(2)}, u32[]{:S(2)}) collective-permute-start(bf16[2,64,2560]{2,1,0:T(8,128)(2,1)S(1)} %get-tuple-element.245), channel_id=1, source_target_pairs={{0,1},{1,0},{2,3},{3,2},{4,5},{5,4},{6,7},{7,6},{8,9},{9,8},{10,11... | collective-permute-start | bytes 1966088 | tf_op jit(solution)/shard_map/ppermute | solution.py:331
  100.7 10.9 %collective-permute-start.36 = (bf16[2,64,2560]{2,1,0:T(8,128)(2,1)S(1)}, bf16[2,64,2560]{2,1,0:T(8,128)(2,1)S(1)}, u32[]{:S(2)}, u32[]{:S(2)}) collective-permute-start(bf16[2,64,2560]{2,1,0:T(8,128)(2,1)S(1)} %get-tuple-element.254), channel_id=1, source_target_pairs={{0,1},{1,0},{2,3},{3,2},{4,5},{5,4},{6,7},{7,6},{8,9},{9,8},{10,11... | collective-permute-start | bytes 1966088 | tf_op jit(solution)/shard_map/ppermute | solution.py:331
  102.4 9.2 %collective-permute-start.37 = (bf16[128,1280]{1,0:T(8,128)(2,1)S(1)}, bf16[128,1280]{1,0:T(8,128)(2,1)S(1)}, u32[]{:S(2)}, u32[]{:S(2)}) collective-permute-start(bf16[128,1280]{1,0:T(8,128)(2,1)S(1)} %shard_map.161), channel_id=1, source_target_pairs={{0,4},{1,3},{4,8},{5,1},{8,12},{9,5},{12,14},{13,9},{14,10},{15,13... | collective-permute-start | bytes 983048 | tf_op jit(solution)/shard_map/ppermute | solution.py:330
  105.0 8.7 %collective-permute-start.38 = (bf16[128,1280]{1,0:T(8,128)(2,1)S(1)}, bf16[128,1280]{1,0:T(8,128)(2,1)S(1)}, u32[]{:S(2)}, u32[]{:S(2)}) collective-permute-start(bf16[128,1280]{1,0:T(8,128)(2,1)S(1)} %shard_map.162), channel_id=1, source_target_pairs={{0,4},{1,3},{4,8},{5,1},{8,12},{9,5},{12,14},{13,9},{14,10},{15,13... | collective-permute-start | bytes 983048 | tf_op jit(solution)/shard_map/ppermute | solution.py:330
  109.5 10.7 %collective-permute-start.35 = (bf16[128,1280]{1,0:T(8,128)(2,1)S(1)}, bf16[128,1280]{1,0:T(8,128)(2,1)S(1)}, u32[]{:S(2)}, u32[]{:S(2)}) collective-permute-start(bf16[128,1280]{1,0:T(8,128)(2,1)S(1)} %get-tuple-element.249), channel_id=1, source_target_pairs={{0,16},{16,0},{1,17},{17,1},{2,18},{18,2},{3,19},{19,3},{4,20},{20... | collective-permute-start | bytes 983048 | tf_op jit(solution)/shard_map/ppermute | solution.py:335
  111.1 13.6 %collective-permute-start.44 = (bf16[128,1280]{1,0:T(8,128)(2,1)S(1)}, bf16[128,1280]{1,0:T(8,128)(2,1)S(1)}, u32[]{:S(2)}, u32[]{:S(2)}) collective-permute-start(bf16[128,1280]{1,0:T(8,128)(2,1)S(1)} %get-tuple-element.255), channel_id=1, source_target_pairs={{0,16},{16,0},{1,17},{17,1},{2,18},{18,2},{3,19},{19,3},{4,20},{20... | collective-permute-start | bytes 983048 | tf_op jit(solution)/shard_map/ppermute | solution.py:335
  117.2 10.6 %collective-permute-start.42 = (bf16[2,64,2560]{2,1,0:T(8,128)(2,1)S(1)}, bf16[2,64,2560]{2,1,0:T(8,128)(2,1)S(1)}, u32[]{:S(2)}, u32[]{:S(2)}) collective-permute-start(bf16[2,64,2560]{2,1,0:T(8,128)(2,1)S(1)} %get-tuple-element.272), channel_id=1, source_target_pairs={{0,1},{1,0},{2,3},{3,2},{4,5},{5,4},{6,7},{7,6},{8,9},{9,8},{10,11... | collective-permute-start | bytes 1966088 | tf_op jit(solution)/shard_map/ppermute | solution.py:331
  135.6 14.9 %collective-permute-start.47 = (bf16[128,1280]{1,0:T(8,128)(2,1)S(1)}, bf16[128,1280]{1,0:T(8,128)(2,1)S(1)}, u32[]{:S(2)}, u32[]{:S(2)}) collective-permute-start(bf16[128,1280]{1,0:T(8,128)(2,1)S(1)} %shard_map.174), channel_id=1, source_target_pairs={{0,20},{1,19},{4,24},{5,17},{8,28},{9,21},{12,30},{13,25},{14,26},... | collective-permute-start | bytes 983048 | tf_op jit(solution)/shard_map/ppermute | solution.py:493
  139.1 14.9 %collective-permute-start.49 = (bf16[128,1280]{1,0:T(8,128)(2,1)S(1)}, bf16[128,1280]{1,0:T(8,128)(2,1)S(1)}, u32[]{:S(2)}, u32[]{:S(2)}) collective-permute-start(bf16[128,1280]{1,0:T(8,128)(2,1)S(1)} %shard_map.176), channel_id=1, source_target_pairs={{0,20},{1,19},{4,24},{5,17},{8,28},{9,21},{12,30},{13,25},{14,26},... | collective-permute-start | bytes 983048 | tf_op jit(solution)/shard_map/ppermute | solution.py:493
  (38 other events, 171.3 us)

commit v6 on v5

--- a/solution.py
+++ b/solution.py
@@ -431,6 +431,10 @@
     )
     wide_a, wide_b = (stack(thin).reshape(-1, gate_up.shape[1]) for thin in (thin_a, thin_b))
 
+    parts = [stack(listed[:-1]), stack(listed[-1:])]
+    meta = call(table_body, shape((5 * chips, latent), F32), [SMEM] + [VMEM] * 4)(
+        ids, *parts, *[sibling(x) for x in parts]
+    )
     lat_a, lat_b, groups = [], [], (tuple(range(chips - 1)), (chips - 1,))
     for group in groups:
         lat = call(
@@ -448,12 +452,8 @@
         lat_b.append(sibling(lat))
     chosen.append(choose(listed[-1], first[-1], second[-1], [], lat_a[1]))
     other.append(sibling(chosen[-1][1]))
-    parts = [stack(listed[:-1]), stack(listed[-1:])]
-    meta = call(table_body, shape((5 * chips, latent), F32), [SMEM] + [VMEM] * 4)(
-        ids, *parts, *[sibling(x) for x in parts]
-    )
     att, lat = call(
-        functools.partial(attend_body, most, chips, 4, groups),
+        functools.partial(attend_body, most, chips, 8, groups),
         (shape((owners * most, latent), BF), shape((owners * rows, latent), BF)),
         [SMEM] + [VMEM] * (3 + 4),
         flops=LONG,
@@ -496,7 +496,7 @@
         totals = []
         for i in range(len(pieces)):
             more = [] if k == 1 else [passing[i]]
-            if i == 0 and chips - 3 <= k < chips - 1:
+            if i == 1 and chips - 3 <= k < chips - 1:
                 more = [after(more[0], kept[k - (chips - 3)])]
             totals.append(combine(k, i, done[-1:], *more))
             done.append(totals[i])

time: 155 us -> 154 us (level)
  waiting for transfers between devices: 49.3 us -> 47.5 us
    ppermute x2, waiting for transfers between devices: 2.99 us -> 0.01 us  [on_device(): lax.ppermute(x, 'pipe', [(p, (p + 1) % pipes) for p in range(pipes)])]
where the time goes in v6:
time: 154 us
  starting transfers between devices  55.9 us (36%)
  waiting for transfers between devices  47.5 us (31%)
  Pallas kernels  43.8 us (28%)
  local copies, waits for them, and re-layouts  5.62 us (4%)
    ppermute x27, starting transfers between devices, on_device(): step = lambda x: lax.ppermute(x, 'expert', ring)  45.2 us
    ppermute x27, waiting for transfers between devices, on_device(): step = lambda x: lax.ppermute(x, 'expert', ring)  34.3 us
    ppermute x2, waiting for transfers between devices, on_device(): cross = lambda x: lax.ppermute(x, ('pipe', 'expert'), last)  12.3 us
    pallas_call x8, Pallas kernels, project(): call(functools.partial(gate_up_body, len(parts)), tuple((shape((n, gate_u...  11.5 us
    pallas_call x8, Pallas kernels, choose(): call(functools.partial(choose_body, most), (shape((most, width), BF), sha...  7.89 us
    pallas_call x4, Pallas kernels, expert(): call(functools.partial(expert_body, ks, most, chips), (shape((len(ks), mo...  6.38 us
    pallas_call x1, Pallas kernels, on_device(): call(functools.partial(attend_body, most, chips, 8, groups), (shape((owne...  5.29 us
    ppermute x2, starting transfers between devices, on_device(): cross = lambda x: lax.ppermute(x, ('pipe', 'expert'), last)  5.13 us
  transfers between devices with their start and end apart: 50, of which 26 were waited for; matrix products, arithmetic and copies ran while one was open for 0% of the time, Pallas kernels for 23%

profile of v6, /device:TPU:0, one launch (start us, length us, event | category | flops | bytes accessed | tf_op | source)
XLA Modules:
  0.0 153.5 jit_solution(9369685997423977950)
XLA Ops:
  1.8 3.1 %collective-permute-start.1 = (bf16[320,256]{1,0:T(8,128)(2,1)S(1)}, bf16[320,256]{1,0:T(8,128)(2,1)S(1)}, u32[]{:S(2)}, u32[]{:S(2)}) collective-permute-start(bf16[320,256]{1,0:T(8,128)(2,1)S(1)} %shard_map.109.piece), channel_id=1, source_target_pairs={{0,4},{1,3},{4,8},{5,1},{8,12},{9,5},{12,14},{13,9},{14,10},{15,13... | collective-permute-start | bytes 491528 | tf_op jit(solution)/shard_map/ppermute | solution.py:330
  13.2 2.1 %collective-permute-done.piece.two.refs_3_ = bf16[656,256]{1,0:T(8,128)(2,1)S(1)} collective-permute-done((bf16[656,256]{1,0:T(8,128)(2,1)S(1)}, bf16[656,256]{1,0:T(8,128)(2,1)S(1)}, u32[]{:S(2)}, u32[]{:S(2)}) %collective-permute-start) | collective-permute-done | bytes 335904 | tf_op jit(solution)/shard_map/ppermute | solution.py:330
  16.9 1.7 %shard_map.117 = (bf16[64,1536]{1,0:T(8,128)(2,1)S(1)}, bf16[16,1536]{1,0:T(8,128)(2,1)S(1)}, bf16[16,1536]{1,0:T(8,128)(2,1)S(1)}, bf16[64,1536]{1,0:T(8,128)(2...) custom-call(bf16[2560,1536]{1,0:T(8,128)(2,1)S(1)} %bitcast.14, ...), custom_call_target="tpu_custom_call" | custom-call | tf_op jit(solution)/shard_map/pallas_call | solution.py:376
  18.6 2.0 %collective-permute-done.4.piece.one.refs_2_ = bf16[960,256]{1,0:T(8,128)(2,1)S(1)} collective-permute-done((bf16[960,256]{1,0:T(8,128)(2,1)S(1)}, bf16[960,256]{1,0:T(8,128)(2,1)S(1)}, u32[]{:S(2)}, u32[]{:S(2)}) %collective-permute-start.4) | collective-permute-done | bytes 491552 | tf_op jit(solution)/shard_map/ppermute | solution.py:330
  27.2 2.2 %collective-permute-done.7.piece.one.refs_4_ = bf16[960,256]{1,0:T(8,128)(2,1)S(1)} collective-permute-done((bf16[960,256]{1,0:T(8,128)(2,1)S(1)}, bf16[960,256]{1,0:T(8,128)(2,1)S(1)}, u32[]{:S(2)}, u32[]{:S(2)}) %collective-permute-start.7) | collective-permute-done | bytes 491552 | tf_op jit(solution)/shard_map/ppermute | solution.py:330
  36.0 2.2 %collective-permute-done.10.piece.one.refs_6_ = bf16[960,256]{1,0:T(8,128)(2,1)S(1)} collective-permute-done((bf16[960,256]{1,0:T(8,128)(2,1)S(1)}, bf16[960,256]{1,0:T(8,128)(2,1)S(1)}, u32[]{:S(2)}, u32[]{:S(2)}) %collective-permute-start.10) | collective-permute-done | bytes 491552 | tf_op jit(solution)/shard_map/ppermute | solution.py:330
  44.9 2.2 %collective-permute-done.13.piece.one.refs_8_ = bf16[960,256]{1,0:T(8,128)(2,1)S(1)} collective-permute-done((bf16[960,256]{1,0:T(8,128)(2,1)S(1)}, bf16[960,256]{1,0:T(8,128)(2,1)S(1)}, u32[]{:S(2)}, u32[]{:S(2)}) %collective-permute-start.13) | collective-permute-done | bytes 491552 | tf_op jit(solution)/shard_map/ppermute | solution.py:330
  53.8 2.2 %collective-permute-done.16.piece.one.refs_10_ = bf16[960,256]{1,0:T(8,128)(2,1)S(1)} collective-permute-done((bf16[960,256]{1,0:T(8,128)(2,1)S(1)}, bf16[960,256]{1,0:T(8,128)(2,1)S(1)}, u32[]{:S(2)}, u32[]{:S(2)}) %collective-permute-start.16) | collective-permute-done | bytes 491552 | tf_op jit(solution)/shard_map/ppermute | solution.py:330
  62.6 2.2 %collective-permute-done.19.piece.one.refs_12_ = bf16[960,256]{1,0:T(8,128)(2,1)S(1)} collective-permute-done((bf16[960,256]{1,0:T(8,128)(2,1)S(1)}, bf16[960,256]{1,0:T(8,128)(2,1)S(1)}, u32[]{:S(2)}, u32[]{:S(2)}) %collective-permute-start.19) | collective-permute-done | bytes 491552 | tf_op jit(solution)/shard_map/ppermute | solution.py:330
  65.0 1.8 %collective-permute-start.24 = (bf16[640,256]{1,0:T(8,128)(2,1)S(1)}, bf16[640,256]{1,0:T(8,128)(2,1)S(1)}, u32[]{:S(2)}, u32[]{:S(2)}) collective-permute-start(bf16[640,256]{1,0:T(8,128)(2,1)S(1)} %shard_map.148), channel_id=1, source_target_pairs={{0,4},{1,3},{4,8},{5,1},{8,12},{9,5},{12,14},{13,9},{14,10},{15,13... | collective-permute-start | bytes 983048 | tf_op jit(solution)/shard_map/ppermute | solution.py:330
  76.5 5.3 %shard_map.150 = (bf16[1024,256]{1,0:T(8,128)(2,1)S(1)}, bf16[2048,256]{1,0:T(8,128)(2,1)S(1)}) custom-call(s32[8,256]{1,0:T(8,128)S(1)} %constant_dynamic-slice_fusion.ids.order, s32[8,256]{1,0:T(8,128)S(1)} %constant_dynamic-slice_fusion.ids.order, f32[40,256]{1,0:T(8,128)S(1)} %shard_map.143.meta, bf16[256,256]{1,0:T(8,128)(2,1)S(1)} %bitcast.39, ...), custom_call_target="tpu_custom_call" | custom-call | flops 10000000000 | bytes 100000000 | tf_op jit(solution)/shard_map/pallas_call | solution.py:455
  86.0 1.6 %collective-permute-start.30 = (bf16[128,1280]{1,0:T(8,128)(2,1)S(1)}, bf16[128,1280]{1,0:T(8,128)(2,1)S(1)}, u32[]{:S(2)}, u32[]{:S(2)}) collective-permute-start(bf16[128,1280]{1,0:T(8,128)(2,1)S(1)} %shard_map.156), channel_id=1, source_target_pairs={{0,4},{1,3},{4,8},{5,1},{8,12},{9,5},{12,14},{13,9},{14,10},{15,13... | collective-permute-start | bytes 983048 | tf_op jit(solution)/shard_map/ppermute | solution.py:330
  91.3 1.8 %collective-permute-done.30.refs_0_ = bf16[128,1280]{1,0:T(8,128)(2,1)S(1)} collective-permute-done((bf16[128,1280]{1,0:T(8,128)(2,1)S(1)}, bf16[128,1280]{1,0:T(8,128)(2,1)S(1)}, u32[]{:S(2)}, u32[]{:S(2)}) %collective-permute-start.30) | collective-permute-done | bytes 327712 | tf_op jit(solution)/shard_map/ppermute | solution.py:330
  93.5 1.6 %collective-permute-start.33 = (bf16[128,1280]{1,0:T(8,128)(2,1)S(1)}, bf16[128,1280]{1,0:T(8,128)(2,1)S(1)}, u32[]{:S(2)}, u32[]{:S(2)}) collective-permute-start(bf16[128,1280]{1,0:T(8,128)(2,1)S(1)} %shard_map.158), channel_id=1, source_target_pairs={{0,4},{1,3},{4,8},{5,1},{8,12},{9,5},{12,14},{13,9},{14,10},{15,13... | collective-permute-start | bytes 983048 | tf_op jit(solution)/shard_map/ppermute | solution.py:330
  97.0 1.8 %collective-permute-start.34 = (bf16[128,1280]{1,0:T(8,128)(2,1)S(1)}, bf16[128,1280]{1,0:T(8,128)(2,1)S(1)}, u32[]{:S(2)}, u32[]{:S(2)}) collective-permute-start(bf16[128,1280]{1,0:T(8,128)(2,1)S(1)} %shard_map.159), channel_id=1, source_target_pairs={{0,4},{1,3},{4,8},{5,1},{8,12},{9,5},{12,14},{13,9},{14,10},{15,13... | collective-permute-start | bytes 983048 | tf_op jit(solution)/shard_map/ppermute | solution.py:330
  102.1 1.6 %collective-permute-start.37 = (bf16[128,1280]{1,0:T(8,128)(2,1)S(1)}, bf16[128,1280]{1,0:T(8,128)(2,1)S(1)}, u32[]{:S(2)}, u32[]{:S(2)}) collective-permute-start(bf16[128,1280]{1,0:T(8,128)(2,1)S(1)} %shard_map.161), channel_id=1, source_target_pairs={{0,4},{1,3},{4,8},{5,1},{8,12},{9,5},{12,14},{13,9},{14,10},{15,13... | collective-permute-start | bytes 983048 | tf_op jit(solution)/shard_map/ppermute | solution.py:330
  106.3 2.9 %shard_map.163 = (bf16[128,1280]{1,0:T(8,128)(2,1)S(1)}, bf16[128,1280]{1,0:T(8,128)(2,1)S(1)}) custom-call(s32[8,256]{1,0:T(8,128)S(1)} %constant_dynamic-slice_fusion.ids.order, s32[8,256]{1,0:T(8,128)S(1)} %constant_dynamic-slice_fusion.ids.order, f32[40,256]{1,0:T(8,128)S(1)} %shard_map.143.meta, bf16[256,256]{1,0:T(8,128)(2,1)S(1)} %bitcast.40, ...), custom_call_target="tpu_custom_call" | custom-call | tf_op jit(solution)/shard_map/pallas_call | solution.py:509
  117.0 1.9 %collective-permute-done.39.refs_0_ = bf16[128,1280]{1,0:T(8,128)(2,1)S(1)} collective-permute-done((bf16[128,1280]{1,0:T(8,128)(2,1)S(1)}, bf16[128,1280]{1,0:T(8,128)(2,1)S(1)}, u32[]{:S(2)}, u32[]{:S(2)}) %collective-permute-start.39) | collective-permute-done | bytes 327712 | tf_op jit(solution)/shard_map/ppermute | solution.py:330
  124.3 2.0 %collective-permute-done.43.refs_0_ = bf16[128,1280]{1,0:T(8,128)(2,1)S(1)} collective-permute-done((bf16[128,1280]{1,0:T(8,128)(2,1)S(1)}, bf16[128,1280]{1,0:T(8,128)(2,1)S(1)}, u32[]{:S(2)}, u32[]{:S(2)}) %collective-permute-start.43) | collective-permute-done | bytes 327712 | tf_op jit(solution)/shard_map/ppermute | solution.py:330
  131.8 2.0 %collective-permute-done.46.refs_0_ = bf16[128,1280]{1,0:T(8,128)(2,1)S(1)} collective-permute-done((bf16[128,1280]{1,0:T(8,128)(2,1)S(1)}, bf16[128,1280]{1,0:T(8,128)(2,1)S(1)}, u32[]{:S(2)}, u32[]{:S(2)}) %collective-permute-start.46) | collective-permute-done | bytes 327712 | tf_op jit(solution)/shard_map/ppermute | solution.py:330
  134.2 2.6 %collective-permute-start.47 = (bf16[128,1280]{1,0:T(8,128)(2,1)S(1)}, bf16[128,1280]{1,0:T(8,128)(2,1)S(1)}, u32[]{:S(2)}, u32[]{:S(2)}) collective-permute-start(bf16[128,1280]{1,0:T(8,128)(2,1)S(1)} %shard_map.174), channel_id=1, source_target_pairs={{0,20},{1,19},{4,24},{5,17},{8,28},{9,21},{12,30},{13,25},{14,26},... | collective-permute-start | bytes 983048 | tf_op jit(solution)/shard_map/ppermute | solution.py:493
  137.7 2.6 %collective-permute-start.49 = (bf16[128,1280]{1,0:T(8,128)(2,1)S(1)}, bf16[128,1280]{1,0:T(8,128)(2,1)S(1)}, u32[]{:S(2)}, u32[]{:S(2)}) collective-permute-start(bf16[128,1280]{1,0:T(8,128)(2,1)S(1)} %shard_map.176), channel_id=1, source_target_pairs={{0,20},{1,19},{4,24},{5,17},{8,28},{9,21},{12,30},{13,25},{14,26},... | collective-permute-start | bytes 983048 | tf_op jit(solution)/shard_map/ppermute | solution.py:493
  140.2 8.9 %collective-permute-done.47.two = bf16[128,1280]{1,0:T(8,128)(2,1)S(1)} collective-permute-done((bf16[128,1280]{1,0:T(8,128)(2,1)S(1)}, bf16[128,1280]{1,0:T(8,128)(2,1)S(1)}, u32[]{:S(2)}, u32[]{:S(2)}) %collective-permute-start.47) | collective-permute-done | bytes 327712 | tf_op jit(solution)/shard_map/ppermute | solution.py:493
  149.2 3.4 %collective-permute-done.49.two = bf16[128,1280]{1,0:T(8,128)(2,1)S(1)} collective-permute-done((bf16[128,1280]{1,0:T(8,128)(2,1)S(1)}, bf16[128,1280]{1,0:T(8,128)(2,1)S(1)}, u32[]{:S(2)}, u32[]{:S(2)}) %collective-permute-start.49) | collective-permute-done | bytes 327712 | tf_op jit(solution)/shard_map/ppermute | solution.py:493
  (171 shorter events, 91.1 us)
Async XLA Ops:
  11.6 9.0 %collective-permute-start.4 = (bf16[960,256]{1,0:T(8,128)(2,1)S(1)}, bf16[960,256]{1,0:T(8,128)(2,1)S(1)}, u32[]{:S(2)}, u32[]{:S(2)}) collective-permute-start(bf16[960,256]{1,0:T(8,128)(2,1)S(1)} %shard_map.112.one.refs_0_), channel_id=1, source_target_pairs={{0,4},{1,3},{4,8},{5,1},{8,12},{9,5},{12,14},{13,9},{14,10},{15,13... | collective-permute-start | bytes 1474568 | tf_op jit(solution)/shard_map/ppermute | solution.py:330
  15.3 8.9 %collective-permute-start.2 = (bf16[656,256]{1,0:T(8,128)(2,1)S(1)}, bf16[656,256]{1,0:T(8,128)(2,1)S(1)}, u32[]{:S(2)}, u32[]{:S(2)}) collective-permute-start(bf16[656,256]{1,0:T(8,128)(2,1)S(1)} %collective-permute-done.piece.two.refs_3_), channel_id=1, source_target_pairs={{0,4},{1,3},{4,8},{5,1},{8,12},{9,5},{12,14},{13,9},{14,10},{15,13... | collective-permute-start | bytes 1007624 | tf_op jit(solution)/shard_map/ppermute | solution.py:330
  20.6 8.9 %collective-permute-start.7 = (bf16[960,256]{1,0:T(8,128)(2,1)S(1)}, bf16[960,256]{1,0:T(8,128)(2,1)S(1)}, u32[]{:S(2)}, u32[]{:S(2)}) collective-permute-start(bf16[960,256]{1,0:T(8,128)(2,1)S(1)} %collective-permute-done.4.piece.one.refs_2_), channel_id=1, source_target_pairs={{0,4},{1,3},{4,8},{5,1},{8,12},{9,5},{12,14},{13,9},{14,10},{15,13... | collective-permute-start | bytes 1474568 | tf_op jit(solution)/shard_map/ppermute | solution.py:330
  24.2 8.9 %collective-permute-start.5 = (bf16[656,256]{1,0:T(8,128)(2,1)S(1)}, bf16[656,256]{1,0:T(8,128)(2,1)S(1)}, u32[]{:S(2)}, u32[]{:S(2)}) collective-permute-start(bf16[656,256]{1,0:T(8,128)(2,1)S(1)} %collective-permute-done.2.piece.two.refs_5_), channel_id=1, source_target_pairs={{0,4},{1,3},{4,8},{5,1},{8,12},{9,5},{12,14},{13,9},{14,10},{15,13... | collective-permute-start | bytes 1007624 | tf_op jit(solution)/shard_map/ppermute | solution.py:330
  29.4 8.9 %collective-permute-start.10 = (bf16[960,256]{1,0:T(8,128)(2,1)S(1)}, bf16[960,256]{1,0:T(8,128)(2,1)S(1)}, u32[]{:S(2)}, u32[]{:S(2)}) collective-permute-start(bf16[960,256]{1,0:T(8,128)(2,1)S(1)} %collective-permute-done.7.piece.one.refs_4_), channel_id=1, source_target_pairs={{0,4},{1,3},{4,8},{5,1},{8,12},{9,5},{12,14},{13,9},{14,10},{15,13... | collective-permute-start | bytes 1474568 | tf_op jit(solution)/shard_map/ppermute | solution.py:330
  33.0 8.9 %collective-permute-start.8 = (bf16[656,256]{1,0:T(8,128)(2,1)S(1)}, bf16[656,256]{1,0:T(8,128)(2,1)S(1)}, u32[]{:S(2)}, u32[]{:S(2)}) collective-permute-start(bf16[656,256]{1,0:T(8,128)(2,1)S(1)} %collective-permute-done.5.piece.two.refs_7_), channel_id=1, source_target_pairs={{0,4},{1,3},{4,8},{5,1},{8,12},{9,5},{12,14},{13,9},{14,10},{15,13... | collective-permute-start | bytes 1007624 | tf_op jit(solution)/shard_map/ppermute | solution.py:330
  38.3 8.9 %collective-permute-start.13 = (bf16[960,256]{1,0:T(8,128)(2,1)S(1)}, bf16[960,256]{1,0:T(8,128)(2,1)S(1)}, u32[]{:S(2)}, u32[]{:S(2)}) collective-permute-start(bf16[960,256]{1,0:T(8,128)(2,1)S(1)} %collective-permute-done.10.piece.one.refs_6_), channel_id=1, source_target_pairs={{0,4},{1,3},{4,8},{5,1},{8,12},{9,5},{12,14},{13,9},{14,10},{15,13... | collective-permute-start | bytes 1474568 | tf_op jit(solution)/shard_map/ppermute | solution.py:330
  41.9 8.9 %collective-permute-start.11 = (bf16[656,256]{1,0:T(8,128)(2,1)S(1)}, bf16[656,256]{1,0:T(8,128)(2,1)S(1)}, u32[]{:S(2)}, u32[]{:S(2)}) collective-permute-start(bf16[656,256]{1,0:T(8,128)(2,1)S(1)} %collective-permute-done.8.piece.two.refs_9_), channel_id=1, source_target_pairs={{0,4},{1,3},{4,8},{5,1},{8,12},{9,5},{12,14},{13,9},{14,10},{15,13... | collective-permute-start | bytes 1007624 | tf_op jit(solution)/shard_map/ppermute | solution.py:330
  47.1 8.9 %collective-permute-start.16 = (bf16[960,256]{1,0:T(8,128)(2,1)S(1)}, bf16[960,256]{1,0:T(8,128)(2,1)S(1)}, u32[]{:S(2)}, u32[]{:S(2)}) collective-permute-start(bf16[960,256]{1,0:T(8,128)(2,1)S(1)} %collective-permute-done.13.piece.one.refs_8_), channel_id=1, source_target_pairs={{0,4},{1,3},{4,8},{5,1},{8,12},{9,5},{12,14},{13,9},{14,10},{15,13... | collective-permute-start | bytes 1474568 | tf_op jit(solution)/shard_map/ppermute | solution.py:330
  50.7 8.9 %collective-permute-start.14 = (bf16[656,256]{1,0:T(8,128)(2,1)S(1)}, bf16[656,256]{1,0:T(8,128)(2,1)S(1)}, u32[]{:S(2)}, u32[]{:S(2)}) collective-permute-start(bf16[656,256]{1,0:T(8,128)(2,1)S(1)} %collective-permute-done.11.piece.two.refs_11_), channel_id=1, source_target_pairs={{0,4},{1,3},{4,8},{5,1},{8,12},{9,5},{12,14},{13,9},{14,10},{15,13... | collective-permute-start | bytes 1007624 | tf_op jit(solution)/shard_map/ppermute | solution.py:330
  56.0 8.9 %collective-permute-start.19 = (bf16[960,256]{1,0:T(8,128)(2,1)S(1)}, bf16[960,256]{1,0:T(8,128)(2,1)S(1)}, u32[]{:S(2)}, u32[]{:S(2)}) collective-permute-start(bf16[960,256]{1,0:T(8,128)(2,1)S(1)} %collective-permute-done.16.piece.one.refs_10_), channel_id=1, source_target_pairs={{0,4},{1,3},{4,8},{5,1},{8,12},{9,5},{12,14},{13,9},{14,10},{15,13... | collective-permute-start | bytes 1474568 | tf_op jit(solution)/shard_map/ppermute | solution.py:330
  58.7 9.1 %collective-permute-start.22 = (bf16[7,160,256]{2,1,0:T(8,128)(2,1)S(1)}, bf16[7,160,256]{2,1,0:T(8,128)(2,1)S(1)}, u32[]{:S(2)}, u32[]{:S(2)}) collective-permute-start(bf16[7,160,256]{2,1,0:T(8,128)(2,1)S(1)} %shard_map.144.refs_0_), channel_id=1, source_target_pairs={{0,1},{1,0},{2,3},{3,2},{4,5},{5,4},{6,7},{7,6},{8,9},{9,8},{10,11... | collective-permute-start | bytes 1720328 | tf_op jit(solution)/shard_map/ppermute | solution.py:331
  59.6 11.2 %collective-permute-start.17 = (bf16[656,256]{1,0:T(8,128)(2,1)S(1)}, bf16[656,256]{1,0:T(8,128)(2,1)S(1)}, u32[]{:S(2)}, u32[]{:S(2)}) collective-permute-start(bf16[656,256]{1,0:T(8,128)(2,1)S(1)} %collective-permute-done.14.piece.two.refs_13_), channel_id=1, source_target_pairs={{0,4},{1,3},{4,8},{5,1},{8,12},{9,5},{12,14},{13,9},{14,10},{15,13... | collective-permute-start | bytes 1007624 | tf_op jit(solution)/shard_map/ppermute | solution.py:330
  84.8 15.6 %collective-permute-start.41 = (bf16[64,2560]{1,0:T(8,128)(2,1)S(1)}, bf16[64,2560]{1,0:T(8,128)(2,1)S(1)}, u32[]{:S(2)}, u32[]{:S(2)}) collective-permute-start(bf16[64,2560]{1,0:T(8,128)(2,1)S(1)} %get-tuple-element.267), channel_id=1, source_target_pairs={{0,1},{1,0},{2,3},{3,2},{4,5},{5,4},{6,7},{7,6},{8,9},{9,8},{10,11... | collective-permute-start | bytes 983048 | tf_op jit(solution)/shard_map/ppermute | solution.py:331
  85.1 21.2 %collective-permute-start.27 = (bf16[128,2560]{1,0:T(8,128)(2,1)S(1)}, bf16[128,2560]{1,0:T(8,128)(2,1)S(1)}, u32[]{:S(2)}, u32[]{:S(2)}) collective-permute-start(bf16[128,2560]{1,0:T(8,128)(2,1)S(1)} %bitcast.37), channel_id=1, source_target_pairs={{0,1},{1,0},{2,3},{3,2},{4,5},{5,4},{6,7},{7,6},{8,9},{9,8},{10,11... | collective-permute-start | bytes 1966088 | tf_op jit(solution)/shard_map/ppermute | solution.py:331
  88.0 8.6 %collective-permute-start.31 = (bf16[128,1280]{1,0:T(8,128)(2,1)S(1)}, bf16[128,1280]{1,0:T(8,128)(2,1)S(1)}, u32[]{:S(2)}, u32[]{:S(2)}) collective-permute-start(bf16[128,1280]{1,0:T(8,128)(2,1)S(1)} %shard_map.157), channel_id=1, source_target_pairs={{0,4},{1,3},{4,8},{5,1},{8,12},{9,5},{12,14},{13,9},{14,10},{15,13... | collective-permute-start | bytes 983048 | tf_op jit(solution)/shard_map/ppermute | solution.py:330
  91.2 10.5 %collective-permute-start.32 = (bf16[2,64,2560]{2,1,0:T(8,128)(2,1)S(1)}, bf16[2,64,2560]{2,1,0:T(8,128)(2,1)S(1)}, u32[]{:S(2)}, u32[]{:S(2)}) collective-permute-start(bf16[2,64,2560]{2,1,0:T(8,128)(2,1)S(1)} %get-tuple-element.245), channel_id=1, source_target_pairs={{0,1},{1,0},{2,3},{3,2},{4,5},{5,4},{6,7},{7,6},{8,9},{9,8},{10,11... | collective-permute-start | bytes 1966088 | tf_op jit(solution)/shard_map/ppermute | solution.py:331
  100.4 10.9 %collective-permute-start.36 = (bf16[2,64,2560]{2,1,0:T(8,128)(2,1)S(1)}, bf16[2,64,2560]{2,1,0:T(8,128)(2,1)S(1)}, u32[]{:S(2)}, u32[]{:S(2)}) collective-permute-start(bf16[2,64,2560]{2,1,0:T(8,128)(2,1)S(1)} %get-tuple-element.254), channel_id=1, source_target_pairs={{0,1},{1,0},{2,3},{3,2},{4,5},{5,4},{6,7},{7,6},{8,9},{9,8},{10,11... | collective-permute-start | bytes 1966088 | tf_op jit(solution)/shard_map/ppermute | solution.py:331
  102.1 9.2 %collective-permute-start.37 = (bf16[128,1280]{1,0:T(8,128)(2,1)S(1)}, bf16[128,1280]{1,0:T(8,128)(2,1)S(1)}, u32[]{:S(2)}, u32[]{:S(2)}) collective-permute-start(bf16[128,1280]{1,0:T(8,128)(2,1)S(1)} %shard_map.161), channel_id=1, source_target_pairs={{0,4},{1,3},{4,8},{5,1},{8,12},{9,5},{12,14},{13,9},{14,10},{15,13... | collective-permute-start | bytes 983048 | tf_op jit(solution)/shard_map/ppermute | solution.py:330
  104.7 8.6 %collective-permute-start.38 = (bf16[128,1280]{1,0:T(8,128)(2,1)S(1)}, bf16[128,1280]{1,0:T(8,128)(2,1)S(1)}, u32[]{:S(2)}, u32[]{:S(2)}) collective-permute-start(bf16[128,1280]{1,0:T(8,128)(2,1)S(1)} %shard_map.162), channel_id=1, source_target_pairs={{0,4},{1,3},{4,8},{5,1},{8,12},{9,5},{12,14},{13,9},{14,10},{15,13... | collective-permute-start | bytes 983048 | tf_op jit(solution)/shard_map/ppermute | solution.py:330
  109.2 11.6 %collective-permute-start.35 = (bf16[128,1280]{1,0:T(8,128)(2,1)S(1)}, bf16[128,1280]{1,0:T(8,128)(2,1)S(1)}, u32[]{:S(2)}, u32[]{:S(2)}) collective-permute-start(bf16[128,1280]{1,0:T(8,128)(2,1)S(1)} %get-tuple-element.249), channel_id=1, source_target_pairs={{0,16},{16,0},{1,17},{17,1},{2,18},{18,2},{3,19},{19,3},{4,20},{20... | collective-permute-start | bytes 983048 | tf_op jit(solution)/shard_map/ppermute | solution.py:335
  110.8 17.5 %collective-permute-start.45 = (bf16[128,1280]{1,0:T(8,128)(2,1)S(1)}, bf16[128,1280]{1,0:T(8,128)(2,1)S(1)}, u32[]{:S(2)}, u32[]{:S(2)}) collective-permute-start(bf16[128,1280]{1,0:T(8,128)(2,1)S(1)} %get-tuple-element.255), channel_id=1, source_target_pairs={{0,16},{16,0},{1,17},{17,1},{2,18},{18,2},{3,19},{19,3},{4,20},{20... | collective-permute-start | bytes 983048 | tf_op jit(solution)/shard_map/ppermute | solution.py:335
  134.2 14.9 %collective-permute-start.47 = (bf16[128,1280]{1,0:T(8,128)(2,1)S(1)}, bf16[128,1280]{1,0:T(8,128)(2,1)S(1)}, u32[]{:S(2)}, u32[]{:S(2)}) collective-permute-start(bf16[128,1280]{1,0:T(8,128)(2,1)S(1)} %shard_map.174), channel_id=1, source_target_pairs={{0,20},{1,19},{4,24},{5,17},{8,28},{9,21},{12,30},{13,25},{14,26},... | collective-permute-start | bytes 983048 | tf_op jit(solution)/shard_map/ppermute | solution.py:493
  137.7 14.9 %collective-permute-start.49 = (bf16[128,1280]{1,0:T(8,128)(2,1)S(1)}, bf16[128,1280]{1,0:T(8,128)(2,1)S(1)}, u32[]{:S(2)}, u32[]{:S(2)}) collective-permute-start(bf16[128,1280]{1,0:T(8,128)(2,1)S(1)} %shard_map.176), channel_id=1, source_target_pairs={{0,20},{1,19},{4,24},{5,17},{8,28},{9,21},{12,30},{13,25},{14,26},... | collective-permute-start | bytes 983048 | tf_op jit(solution)/shard_map/ppermute | solution.py:493
  (38 other events, 167.6 us)
